TPU v7x, 32 devices: a whole 2x2x4 slice. The times are simulated.
32 devices in a mesh: groups: 2 (over y), req: 4 (over x, core), tp: 4 (over z).
Axes of the slice: x: 2, y: 2, z: 4, core: 2. Of those that a mesh axis runs over, the one named last changes fastest.
Arguments:
- x_in: bfloat16 [8192, 16384], P(('groups', 'req'), 'tp'), parts along dimension 0, may hold values from -6 to 6
- gate_in: bfloat16 [8192, 16384], P(('groups', 'req'), 'tp'), parts along dimension 0, may hold values from -6 to 6
- b_in: bfloat16 [8192, 2048], P(('groups', 'req'), 'tp'), parts along dimension 0, may hold values from -6 to 6
- c_in: bfloat16 [8192, 2048], P(('groups', 'req'), 'tp'), parts along dimension 0, may hold values from -6 to 6
- dt_raw: bfloat16 [8192, 256], P(('groups', 'req'), 'tp'), parts along dimension 0, may hold values from -3 to 3
- conv_x: bfloat16 [4, 16384], P(None, 'tp'), may hold values from -3 to 3
- conv_b: bfloat16 [4, 2048], P(None, 'tp'), may hold values from -3 to 3
- conv_c: bfloat16 [4, 2048], P(None, 'tp'), may hold values from -3 to 3
- dt_bias: float32 [256], P('tp'), may hold values from -3 to 0
- a_log: float32 [256], P('tp'), may hold values from -7 to -2.5
- skip: float32 [256], P('tp'), may hold values from 0.5 to 1.5
- norm_gain: float32 [16384], P('tp'), may hold values from 0.5 to 1.5
- segment: int32 [8192], P(('groups', 'req')), parts along dimension 0, may hold values from 0 to 3, never falling along the last dimension, each value on 1 to 2048 neighbouring positions
Outputs:
- mixed: bfloat16 [8192, 16384], P(('groups', 'req'), 'tp'), parts along dimension 0
There are 2 independent parts, one for each index of `groups`. A program takes and returns all parts, laid end to end along the dimension named above; an argument that names none is the same for every part. Nothing has to cross between parts.
Inputs may be any that keep to these rules, and one draw needn't show every extreme that they name: `segment`: never falls along the stream; each prompt's tokens are contiguous; one prompt has exactly 2048 tokens.
All inputs are finite; a program needn't handle non-finite values.
Results may differ from a plain program's by a relative error of at most 0.0085.
Values may be sent and summed in bfloat16 or wider, within the bound.
No kernel may reach another device: no remote copies, remote signals or barrier semaphores. Data moves between devices by JAX's collectives and lax.ppermute only.
A program may use at most 256 MiB of HBM per device.

v0:
```python
import functools

import jax
import jax.numpy as jnp
from jax import lax
from jax.experimental import pallas as pl
from jax.experimental.pallas import tpu as pltpu
from jax.sharding import PartitionSpec as P

P_SIZE = 64
N = 256
L = 256
SPAN = 2 * L
KCONV = 4
REACH = KCONV - 1
LANES = 128
CHUNK = 256
TILE = 128
F32 = jnp.float32
BF16 = jnp.bfloat16


def dot(a, b):
    return jnp.dot(a, b, preferred_element_type=F32)


def split_high_low(value, heads):
    lane = lax.broadcasted_iota(jnp.int32, value.shape, 1)
    high = value.astype(BF16).astype(F32)
    low = jnp.where(lane < 2 * heads, value - high, 0.0)
    return jnp.where(lane < heads, high, low).astype(BF16)


def silu_of_half(half):
    return half + half * jnp.tanh(half)


def spread_matrix(ref, first_head, heads):
    width = ref.shape[1]
    rows = lax.broadcasted_iota(jnp.int32, (LANES, width), 0) & (heads - 1)
    cols = lax.broadcasted_iota(jnp.int32, (LANES, width), 1) >> 6
    ref[...] = jnp.where(rows == cols + first_head, 1.0, 0.0).astype(BF16)


def conv_tile(buf, index, weights, row, rows, code):
    acc = None
    for step in range(KCONV):
        term = buf[index, pl.ds(8 - step + row, rows), :] * weights[REACH - step : KCONV - step]
        if code is not None and step > 0:
            term = jnp.where(code >= step, term, 0.0)
        acc = term if acc is None else acc + term
    return acc


def tail_kernel(seg_s, x_ref, b_ref, c_ref, out_ref):
    rows = seg_s.shape[0]
    start = 0
    for ref in (x_ref, b_ref, c_ref):
        width = ref.shape[1]
        value = ref[...].astype(F32)
        out_ref[:, start : start + width] = value[16 - REACH :].astype(BF16)
        start += width
    ids = [jnp.full((1, LANES), seg_s[rows - REACH + k] + 1, jnp.int32).astype(F32) for k in range(REACH)]
    out_ref[:, start:] = jnp.concatenate(ids, axis=0).astype(BF16)


def decay_kernel(dt_ref, bias_ref, a_log_ref, skip_ref, a_ref, e_ref, w_ref, em_ref):
    heads = dt_ref.shape[1]
    copies = LANES // heads
    wide = lambda value: jnp.concatenate([value] * copies, axis=1)
    z = wide(dt_ref[...].astype(F32)) + wide(bias_ref[...])
    dt = jnp.maximum(z, 0.0) + jnp.log1p(jnp.exp(-jnp.abs(z)))
    fall = -dt * wide(jnp.exp(a_log_ref[...]))
    rows = lax.broadcasted_iota(jnp.int32, (L, L), 0)
    cols = lax.broadcasted_iota(jnp.int32, (L, L), 1)
    lower = jnp.where(rows >= cols, 1.0, 0.0)
    sums = lambda value: jnp.dot(lower, value, precision=lax.Precision.HIGHEST, preferred_element_type=F32)
    upper_half = sums(fall[:L])
    cum = jnp.concatenate([upper_half, sums(fall[L:]) + upper_half[L - 1 : L]], axis=0)
    middle = 0.5 * cum[SPAN - 1 : SPAN]
    a_ref[...] = split_high_low(jnp.exp(middle - cum) * dt, heads)
    e_ref[...] = split_high_low(jnp.exp(cum - middle), heads)
    w_ref[...] = split_high_low(wide(skip_ref[...]) / dt, heads)
    em_ref[0] = split_high_low(jnp.broadcast_to(jnp.exp(middle), (16, LANES)), heads)


def score_kernel(
    seg_s, b_ref, c_ref, halo_ref, ids_ref, wb_ref, wc_ref, seg_ref,
    m_ref, bt_ref, code_ref, info_ref,
    bc_buf, seg_buf, held, *, parts
):
    span = pl.program_id(0)
    width = parts * N
    pieces = width // LANES
    ids = ids_ref[...].astype(F32)
    start = span * SPAN
    first = seg_s[start]
    last = seg_s[start + SPAN - 1]
    oldest_device = (jnp.max(ids[0:1]) - 1.0).astype(jnp.int32)
    before_device = (jnp.max(ids[REACH - 1 : REACH]) - 1.0).astype(jnp.int32)
    before = jnp.where(span == 0, before_device, seg_s[jnp.maximum(start - 1, 0)])
    oldest = jnp.where(span == 0, oldest_device, seg_s[jnp.maximum(start - REACH, 0)])
    cut = (first != last) | ((oldest != first) & (oldest >= 0))
    info_ref[2 * span] = cut.astype(jnp.int32)
    info_ref[2 * span + 1] = (before == last).astype(jnp.int32)

    @pl.when(span == 0)
    def _():
        seg_buf[8 - REACH : 8, :] = ids - 1.0
        for piece in range(2 * pieces):
            bc_buf[piece, 8 - REACH : 8, :] = halo_ref[:, piece * LANES : (piece + 1) * LANES].astype(F32)

    @pl.when(span > 0)
    def _():
        seg_buf[0:8, :] = seg_buf[SPAN : SPAN + 8, :]
        for piece in range(2 * pieces):
            bc_buf[piece, 0:8, :] = bc_buf[piece, SPAN : SPAN + 8, :]

    seg_rows, seg_cols = [], []
    for half in range(2):
        seg_row = seg_ref[:, half * L : (half + 1) * L].astype(F32)
        seg_col = jnp.transpose(jnp.broadcast_to(seg_row, (L, L)))
        seg_rows.append(seg_row)
        seg_cols.append(seg_col)
        seg_buf[8 + half * L : 8 + (half + 1) * L, :] = seg_col[:, :LANES]
    for half in range(2):
        code = jnp.zeros((L, LANES), F32)
        for step in range(1, KCONV):
            same = seg_buf[pl.ds(8 - step + half * L, L), :] == seg_cols[half][:, :LANES]
            code = code + jnp.where(same, 1.0, 0.0)
        code_ref[half * L : (half + 1) * L, :] = code

    weights_b = 0.5 * wb_ref[...].astype(F32)
    weights_c = 0.5 * wc_ref[...].astype(F32)
    for piece in range(pieces):
        lanes = slice(piece * LANES, (piece + 1) * LANES)
        bc_buf[piece, 8 : 8 + SPAN, :] = b_ref[:, lanes].astype(F32)
        bc_buf[pieces + piece, 8 : 8 + SPAN, :] = c_ref[:, lanes].astype(F32)
        for index, weights in ((piece, weights_b), (pieces + piece, weights_c)):
            for row in range(0, SPAN, TILE):
                acc = conv_tile(bc_buf, index, weights[:, lanes], row, TILE, code_ref[row : row + TILE, :])
                held[index, row : row + TILE, :] = silu_of_half(acc)

    rows = lax.broadcasted_iota(jnp.int32, (L, L), 0)
    cols = lax.broadcasted_iota(jnp.int32, (L, L), 1)
    causal = rows >= cols
    across = (((1,), (1,)), ((), ()))
    for g in range(parts):
        per = N // LANES

        def take(first_piece, half):
            parts_ = [held[first_piece + k, half * L : (half + 1) * L, :] for k in range(per)]
            return jnp.concatenate(parts_, axis=1)

        bs = [take(g * per, half) for half in range(2)]
        cs = [take(pieces + g * per, half) for half in range(2)]
        bs16 = [value.astype(BF16) for value in bs]
        cs16 = [value.astype(BF16) for value in cs]
        for half in range(2):
            own = slice(half * L, (half + 1) * L)
            scores = lax.dot_general(cs16[half], bs16[half], across, preferred_element_type=F32)
            allowed = causal & (seg_cols[half] == seg_rows[half])
            m_ref[g, own, 0:L] = jnp.where(allowed, scores, 0.0).astype(BF16)
            enters = seg_cols[half] == before.astype(F32)
            m_ref[g, own, L : L + N] = jnp.where(enters, cs[half], 0.0).astype(BF16)
            latest = seg_cols[half] == last.astype(F32)
            bt_ref[g, :, own] = jnp.transpose(jnp.where(latest, bs[half], 0.0)).astype(BF16)
        scores = lax.dot_general(cs16[1], bs16[0], across, preferred_element_type=F32)
        m_ref[g, L:SPAN, L + N :] = jnp.where(seg_cols[1] == seg_rows[0], scores, 0.0).astype(BF16)
        m_ref[g, 0:L, L + N :] = jnp.zeros((L, L), BF16)


def state_kernel(
    info_ref, x_ref, halo_ref, w_ref, bt_ref, a_ref, em_ref, code_ref,
    u_ref, state_ref, first_ref, factor_ref,
    buf, carry, spread, *, first_head, heads
):
    span = pl.program_id(1)
    width = x_ref.shape[1]
    chunks = width // CHUNK
    inner = CHUNK // LANES
    cut = info_ref[2 * span] > 0

    @pl.when(span == 0)
    def _():
        spread_matrix(spread, first_head + pl.program_id(0) * (width // P_SIZE), heads)
        for piece in range(width // LANES):
            buf[piece, 8 - REACH : 8, :] = halo_ref[:, piece * LANES : (piece + 1) * LANES].astype(F32)

    @pl.when(span > 0)
    def _():
        buf[:, 0:8, :] = buf[:, SPAN : SPAN + 8, :]

    def convolve(masked):
        for chunk in range(chunks):
            cols = slice(chunk * CHUNK, (chunk + 1) * CHUNK)
            scale = dot(a_ref[...], spread[:, cols])
            for piece in range(inner):
                index = chunk * inner + piece
                lanes = slice(index * LANES, (index + 1) * LANES)
                weights = 0.5 * w_ref[:, lanes].astype(F32)
                buf[index, 8 : 8 + SPAN, :] = x_ref[:, lanes].astype(F32)
                for row in range(0, SPAN, TILE):
                    code = code_ref[row : row + TILE, :] if masked else None
                    acc = conv_tile(buf, index, weights, row, TILE, code)
                    factor = scale[row : row + TILE, piece * LANES : (piece + 1) * LANES]
                    u_ref[row : row + TILE, lanes] = (silu_of_half(acc) * factor).astype(BF16)
            grown = dot(bt_ref[0], u_ref[:, cols])
            carry[span, :, cols] = grown

    @pl.when(cut)
    def _():
        convolve(True)

    @pl.when(jnp.logical_not(cut))
    def _():
        convolve(False)

    @pl.when(span == 1)
    def _():
        passes = [info_ref[2 * k + 1].astype(F32) for k in range(2)]
        for chunk in range(chunks):
            cols = slice(chunk * CHUNK, (chunk + 1) * CHUNK)
            early, late = (dot(em_ref[k], spread[:, cols])[0:1] for k in range(2))
            middle = early * carry[0, :, cols]
            first_ref[:, cols] = middle.astype(BF16)
            state_ref[:, cols] = (late * carry[1, :, cols] + (passes[1] * late * late) * middle).astype(BF16)
            factor_ref[:, cols] = (passes[0] * passes[1]) * (early * early * late * late)


def final_kernel(
    info_ref, u_ref, u_first_ref, gate_ref, m_ref, e_ref, w_ref, em_ref, first_ref, t0_ref, t1_ref, t2_ref, gain_ref,
    out_ref,
    enter, spread, held, *, first_head, heads
):
    block = pl.program_id(0)
    width = u_ref.shape[1]
    chunks = width // CHUNK
    spans = [slice(chunk * CHUNK, (chunk + 1) * CHUNK) for chunk in range(chunks)]

    @pl.when(block == 0)
    def _():
        spread_matrix(spread, first_head, heads)
        passes = info_ref[1].astype(F32)
        for cols in spans:
            early, late = (dot(em_ref[k], spread[:, cols])[0:1] for k in range(2))
            came = t0_ref[:, cols].astype(F32) + t1_ref[:, cols].astype(F32) + t2_ref[:, cols].astype(F32)
            enter[0, :, cols] = (early * came).astype(BF16)
            grown = first_ref[:, cols].astype(F32) + (passes * early * early) * came
            enter[1, :, cols] = (late * grown).astype(BF16)

    def rows(odd):
        squares = jnp.zeros((L, LANES), F32)
        for cols in spans:
            part = spread[:, cols]
            u = u_ref[:, cols]
            total = dot(m_ref[0, :, 0:L], u) + dot(m_ref[0, :, L : L + N], enter[block // 2, :, cols])
            if odd:
                total = total + dot(m_ref[0, :, L + N :], u_first_ref[:, cols])
            y = dot(e_ref[...], part) * (total + dot(w_ref[...], part) * u.astype(F32))
            v = y * silu_of_half(0.5 * gate_ref[:, cols].astype(F32))
            held[:, cols] = v
            v2 = v * v
            for piece in range(CHUNK // LANES):
                squares = squares + v2[:, piece * LANES : (piece + 1) * LANES]
        mean = jnp.sum(squares, axis=1, keepdims=True) * (1.0 / width)
        scale = lax.rsqrt(mean + 1e-05)
        for cols in spans:
            out_ref[:, cols] = (held[:, cols] * scale * gain_ref[:, cols]).astype(BF16)

    @pl.when(block % 2 == 0)
    def _():
        rows(False)

    @pl.when(block % 2 == 1)
    def _():
        rows(True)


def final_into_kernel(*refs, first_head, heads):
    final_kernel(*refs[:13], *refs[14:], first_head=first_head, heads=heads)


def per_device(
    x_in, gate_in, b_in, c_in, dt_raw, conv_x, conv_b, conv_c, dt_bias, a_log, skip, norm_gain, segment
):
    rows, channels = x_in.shape
    width_bc = b_in.shape[1]
    parts = width_bc // N
    width = channels // parts
    heads = width // P_SIZE
    all_heads = dt_raw.shape[1]
    blocks = rows // L
    spans = rows // SPAN
    assert spans == 2
    devices = lax.axis_size("req")
    step_width = width // 2
    shape = jax.ShapeDtypeStruct
    smem = pl.BlockSpec(memory_space=pltpu.SMEM)
    whole = lambda *_: (0, 0)
    at_row = lambda k, *_: (k, 0)

    def params(axes):
        return pltpu.CompilerParams(dimension_semantics=("arbitrary",) * axes, vmem_limit_bytes=30 << 20)

    def cost(flops, mib):
        return pl.CostEstimate(flops=flops, bytes_accessed=mib << 20, transcendentals=0)

    shift = [(k, k + 1) for k in range(devices - 1)]
    inside = [(k, k + 1) for k in range(0, devices - 1, 2)]
    across = [(k, k + 1) for k in range(1, devices - 1, 2)]

    last_rows = lambda *_: (rows // 16 - 1, 0)
    tail_width = channels + 2 * width_bc + LANES
    tail = pl.pallas_call(
        tail_kernel,
        grid=(1,),
        in_specs=[
            smem,
            pl.BlockSpec((16, channels), last_rows),
            pl.BlockSpec((16, width_bc), last_rows),
            pl.BlockSpec((16, width_bc), last_rows),
        ],
        out_specs=pl.BlockSpec((REACH, tail_width), whole),
        out_shape=shape((REACH, tail_width), BF16),
        compiler_params=params(1),
        cost_estimate=cost(1000, 0),
        name="tails",
    )(segment, x_in, b_in, c_in)
    halo = lax.ppermute(tail, "req", shift)

    row = lambda value: value.reshape(1, -1)
    narrow = pl.BlockSpec((SPAN, LANES), at_row)
    a_hl, e_hl, w_hl, em = pl.pallas_call(
        decay_kernel,
        grid=(spans,),
        in_specs=[pl.BlockSpec((SPAN, all_heads), at_row)] + [pl.BlockSpec((1, all_heads), whole)] * 3,
        out_specs=[narrow, narrow, narrow, pl.BlockSpec((1, 16, LANES), lambda k: (k, 0, 0))],
        out_shape=[shape((rows, LANES), BF16)] * 3 + [shape((spans, 16, LANES), BF16)],
        compiler_params=params(1),
        cost_estimate=cost(3 * 10**9, 1),
        name="decays",
    )(dt_raw, row(dt_bias), row(a_log), row(skip))

    m, bt, code, info = pl.pallas_call(
        functools.partial(score_kernel, parts=parts),
        grid=(spans,),
        in_specs=[
            smem,
            pl.BlockSpec((SPAN, width_bc), at_row),
            pl.BlockSpec((SPAN, width_bc), at_row),
            pl.BlockSpec((REACH, 2 * width_bc), lambda *_: (0, channels // (2 * width_bc))),
            pl.BlockSpec((REACH, LANES), lambda *_: (0, tail_width // LANES - 1)),
            pl.BlockSpec((KCONV, width_bc), whole),
            pl.BlockSpec((KCONV, width_bc), whole),
            pl.BlockSpec((1, SPAN), lambda k: (0, k)),
        ],
        out_specs=[
            pl.BlockSpec((parts, SPAN, N + SPAN), lambda k: (0, k, 0)),
            pl.BlockSpec((parts, N, SPAN), lambda k: (0, 0, k)),
            narrow,
            smem,
        ],
        out_shape=[
            shape((parts, rows, N + SPAN), BF16),
            shape((parts, N, rows), BF16),
            shape((rows, LANES), F32),
            shape((2 * spans,), jnp.int32),
        ],
        scratch_shapes=[
            pltpu.VMEM((2 * width_bc // LANES, SPAN + 8, LANES), F32),
            pltpu.VMEM((SPAN + 8, LANES), F32),
            pltpu.VMEM((2 * width_bc // LANES, SPAN, LANES), F32),
        ],
        compiler_params=params(1),
        cost_estimate=cost(2 * 10**9, 6),
        name="scores",
    )(segment, b_in, c_in, halo, halo, conv_b, conv_c, row(segment))

    em_spec = lambda: pl.BlockSpec((spans, 16, LANES), lambda *_: (0, 0, 0))

    def local(g):
        steps = width // step_width
        at_cols = lambda j, k: (0, g * steps + j)
        return pl.pallas_call(
            functools.partial(state_kernel, first_head=g * heads, heads=all_heads),
            grid=(steps, spans),
            in_specs=[
                smem,
                pl.BlockSpec((SPAN, step_width), lambda j, k: (k, g * steps + j)),
                pl.BlockSpec((REACH, step_width), at_cols),
                pl.BlockSpec((KCONV, step_width), at_cols),
                pl.BlockSpec((1, N, SPAN), lambda j, k: (g, 0, k)),
                pl.BlockSpec((SPAN, LANES), lambda j, k: (k, 0)),
                em_spec(),
                pl.BlockSpec((SPAN, LANES), lambda j, k: (k, 0)),
            ],
            out_specs=[
                pl.BlockSpec((SPAN, step_width), lambda j, k: (k, j)),
                pl.BlockSpec((N, step_width), lambda j, k: (0, j)),
                pl.BlockSpec((N, step_width), lambda j, k: (0, j)),
                pl.BlockSpec((1, step_width), lambda j, k: (0, j)),
            ],
            out_shape=[
                shape((rows, width), BF16),
                shape((N, width), BF16),
                shape((N, width), BF16),
                shape((1, width), F32),
            ],
            scratch_shapes=[
                pltpu.VMEM((step_width // LANES, SPAN + 8, LANES), F32),
                pltpu.VMEM((spans, N, step_width), F32),
                pltpu.VMEM((LANES, step_width), BF16),
            ],
            compiler_params=params(2),
            cost_estimate=cost(6 * 10**9, 10),
            name="state",
        )(info, x_in, halo, conv_x, bt, a_hl, em, code)

    def travel(state, factor):
        def scaled(value):
            return factor * value.astype(F32)

        first = lax.ppermute(state, "req", inside)
        leaving = (state.astype(F32) + scaled(first)).astype(BF16)
        entering, passed = jnp.zeros_like(state), jnp.zeros_like(state)
        rounds = devices // 2 - 1
        for turn in range(rounds):
            entering = lax.ppermute(leaving, "req", across)
            passed = lax.ppermute(scaled(entering).astype(BF16), "req", inside)
            if turn < rounds - 1:
                leaving = (state.astype(F32) + scaled(first.astype(F32) + passed.astype(F32))).astype(BF16)
        return first, entering, passed

    def final(g, u, first, carries, out):
        at_group = lambda *_: (0, g)
        own = pl.BlockSpec((L, width), lambda k: (k, g))
        square = pl.BlockSpec((N, width), whole)
        in_specs = [
            smem,
            pl.BlockSpec((L, width), at_row),
            pl.BlockSpec((L, width), lambda k: (k // 2 * 2, 0)),
            own,
            pl.BlockSpec((1, L, N + SPAN), lambda k: (g, k, 0)),
            pl.BlockSpec((L, LANES), at_row),
            pl.BlockSpec((L, LANES), at_row),
            em_spec(),
            square,
            square,
            square,
            square,
            pl.BlockSpec((1, width), at_group),
        ]
        operands = [info, u, u, gate_in, m, e_hl, w_hl, em, first, *carries, row(norm_gain)]
        if out is not None:
            in_specs.append(pl.BlockSpec(memory_space=pl.ANY))
            operands.append(out)
        return pl.pallas_call(
            functools.partial(final_kernel if out is None else final_into_kernel, first_head=g * heads, heads=all_heads),
            grid=(blocks,),
            in_specs=in_specs,
            out_specs=own,
            out_shape=shape((rows, channels), BF16),
            scratch_shapes=[
                pltpu.VMEM((spans, N, width), BF16),
                pltpu.VMEM((LANES, width), BF16),
                pltpu.VMEM((L, width), F32),
            ],
            input_output_aliases={} if out is None else {13: 0},
            compiler_params=params(1),
            cost_estimate=cost(6 * 10**9, 16),
            name="final",
        )(*operands)

    locals_ = [local(g) for g in range(parts)]
    carries = [travel(state, factor) for _, state, _, factor in locals_]
    out = None
    for g in range(parts):
        out = final(g, locals_[g][0], locals_[g][2], carries[g], out)
    return out


def solution(mesh):
    rows = P(("groups", "req"), "tp")
    placed = (rows,) * 5 + (P(None, "tp"),) * 3 + (P("tp"),) * 4 + (P(("groups", "req")),)
    return jax.shard_map(
        per_device,
        mesh=mesh,
        in_specs=placed,
        out_specs=rows,
        check_vma=False,
    )
```

profile of v0, /device:TPU:0, one launch (start us, length us, event | category | flops | bytes accessed | tf_op | source)
XLA Modules:
  0.0 97.3 jit_solution(10886698730594715223)
XLA Ops:
  0.0 0.0 copy-start.2
  0.0 3.4 %copy-done.2 = bf16[1024,4096]{1,0:T(8,128)(2,1)S(1)} copy-done((bf16[1024,4096]{1,0:T(8,128)(2,1)S(1)}, bf16[1024,4096]{1,0:T(8,128)(2,1)}, u32[]{:S(2)}) %copy-start.2) | copy-done | bytes 8388632
  3.4 1.2 %copy-done.4 = bf16[1024,512]{1,0:T(8,128)(2,1)S(1)} copy-done((bf16[1024,512]{1,0:T(8,128)(2,1)S(1)}, bf16[1024,512]{1,0:T(8,128)(2,1)}, u32[]{:S(2)}) %copy-start.4) | copy-done | bytes 1048600
  4.6 0.0 copy-start.6
  4.6 1.2 %copy-done.6 = bf16[1024,512]{1,0:T(8,128)(2,1)S(1)} copy-done((bf16[1024,512]{1,0:T(8,128)(2,1)S(1)}, bf16[1024,512]{1,0:T(8,128)(2,1)}, u32[]{:S(2)}) %copy-start.6) | copy-done | bytes 1048600
  5.8 0.0 copy-start.9
  5.8 0.7 copy-done.9
  6.5 0.0 copy-start.17
  6.5 0.0 copy-start.15
  6.5 0.0 copy-start.16
  6.5 0.6 tails.1
  7.2 2.4 %collective-permute-start = (bf16[3,5248]{1,0:T(4,128)(2,1)S(1)}, bf16[3,5248]{1,0:T(4,128)(2,1)S(1)}, u32[]{:S(2)}, u32[]{:S(2)}) collective-permute-start(bf16[3,5248]{1,0:T(4,128)(2,1)S(1)} %tails.1), channel_id=1, source_target_pairs={{0,4},{4,8},{8,12},{1,5},{5,9},{9,13},{2,6},{6,10},{10,14},{3,7},{... | collective-permute-start | bytes 94472 | tf_op jit(solution)/shard_map/ppermute | solution.py:330
  9.5 0.0 copy-done.17
  9.5 0.2 copy.15.dt_ref
  9.7 0.0 copy-done.14
  9.7 0.0 copy-done.15
  9.7 0.0 copy-done.16
  9.7 0.0 copy-start.5
  9.8 0.0 copy-start.7
  9.8 0.0 copy-start.10
  9.8 0.0 copy-start.12
  9.8 0.0 copy-start.13
  9.8 2.2 %decays.1 = (bf16[1024,128]{1,0:T(8,128)(2,1)S(1)}, bf16[1024,128]{1,0:T(8,128)(2,1)S(1)}, bf16[1024,128]{1,0:T(8,128)(2,1)S(1)}, bf16[2,16,128]{2,1,0:T(8,128)(2,1)S(1)}) custom-call(bf16[1024,64]{1,0:T(8,128)(2,1)S(1)} %copy.15.dt_ref, f32[1,64]{1,0:T(1,128)S(1)} %bitcast.16, f32[1,64]{1,0:T(1,128)S(1)} %bitcast.17, f32[1,64]{1,0:T(1,128)S(1)} %bitcast.18), custom_call_target="tpu_custom_call" | custom-call | flops 3000000000 | bytes 1048576 | tf_op jit(solution)/shard_map/decays/pallas_call | solution.py:334
  12.0 0.0 collective-permute-done.halo_ref.ids_ref
  12.0 0.0 copy-done.5
  12.1 0.0 copy-done.7
  12.1 0.0 copy-done.10
  12.1 0.0 copy-done.12
  12.1 0.0 copy-done.13
  12.1 0.0 copy-start.11
  12.1 5.8 %scores.1 = (bf16[2,1024,768]{2,1,0:T(8,128)(2,1)S(1)}, bf16[2,256,1024]{2,1,0:T(8,128)(2,1)S(1)}, f32[1024,128]{1,0:T(8,128)S(1)}, s32[4]{0:T(128)S(1)}) custom-call(s32[1024]{0:T(1024)S(1)} %copy-done.10, bf16[1024,512]{1,0:T(8,128)(2,1)S(1)} %copy-done.5, bf16[1024,512]{1,0:T(8,128)(2,1)S(1)} %copy-done.7, ...), custom_call_target="tpu_custom_call" | custom-call | flops 2000000000 | bytes 6291456 | tf_op jit(solution)/shard_map/scores/pallas_call | solution.py:345
  17.9 0.0 copy-start
  17.9 1.7 %copy-done = bf16[2,1024,768]{2,1,0:T(8,128)(2,1)} copy-done((bf16[2,1024,768]{2,1,0:T(8,128)(2,1)}, bf16[2,1024,768]{2,1,0:T(8,128)(2,1)S(1)}, u32[]{:S(2)}) %copy-start) | copy-done | bytes 3145752
  19.6 0.0 copy-done.11
  19.6 0.0 copy-start.3
  19.6 3.4 %copy-done.3 = bf16[1024,4096]{1,0:T(8,128)(2,1)S(1)} copy-done((bf16[1024,4096]{1,0:T(8,128)(2,1)S(1)}, bf16[1024,4096]{1,0:T(8,128)(2,1)}, u32[]{:S(2)}) %copy-start.3) | copy-done | bytes 8388632
  23.0 9.5 %state.3 = (bf16[1024,2048]{1,0:T(8,128)(2,1)S(1)}, bf16[256,2048]{1,0:T(8,128)(2,1)S(1)}, bf16[256,2048]{1,0:T(8,128)(2,1)S(1)}, f32[1,2048]{1,0:T(1,128)S(1)}) custom-call(s32[4]{0:T(128)S(1)} %get-tuple-element.21.info_ref.refs_0_, bf16[1024,4096]{1,0:T(8,128)(2,1)S(1)} %copy-done.3, bf16[3,5248]{1,0:T(4,128)(2,1)S(1)} %collective-permute-done.halo_ref.ids_ref, ...), custom_call_target="tpu_custom_call" | custom-call | flops 6000000000 | bytes 10485760 | tf_op jit(solution)/shard_map/state/pallas_call | solution.py:385
  32.5 0.0 slice-start
  32.5 0.0 slice-start.1
  32.5 4.8 %collective-permute-start.4 = (bf16[256,2048]{1,0:T(8,128)(2,1)S(1)}, bf16[256,2048]{1,0:T(8,128)(2,1)S(1)}, u32[]{:S(2)}, u32[]{:S(2)}) collective-permute-start(bf16[256,2048]{1,0:T(8,128)(2,1)S(1)} %get-tuple-element.35), channel_id=1, source_target_pairs={{0,4},{8,12},{1,5},{9,13},{2,6},{10,14},{3,7},{11,15},{16,20},{24,... | collective-permute-start | bytes 3145736 | tf_op jit(solution)/shard_map/ppermute | solution.py:424
  37.3 9.5 %state.2 = (bf16[1024,2048]{1,0:T(8,128)(2,1)S(1)}, bf16[256,2048]{1,0:T(8,128)(2,1)S(1)}, bf16[256,2048]{1,0:T(8,128)(2,1)S(1)}, f32[1,2048]{1,0:T(1,128)S(1)}) custom-call(s32[4]{0:T(128)S(1)} %get-tuple-element.21.info_ref.refs_0_, bf16[1024,4096]{1,0:T(8,128)(2,1)S(1)} %copy-done.3, bf16[3,5248]{1,0:T(4,128)(2,1)S(1)} %collective-permute-done.halo_ref.ids_ref, ...), custom_call_target="tpu_custom_call" | custom-call | flops 6000000000 | bytes 10485760 | tf_op jit(solution)/shard_map/state/pallas_call | solution.py:385
  46.9 1.4 %collective-permute-start.1 = (bf16[256,2048]{1,0:T(8,128)(2,1)S(1)}, bf16[256,2048]{1,0:T(8,128)(2,1)S(1)}, u32[]{:S(2)}, u32[]{:S(2)}) collective-permute-start(bf16[256,2048]{1,0:T(8,128)(2,1)S(1)} %get-tuple-element.31), channel_id=1, source_target_pairs={{0,4},{8,12},{1,5},{9,13},{2,6},{10,14},{3,7},{11,15},{16,20},{24,... | collective-permute-start | bytes 3145736 | tf_op jit(solution)/shard_map/ppermute | solution.py:424
  48.3 0.0 collective-permute-done.4.t0_ref
  48.3 0.4 add_convert_fusion
  48.7 0.7 collective-permute-start.5
  49.4 1.1 %collective-permute-done.1.refs_9_ = bf16[256,2048]{1,0:T(8,128)(2,1)S(1)} collective-permute-done((bf16[256,2048]{1,0:T(8,128)(2,1)S(1)}, bf16[256,2048]{1,0:T(8,128)(2,1)S(1)}, u32[]{:S(2)}, u32[]{:S(2)}) %collective-permute-start.1) | collective-permute-done | bytes 1048608 | tf_op jit(solution)/shard_map/ppermute | solution.py:424
  50.5 0.4 add_convert_fusion.1
  50.9 0.0 copy-start.1
  50.9 0.0 copy-start.8
  50.9 0.9 collective-permute-start.2
  51.8 0.0 collective-permute-done.5.t1_ref
  51.8 0.2 multiply_convert_fusion
  52.0 12.8 %collective-permute-start.6 = (bf16[256,2048]{1,0:T(8,128)(2,1)S(1)}, bf16[256,2048]{1,0:T(8,128)(2,1)S(1)}, u32[]{:S(2)}, u32[]{:S(2)}) collective-permute-start(bf16[256,2048]{1,0:T(8,128)(2,1)S(1)} %multiply_convert_fusion), channel_id=1, source_target_pairs={{0,4},{8,12},{1,5},{9,13},{2,6},{10,14},{3,7},{11,15},{16,20},{24,... | collective-permute-start | bytes 3145736 | tf_op jit(solution)/shard_map/ppermute | solution.py:430
  64.8 0.0 collective-permute-done.2.refs_10_
  64.8 0.2 multiply_convert_fusion.1
  65.0 11.0 %collective-permute-start.3 = (bf16[256,2048]{1,0:T(8,128)(2,1)S(1)}, bf16[256,2048]{1,0:T(8,128)(2,1)S(1)}, u32[]{:S(2)}, u32[]{:S(2)}) collective-permute-start(bf16[256,2048]{1,0:T(8,128)(2,1)S(1)} %multiply_convert_fusion.1), channel_id=1, source_target_pairs={{0,4},{8,12},{1,5},{9,13},{2,6},{10,14},{3,7},{11,15},{16,20},{24,... | collective-permute-start | bytes 3145736 | tf_op jit(solution)/shard_map/ppermute | solution.py:430
  76.0 0.0 collective-permute-done.6.t2_ref
  76.0 0.0 slice-done
  76.0 0.0 slice-done.1
  76.1 0.0 copy-done.1
  76.1 0.0 copy-done.8
  76.1 10.6 %final.2.refs_13_ = bf16[1024,4096]{1,0:T(8,128)(2,1)} custom-call(s32[4]{0:T(128)S(1)} %get-tuple-element.21.info_ref.refs_0_, bf16[1024,2048]{1,0:T(8,128)(2,1)S(1)} %get-tuple-element.33.u_ref.u_first_ref, bf16[1024,2048]{1,0:T(8,128)(2,1)S(1)} %get-tuple-element.33.u_ref.u_first_ref, bf16[1024,4096]{1,0:T(8,128)(2,1)S(1)} %bitcast.8, ...), custom_call_target="tpu_custom_call" | custom-call | flops 6000000000 | bytes 16777216 | tf_op jit(solution)/shard_map/final/pallas_call | solution.py:458
  86.7 0.0 collective-permute-done.3.refs_11_
  86.7 10.6 %final.3 = bf16[1024,4096]{1,0:T(8,128)(2,1)} custom-call(s32[4]{0:T(128)S(1)} %get-tuple-element.21.info_ref.refs_0_, bf16[1024,2048]{1,0:T(8,128)(2,1)S(1)} %get-tuple-element.26.refs_1_.refs_2_, bf16[1024,2048]{1,0:T(8,128)(2,1)S(1)} %get-tuple-element.26.refs_1_.refs_2_, bf16[1024,4096]{1,0:T(8,128)(2,1)S(1)} %bitcast.8, ...), custom_call_target="tpu_custom_call", output_to_operand_aliasing={{}: (13, {})} | custom-call | flops 6000000000 | bytes 16777216 | tf_op jit(solution)/shard_map/final/pallas_call | solution.py:458
  (3 shorter events, 0.0 us)
Async XLA Ops:
  0.0 3.4 %copy-start.2 = (bf16[1024,4096]{1,0:T(8,128)(2,1)S(1)}, bf16[1024,4096]{1,0:T(8,128)(2,1)}, u32[]{:S(2)}) copy-start(bf16[1024,4096]{1,0:T(8,128)(2,1)} %x_ref.5) | copy-start | bytes 25165828
  3.4 1.2 %copy-start.4 = (bf16[1024,512]{1,0:T(8,128)(2,1)S(1)}, bf16[1024,512]{1,0:T(8,128)(2,1)}, u32[]{:S(2)}) copy-start(bf16[1024,512]{1,0:T(8,128)(2,1)} %b_ref.3) | copy-start | bytes 3145732
  4.6 1.2 %copy-start.6 = (bf16[1024,512]{1,0:T(8,128)(2,1)S(1)}, bf16[1024,512]{1,0:T(8,128)(2,1)}, u32[]{:S(2)}) copy-start(bf16[1024,512]{1,0:T(8,128)(2,1)} %c_ref.3) | copy-start | bytes 3145732
  5.8 0.7 copy-start.9
  6.5 3.0 %copy-start.17 = (bf16[1024,64]{0,1:T(8,128)(2,1)S(1)}, bf16[1024,64]{0,1:T(8,128)(2,1)}, u32[]{:S(2)}) copy-start(bf16[1024,64]{0,1:T(8,128)(2,1)} %param.17) | copy-start | bytes 393220
  6.5 3.2 %copy-start.14 = (f32[64]{0:T(128)S(1)}, f32[64]{0:T(128)}, u32[]{:S(2)}) copy-start(f32[64]{0:T(128)} %param.21) | copy-start | bytes 772
  6.5 3.2 %copy-start.15 = (f32[64]{0:T(128)S(1)}, f32[64]{0:T(128)}, u32[]{:S(2)}) copy-start(f32[64]{0:T(128)} %param.22) | copy-start | bytes 772
  6.5 3.2 %copy-start.16 = (f32[64]{0:T(128)S(1)}, f32[64]{0:T(128)}, u32[]{:S(2)}) copy-start(f32[64]{0:T(128)} %param.23) | copy-start | bytes 772
  7.2 4.9 %collective-permute-start = (bf16[3,5248]{1,0:T(4,128)(2,1)S(1)}, bf16[3,5248]{1,0:T(4,128)(2,1)S(1)}, u32[]{:S(2)}, u32[]{:S(2)}) collective-permute-start(bf16[3,5248]{1,0:T(4,128)(2,1)S(1)} %tails.1), channel_id=1, source_target_pairs={{0,4},{4,8},{8,12},{1,5},{5,9},{9,13},{2,6},{6,10},{10,14},{3,7},{... | collective-permute-start | bytes 94472 | tf_op jit(solution)/shard_map/ppermute | solution.py:330
  9.7 2.3 %copy-start.5 = (bf16[1024,512]{1,0:T(8,128)(2,1)S(1)}, bf16[1024,512]{1,0:T(8,128)(2,1)}, u32[]{:S(2)}) copy-start(bf16[1024,512]{1,0:T(8,128)(2,1)} %b_ref.3) | copy-start | bytes 3145732
  9.8 2.3 %copy-start.7 = (bf16[1024,512]{1,0:T(8,128)(2,1)S(1)}, bf16[1024,512]{1,0:T(8,128)(2,1)}, u32[]{:S(2)}) copy-start(bf16[1024,512]{1,0:T(8,128)(2,1)} %c_ref.3) | copy-start | bytes 3145732
  9.8 2.3 %copy-start.10 = (s32[1024]{0:T(1024)S(1)}, s32[1024]{0:T(1024)}, u32[]{:S(2)}) copy-start(s32[1024]{0:T(1024)} %seg_s.3) | copy-start | bytes 12292
  9.8 2.3 %copy-start.12 = (bf16[4,512]{1,0:T(4,128)(2,1)S(1)}, bf16[4,512]{1,0:T(4,128)(2,1)}, u32[]{:S(2)}) copy-start(bf16[4,512]{1,0:T(4,128)(2,1)} %wb_ref.1) | copy-start | bytes 12292
  9.8 2.3 %copy-start.13 = (bf16[4,512]{1,0:T(4,128)(2,1)S(1)}, bf16[4,512]{1,0:T(4,128)(2,1)}, u32[]{:S(2)}) copy-start(bf16[4,512]{1,0:T(4,128)(2,1)} %wc_ref.1) | copy-start | bytes 12292
  12.1 7.5 %copy-start.11 = (bf16[4,4096]{1,0:T(4,128)(2,1)S(1)}, bf16[4,4096]{1,0:T(4,128)(2,1)}, u32[]{:S(2)}) copy-start(bf16[4,4096]{1,0:T(4,128)(2,1)} %w_ref.3) | copy-start | bytes 98308
  17.9 1.7 %copy-start = (bf16[2,1024,768]{2,1,0:T(8,128)(2,1)}, bf16[2,1024,768]{2,1,0:T(8,128)(2,1)S(1)}, u32[]{:S(2)}) copy-start(bf16[2,1024,768]{2,1,0:T(8,128)(2,1)S(1)} %get-tuple-element.27.m_ref.refs_4_) | copy-start | bytes 9437188
  19.6 3.4 %copy-start.3 = (bf16[1024,4096]{1,0:T(8,128)(2,1)S(1)}, bf16[1024,4096]{1,0:T(8,128)(2,1)}, u32[]{:S(2)}) copy-start(bf16[1024,4096]{1,0:T(8,128)(2,1)} %x_ref.5) | copy-start | bytes 25165828
  32.5 43.6 %slice-start = ((s8[8388608]{0:T(1024)(128)(4,1)}), s8[4194304]{0:T(1024)(128)(4,1)S(1)}, s32[]{:S(2)}) async-start(s8[8388608]{0:T(1024)(128)(4,1)} %bitcast.7), calls=%async_computation | async-start | bytes 8388608
  32.5 43.6 %slice-start.1 = ((s8[8388608]{0:T(1024)(128)(4,1)}), s8[4194304]{0:T(1024)(128)(4,1)S(1)}, s32[]{:S(2)}) async-start(s8[8388608]{0:T(1024)(128)(4,1)} %bitcast.7), calls=%async_computation.1 | async-start | bytes 8388608
  32.5 15.8 %collective-permute-start.4 = (bf16[256,2048]{1,0:T(8,128)(2,1)S(1)}, bf16[256,2048]{1,0:T(8,128)(2,1)S(1)}, u32[]{:S(2)}, u32[]{:S(2)}) collective-permute-start(bf16[256,2048]{1,0:T(8,128)(2,1)S(1)} %get-tuple-element.35), channel_id=1, source_target_pairs={{0,4},{8,12},{1,5},{9,13},{2,6},{10,14},{3,7},{11,15},{16,20},{24,... | collective-permute-start | bytes 3145736 | tf_op jit(solution)/shard_map/ppermute | solution.py:424
  46.9 3.6 %collective-permute-start.1 = (bf16[256,2048]{1,0:T(8,128)(2,1)S(1)}, bf16[256,2048]{1,0:T(8,128)(2,1)S(1)}, u32[]{:S(2)}, u32[]{:S(2)}) collective-permute-start(bf16[256,2048]{1,0:T(8,128)(2,1)S(1)} %get-tuple-element.31), channel_id=1, source_target_pairs={{0,4},{8,12},{1,5},{9,13},{2,6},{10,14},{3,7},{11,15},{16,20},{24,... | collective-permute-start | bytes 3145736 | tf_op jit(solution)/shard_map/ppermute | solution.py:424
  48.7 3.1 %collective-permute-start.5 = (bf16[256,2048]{1,0:T(8,128)(2,1)S(1)}, bf16[256,2048]{1,0:T(8,128)(2,1)S(1)}, u32[]{:S(2)}, u32[]{:S(2)}) collective-permute-start(bf16[256,2048]{1,0:T(8,128)(2,1)S(1)} %add_convert_fusion), channel_id=1, source_target_pairs={{4,8},{5,9},{6,10},{7,11},{20,24},{21,25},{22,26},{23,27}} | collective-permute-start | bytes 3145736 | tf_op jit(solution)/shard_map/ppermute | solution.py:429
  50.9 25.2 %copy-start.1 = (bf16[2,1024,768]{2,1,0:T(8,128)(2,1)S(1)}, bf16[2,1024,768]{2,1,0:T(8,128)(2,1)}, u32[]{:S(2)}) copy-start(bf16[2,1024,768]{2,1,0:T(8,128)(2,1)} %copy-done) | copy-start | bytes 9437188
  50.9 25.2 %copy-start.8 = (f32[4096]{0:T(1024)S(1)}, f32[4096]{0:T(1024)}, u32[]{:S(2)}) copy-start(f32[4096]{0:T(1024)} %param.24) | copy-start | bytes 49156
  50.9 13.9 %collective-permute-start.2 = (bf16[256,2048]{1,0:T(8,128)(2,1)S(1)}, bf16[256,2048]{1,0:T(8,128)(2,1)S(1)}, u32[]{:S(2)}, u32[]{:S(2)}) collective-permute-start(bf16[256,2048]{1,0:T(8,128)(2,1)S(1)} %add_convert_fusion.1), channel_id=1, source_target_pairs={{4,8},{5,9},{6,10},{7,11},{20,24},{21,25},{22,26},{23,27}} | collective-permute-start | bytes 3145736 | tf_op jit(solution)/shard_map/ppermute | solution.py:429
  52.0 24.0 %collective-permute-start.6 = (bf16[256,2048]{1,0:T(8,128)(2,1)S(1)}, bf16[256,2048]{1,0:T(8,128)(2,1)S(1)}, u32[]{:S(2)}, u32[]{:S(2)}) collective-permute-start(bf16[256,2048]{1,0:T(8,128)(2,1)S(1)} %multiply_convert_fusion), channel_id=1, source_target_pairs={{0,4},{8,12},{1,5},{9,13},{2,6},{10,14},{3,7},{11,15},{16,20},{24,... | collective-permute-start | bytes 3145736 | tf_op jit(solution)/shard_map/ppermute | solution.py:430
  65.0 21.7 %collective-permute-start.3 = (bf16[256,2048]{1,0:T(8,128)(2,1)S(1)}, bf16[256,2048]{1,0:T(8,128)(2,1)S(1)}, u32[]{:S(2)}, u32[]{:S(2)}) collective-permute-start(bf16[256,2048]{1,0:T(8,128)(2,1)S(1)} %multiply_convert_fusion.1), channel_id=1, source_target_pairs={{0,4},{8,12},{1,5},{9,13},{2,6},{10,14},{3,7},{11,15},{16,20},{24,... | collective-permute-start | bytes 3145736 | tf_op jit(solution)/shard_map/ppermute | solution.py:430
where the time goes:
time: 97.7 us; the launch traced here: 97.3 us
  Pallas kernels  48.9 us (50%)
  starting transfers between devices  33.9 us (35%)
  local copies, waits for them, and re-layouts  11.8 us (12%)
  other arithmetic  1.23 us (1%)
  waiting for transfers between devices  1.07 us (1%)
    ppermute x2, starting transfers between devices, travel(): passed = lax.ppermute(scaled(entering).astype(BF16), 'req', inside)  23.8 us
    pallas_call x2, Pallas kernels, final(): pl.pallas_call(functools.partial(final_kernel if out is None else final_i...  21.2 us
    pallas_call x2, Pallas kernels, local(): pl.pallas_call(functools.partial(state_kernel, first_head=g * heads, head...  19 us
    unnamed x41, local copies, waits for them, and re-layouts  11.8 us
    ppermute x2, starting transfers between devices, travel(): first = lax.ppermute(state, 'req', inside)  6.2 us
    pallas_call x1, Pallas kernels, per_device(): pl.pallas_call(functools.partial(score_kernel, parts=parts), grid=(spans,...  5.81 us
    ppermute x1, starting transfers between devices, per_device(): halo = lax.ppermute(tail, 'req', shift)  2.36 us
    pallas_call x1, Pallas kernels, per_device(): pl.pallas_call(decay_kernel, grid=(spans,), in_specs=[pl.BlockSpec((SPAN,...  2.23 us
  transfers between devices with their start and end apart: 7, of which 1 were waited for; matrix products, arithmetic and copies ran while one was open for 1% of the time, Pallas kernels for 23%

commit v1 on v0

--- a/solution.py
+++ b/solution.py
@@ -277,6 +277,17 @@
         rows(True)
 
 
+def state_after_kernel(*refs, first_head, heads):
+    state_kernel(*refs[:8], *refs[9:], first_head=first_head, heads=heads)
+
+
+def scale_kernel(value_ref, factor_ref, *refs):
+    out_ref = refs[-1]
+    for row in range(0, N, 64):
+        rows = slice(row, row + 64)
+        out_ref[rows] = (factor_ref[...] * value_ref[rows].astype(F32)).astype(BF16)
+
+
 def final_into_kernel(*refs, first_head, heads):
     final_kernel(*refs[:13], *refs[14:], first_head=first_head, heads=heads)
 
@@ -306,6 +317,7 @@
     def cost(flops, mib):
         return pl.CostEstimate(flops=flops, bytes_accessed=mib << 20, transcendentals=0)
 
+    x_in, b_in, c_in = (pltpu.with_memory_space_constraint(value, pltpu.HBM) for value in (x_in, b_in, c_in))
     shift = [(k, k + 1) for k in range(devices - 1)]
     inside = [(k, k + 1) for k in range(0, devices - 1, 2)]
     across = [(k, k + 1) for k in range(1, devices - 1, 2)]
@@ -379,11 +391,13 @@
 
     em_spec = lambda: pl.BlockSpec((spans, 16, LANES), lambda *_: (0, 0, 0))
 
-    def local(g):
+    anywhere = pl.BlockSpec(memory_space=pl.ANY)
+
+    def local(g, token):
         steps = width // step_width
         at_cols = lambda j, k: (0, g * steps + j)
         return pl.pallas_call(
-            functools.partial(state_kernel, first_head=g * heads, heads=all_heads),
+            functools.partial(state_kernel if token is None else state_after_kernel, first_head=g * heads, heads=all_heads),
             grid=(steps, spans),
             in_specs=[
                 smem,
@@ -394,7 +408,8 @@
                 pl.BlockSpec((SPAN, LANES), lambda j, k: (k, 0)),
                 em_spec(),
                 pl.BlockSpec((SPAN, LANES), lambda j, k: (k, 0)),
-            ],
+            ]
+            + ([] if token is None else [anywhere]),
             out_specs=[
                 pl.BlockSpec((SPAN, step_width), lambda j, k: (k, j)),
                 pl.BlockSpec((N, step_width), lambda j, k: (0, j)),
@@ -415,21 +430,33 @@
             compiler_params=params(2),
             cost_estimate=cost(6 * 10**9, 10),
             name="state",
-        )(info, x_in, halo, conv_x, bt, a_hl, em, code)
-
-    def travel(state, factor):
-        def scaled(value):
-            return factor * value.astype(F32)
-
-        first = lax.ppermute(state, "req", inside)
-        leaving = (state.astype(F32) + scaled(first)).astype(BF16)
+        )(info, x_in, halo, conv_x, bt, a_hl, em, code, *([] if token is None else [token]))
+
+    def scaled(value, factor, token):
+        tokens = [] if token is None else [token]
+        whole_spec = lambda array: pl.BlockSpec(array.shape, whole)
+        return pl.pallas_call(
+            scale_kernel,
+            grid=(1,),
+            in_specs=[whole_spec(value), whole_spec(factor)] + [anywhere] * len(tokens),
+            out_specs=whole_spec(value),
+            out_shape=shape(value.shape, BF16),
+            compiler_params=params(1),
+            cost_estimate=cost(10**6, 2),
+            name="scale",
+        )(value, factor, *tokens)
+
+    def leave(state, first, factor):
+        return (state.astype(F32) + factor * first.astype(F32)).astype(BF16)
+
+    def travel(state, first, leaving, factor, token):
         entering, passed = jnp.zeros_like(state), jnp.zeros_like(state)
         rounds = devices // 2 - 1
         for turn in range(rounds):
             entering = lax.ppermute(leaving, "req", across)
-            passed = lax.ppermute(scaled(entering).astype(BF16), "req", inside)
+            passed = lax.ppermute(scaled(entering, factor, token), "req", inside)
             if turn < rounds - 1:
-                leaving = (state.astype(F32) + scaled(first.astype(F32) + passed.astype(F32))).astype(BF16)
+                leaving = leave(state, first.astype(F32) + passed.astype(F32), factor)
         return first, entering, passed
 
     def final(g, u, first, carries, out):
@@ -472,11 +499,16 @@
             name="final",
         )(*operands)
 
-    locals_ = [local(g) for g in range(parts)]
-    carries = [travel(state, factor) for _, state, _, factor in locals_]
+    leaving, locals_ = None, []
+    for g in range(parts):
+        u, state, inner, factor = local(g, leaving)
+        first = lax.ppermute(state, "req", inside)
+        leaving = leave(state, first, factor)
+        locals_.append((u, inner, state, first, leaving, factor))
     out = None
     for g in range(parts):
-        out = final(g, locals_[g][0], locals_[g][2], carries[g], out)
+        u, inner, *sent = locals_[g]
+        out = final(g, u, inner, travel(*sent, out), out)
     return out
 
 

time: 97.7 us -> 81.4 us (0.83)
  the two profiles are of different devices: /device:TPU:0 before, /device:TPU:11 now
where the time goes in v1:
time: 81.4 us; the launch traced here: 80.4 us
  Pallas kernels  51.6 us (63%)
  waiting for transfers between devices  14.9 us (18%)
  starting transfers between devices  8.36 us (10%)
  local copies, waits for them, and re-layouts  4.31 us (5%)
  other arithmetic  0.87 us (1%)
    pallas_call x2, Pallas kernels, final(): pl.pallas_call(functools.partial(final_kernel if out is None else final_i...  21.1 us
    pallas_call x2, Pallas kernels, local(): pl.pallas_call(functools.partial(state_kernel if token is None else state...  20.5 us
    ppermute x2, waiting for transfers between devices, travel(): passed = lax.ppermute(scaled(entering, factor, token), 'req', inside)  8.85 us
    pallas_call x1, Pallas kernels, per_device(): pl.pallas_call(functools.partial(score_kernel, parts=parts), grid=(spans,...  6.4 us
    ppermute x2, waiting for transfers between devices, per_device(): first = lax.ppermute(state, 'req', inside)  6.02 us
    unnamed x35, local copies, waits for them, and re-layouts  4.31 us
    ppermute x2, starting transfers between devices, travel(): passed = lax.ppermute(scaled(entering, factor, token), 'req', inside)  2.72 us
    ppermute x2, starting transfers between devices, per_device(): first = lax.ppermute(state, 'req', inside)  2.58 us
  transfers between devices with their start and end apart: 7, of which 4 were waited for; matrix products, arithmetic and copies ran while one was open for 1% of the time, Pallas kernels for 29%

profile of v1, /device:TPU:11, one launch (start us, length us, event | category | flops | bytes accessed | tf_op | source)
XLA Modules:
  0.0 80.4 jit_solution(6378164106228480059)
XLA Ops:
  0.0 0.0 copy-start.6
  0.0 0.7 copy-done.6
  0.7 0.0 copy-start.14
  0.7 0.0 copy-start.11
  0.7 0.0 copy-start.12
  0.7 0.0 copy-start.13
  0.7 1.0 %tails.1 = bf16[3,5248]{1,0:T(4,128)(2,1)S(1)} custom-call(s32[1024]{0:T(1024)S(1)} %copy-done.6, bf16[1024,4096]{1,0:T(8,128)(2,1)} %refs_1_.1, bf16[1024,512]{1,0:T(8,128)(2,1)} %b_ref.3, bf16[1024,512]{1,0:T(8,128)(2,1)} %c_ref.3), custom_call_target="tpu_custom_call" | custom-call | flops 1000 | tf_op jit(solution)/shard_map/tails/pallas_call | solution.py:327
  1.7 1.3 %collective-permute-start = (bf16[3,5248]{1,0:T(4,128)(2,1)S(1)}, bf16[3,5248]{1,0:T(4,128)(2,1)S(1)}, u32[]{:S(2)}, u32[]{:S(2)}) collective-permute-start(bf16[3,5248]{1,0:T(4,128)(2,1)S(1)} %tails.1), channel_id=1, source_target_pairs={{0,4},{4,8},{8,12},{1,5},{5,9},{9,13},{2,6},{6,10},{10,14},{3,7},{... | collective-permute-start | bytes 94472 | tf_op jit(solution)/shard_map/ppermute | solution.py:342
  3.0 0.0 copy-done.14
  3.0 0.2 copy.15.dt_ref
  3.2 0.0 copy-done.11
  3.2 0.0 copy-done.12
  3.2 0.0 copy-done.13
  3.2 0.0 copy-start.7
  3.2 0.0 copy-start.9
  3.2 0.0 copy-start.10
  3.2 2.2 %decays.1 = (bf16[1024,128]{1,0:T(8,128)(2,1)S(1)}, bf16[1024,128]{1,0:T(8,128)(2,1)S(1)}, bf16[1024,128]{1,0:T(8,128)(2,1)S(1)}, bf16[2,16,128]{2,1,0:T(8,128)(2,1)S(1)}) custom-call(bf16[1024,64]{1,0:T(8,128)(2,1)S(1)} %copy.15.dt_ref, f32[1,64]{1,0:T(1,128)S(1)} %bitcast.14, f32[1,64]{1,0:T(1,128)S(1)} %bitcast.15, f32[1,64]{1,0:T(1,128)S(1)} %bitcast.16), custom_call_target="tpu_custom_call" | custom-call | flops 3000000000 | bytes 1048576 | tf_op jit(solution)/shard_map/decays/pallas_call | solution.py:346
  5.5 0.0 copy-start.1
  5.5 0.0 collective-permute-done.halo_ref.ids_ref.refs_2_
  5.5 0.0 copy-done.7
  5.5 0.0 copy-done.9
  5.5 0.0 copy-done.10
  5.5 0.0 copy-start.8
  5.5 6.4 %scores.1 = (bf16[2,1024,768]{2,1,0:T(8,128)(2,1)S(1)}, bf16[2,256,1024]{2,1,0:T(8,128)(2,1)S(1)}, f32[1024,128]{1,0:T(8,128)S(1)}, s32[4]{0:T(128)S(1)}) custom-call(s32[1024]{0:T(1024)S(1)} %copy-done.7, bf16[1024,512]{1,0:T(8,128)(2,1)} %b_ref.3, bf16[1024,512]{1,0:T(8,128)(2,1)} %c_ref.3, ...), custom_call_target="tpu_custom_call" | custom-call | flops 2000000000 | bytes 6291456 | tf_op jit(solution)/shard_map/scores/pallas_call | solution.py:357
  12.0 0.0 copy-done.8
  12.0 9.9 %state.2 = (bf16[1024,2048]{1,0:T(8,128)(2,1)S(1)}, bf16[256,2048]{1,0:T(8,128)(2,1)S(1)}, bf16[256,2048]{1,0:T(8,128)(2,1)S(1)}, f32[1,2048]{1,0:T(1,128)S(1)}) custom-call(s32[4]{0:T(128)S(1)} %get-tuple-element.21.info_ref.refs_0_, bf16[1024,4096]{1,0:T(8,128)(2,1)} %refs_1_.1, bf16[3,5248]{1,0:T(4,128)(2,1)S(1)} %collective-permute-done.halo_ref.ids_ref.refs_2_, ...), custom_call_target="tpu_custom_call" | custom-call | flops 6000000000 | bytes 10485760 | tf_op jit(solution)/shard_map/state/pallas_call | solution.py:399
  21.9 1.3 %collective-permute-start.1 = (bf16[256,2048]{1,0:T(8,128)(2,1)S(1)}, bf16[256,2048]{1,0:T(8,128)(2,1)S(1)}, u32[]{:S(2)}, u32[]{:S(2)}) collective-permute-start(bf16[256,2048]{1,0:T(8,128)(2,1)S(1)} %get-tuple-element.26), channel_id=1, source_target_pairs={{0,4},{8,12},{1,5},{9,13},{2,6},{10,14},{3,7},{11,15},{16,20},{24,... | collective-permute-start | bytes 3145736 | tf_op jit(solution)/shard_map/ppermute | solution.py:505
  23.2 4.3 %collective-permute-done.1.t0_ref = bf16[256,2048]{1,0:T(8,128)(2,1)S(1)} collective-permute-done((bf16[256,2048]{1,0:T(8,128)(2,1)S(1)}, bf16[256,2048]{1,0:T(8,128)(2,1)S(1)}, u32[]{:S(2)}, u32[]{:S(2)}) %collective-permute-start.1) | collective-permute-done | bytes 1048608 | tf_op jit(solution)/shard_map/ppermute | solution.py:505
  27.5 0.0 slice-start
  27.5 0.4 add_convert_fusion.1.refs_8_
  27.9 0.0 slice-start.1
  27.9 0.9 %collective-permute-start.4 = (bf16[256,2048]{1,0:T(8,128)(2,1)S(1)}, bf16[256,2048]{1,0:T(8,128)(2,1)S(1)}, u32[]{:S(2)}, u32[]{:S(2)}) collective-permute-start(bf16[256,2048]{1,0:T(8,128)(2,1)S(1)} %add_convert_fusion.1.refs_8_), channel_id=1, source_target_pairs={{4,8},{5,9},{6,10},{7,11},{20,24},{21,25},{22,26},{23,27}} | collective-permute-start | bytes 3145736 | tf_op jit(solution)/shard_map/ppermute | solution.py:456
  28.8 10.6 %state.3 = (bf16[1024,2048]{1,0:T(8,128)(2,1)S(1)}, bf16[256,2048]{1,0:T(8,128)(2,1)S(1)}, bf16[256,2048]{1,0:T(8,128)(2,1)S(1)}, f32[1,2048]{1,0:T(1,128)S(1)}) custom-call(s32[4]{0:T(128)S(1)} %get-tuple-element.21.info_ref.refs_0_, bf16[1024,4096]{1,0:T(8,128)(2,1)} %refs_1_.1, bf16[3,5248]{1,0:T(4,128)(2,1)S(1)} %collective-permute-done.halo_ref.ids_ref.refs_2_, ...), custom_call_target="tpu_custom_call" | custom-call | flops 6000000000 | bytes 10485760 | tf_op jit(solution)/shard_map/state/pallas_call | solution.py:399
  39.4 0.0 copy-start.3
  39.4 1.3 %collective-permute-start.2 = (bf16[256,2048]{1,0:T(8,128)(2,1)S(1)}, bf16[256,2048]{1,0:T(8,128)(2,1)S(1)}, u32[]{:S(2)}, u32[]{:S(2)}) collective-permute-start(bf16[256,2048]{1,0:T(8,128)(2,1)S(1)} %get-tuple-element.33), channel_id=1, source_target_pairs={{0,4},{8,12},{1,5},{9,13},{2,6},{10,14},{3,7},{11,15},{16,20},{24,... | collective-permute-start | bytes 3145736 | tf_op jit(solution)/shard_map/ppermute | solution.py:505
  40.7 0.0 collective-permute-done.4.value_ref.t1_ref
  40.7 0.2 scale.2
  40.9 0.0 copy-start.5
  40.9 1.3 %collective-permute-start.5 = (bf16[256,2048]{1,0:T(8,128)(2,1)S(1)}, bf16[256,2048]{1,0:T(8,128)(2,1)S(1)}, u32[]{:S(2)}, u32[]{:S(2)}) collective-permute-start(bf16[256,2048]{1,0:T(8,128)(2,1)S(1)} %scale.2), channel_id=1, source_target_pairs={{0,4},{8,12},{1,5},{9,13},{2,6},{10,14},{3,7},{11,15},{16,20},{24,... | collective-permute-start | bytes 3145736 | tf_op jit(solution)/shard_map/ppermute | solution.py:457
  42.2 1.8 %collective-permute-done.2.refs_9_ = bf16[256,2048]{1,0:T(8,128)(2,1)S(1)} collective-permute-done((bf16[256,2048]{1,0:T(8,128)(2,1)S(1)}, bf16[256,2048]{1,0:T(8,128)(2,1)S(1)}, u32[]{:S(2)}, u32[]{:S(2)}) %collective-permute-start.2) | collective-permute-done | bytes 1048608 | tf_op jit(solution)/shard_map/ppermute | solution.py:505
  43.9 0.5 add_convert_fusion
  44.4 0.0 copy-done.3
  44.4 0.9 %collective-permute-start.3 = (bf16[256,2048]{1,0:T(8,128)(2,1)S(1)}, bf16[256,2048]{1,0:T(8,128)(2,1)S(1)}, u32[]{:S(2)}, u32[]{:S(2)}) collective-permute-start(bf16[256,2048]{1,0:T(8,128)(2,1)S(1)} %add_convert_fusion), channel_id=1, source_target_pairs={{4,8},{5,9},{6,10},{7,11},{20,24},{21,25},{22,26},{23,27}} | collective-permute-start | bytes 3145736 | tf_op jit(solution)/shard_map/ppermute | solution.py:456
  45.3 2.7 %collective-permute-done.5.t2_ref = bf16[256,2048]{1,0:T(8,128)(2,1)S(1)} collective-permute-done((bf16[256,2048]{1,0:T(8,128)(2,1)S(1)}, bf16[256,2048]{1,0:T(8,128)(2,1)S(1)}, u32[]{:S(2)}, u32[]{:S(2)}) %collective-permute-start.5) | collective-permute-done | bytes 1048608 | tf_op jit(solution)/shard_map/ppermute | solution.py:457
  48.0 0.0 copy-done.1
  48.0 0.0 slice-done
  48.0 0.0 slice-done.1
  48.0 0.0 copy-done.5
  48.1 10.5 %final.2.refs_0_.refs_13_ = bf16[1024,4096]{1,0:T(8,128)(2,1)} custom-call(s32[4]{0:T(128)S(1)} %get-tuple-element.21.info_ref.refs_0_, bf16[1024,2048]{1,0:T(8,128)(2,1)S(1)} %get-tuple-element.35.u_ref.u_first_ref, bf16[1024,2048]{1,0:T(8,128)(2,1)S(1)} %get-tuple-element.35.u_ref.u_first_ref, bf16[1024,4096]{1,0:T(8,128)(2,1)S(1)} %bitcast.8, ...), custom_call_target="tpu_custom_call" | custom-call | flops 6000000000 | bytes 16777216 | tf_op jit(solution)/shard_map/final/pallas_call | solution.py:485
  58.5 0.0 collective-permute-done.3.value_ref.refs_10_
  58.5 0.0 copy-start
  58.6 3.4 %copy-done = bf16[1024,4096]{1,0:T(8,128)(2,1)S(1)} copy-done((bf16[1024,4096]{1,0:T(8,128)(2,1)S(1)}, bf16[1024,4096]{1,0:T(8,128)(2,1)}, u32[]{:S(2)}) %copy-start) | copy-done | bytes 8388632
  61.9 0.0 copy-start.2
  61.9 0.0 copy-start.4
  61.9 0.2 scale.3
  62.1 1.4 %collective-permute-start.6 = (bf16[256,2048]{1,0:T(8,128)(2,1)S(1)}, bf16[256,2048]{1,0:T(8,128)(2,1)S(1)}, u32[]{:S(2)}, u32[]{:S(2)}) collective-permute-start(bf16[256,2048]{1,0:T(8,128)(2,1)S(1)} %scale.3), channel_id=1, source_target_pairs={{0,4},{8,12},{1,5},{9,13},{2,6},{10,14},{3,7},{11,15},{16,20},{24,... | collective-permute-start | bytes 3145736 | tf_op jit(solution)/shard_map/ppermute | solution.py:457
  63.5 6.2 %collective-permute-done.6.refs_11_ = bf16[256,2048]{1,0:T(8,128)(2,1)S(1)} collective-permute-done((bf16[256,2048]{1,0:T(8,128)(2,1)S(1)}, bf16[256,2048]{1,0:T(8,128)(2,1)S(1)}, u32[]{:S(2)}, u32[]{:S(2)}) %collective-permute-start.6) | collective-permute-done | bytes 1048608 | tf_op jit(solution)/shard_map/ppermute | solution.py:457
  69.7 0.0 copy-done.2
  69.7 0.0 copy-done.4
  69.7 10.6 %final.3 = bf16[1024,4096]{1,0:T(8,128)(2,1)} custom-call(s32[4]{0:T(128)S(1)} %get-tuple-element.21.info_ref.refs_0_, bf16[1024,2048]{1,0:T(8,128)(2,1)S(1)} %get-tuple-element.28.refs_1_.refs_2_, bf16[1024,2048]{1,0:T(8,128)(2,1)S(1)} %get-tuple-element.28.refs_1_.refs_2_, bf16[1024,4096]{1,0:T(8,128)(2,1)S(1)} %bitcast.8, ...), custom_call_target="tpu_custom_call", output_to_operand_aliasing={{}: (13, {})} | custom-call | flops 6000000000 | bytes 16777216 | tf_op jit(solution)/shard_map/final/pallas_call | solution.py:485
  (1 shorter events, 0.0 us)
Async XLA Ops:
  0.0 0.7 copy-start.6
  0.7 2.3 %copy-start.14 = (bf16[1024,64]{0,1:T(8,128)(2,1)S(1)}, bf16[1024,64]{0,1:T(8,128)(2,1)}, u32[]{:S(2)}) copy-start(bf16[1024,64]{0,1:T(8,128)(2,1)} %param.17) | copy-start | bytes 393220
  0.7 2.5 %copy-start.11 = (f32[64]{0:T(128)S(1)}, f32[64]{0:T(128)}, u32[]{:S(2)}) copy-start(f32[64]{0:T(128)} %param.21) | copy-start | bytes 772
  0.7 2.5 %copy-start.12 = (f32[64]{0:T(128)S(1)}, f32[64]{0:T(128)}, u32[]{:S(2)}) copy-start(f32[64]{0:T(128)} %param.22) | copy-start | bytes 772
  0.7 2.5 %copy-start.13 = (f32[64]{0:T(128)S(1)}, f32[64]{0:T(128)}, u32[]{:S(2)}) copy-start(f32[64]{0:T(128)} %param.23) | copy-start | bytes 772
  1.7 3.8 %collective-permute-start = (bf16[3,5248]{1,0:T(4,128)(2,1)S(1)}, bf16[3,5248]{1,0:T(4,128)(2,1)S(1)}, u32[]{:S(2)}, u32[]{:S(2)}) collective-permute-start(bf16[3,5248]{1,0:T(4,128)(2,1)S(1)} %tails.1), channel_id=1, source_target_pairs={{0,4},{4,8},{8,12},{1,5},{5,9},{9,13},{2,6},{6,10},{10,14},{3,7},{... | collective-permute-start | bytes 94472 | tf_op jit(solution)/shard_map/ppermute | solution.py:342
  3.2 2.3 %copy-start.7 = (s32[1024]{0:T(1024)S(1)}, s32[1024]{0:T(1024)}, u32[]{:S(2)}) copy-start(s32[1024]{0:T(1024)} %seg_s.3) | copy-start | bytes 12292
  3.2 2.3 %copy-start.9 = (bf16[4,512]{1,0:T(4,128)(2,1)S(1)}, bf16[4,512]{1,0:T(4,128)(2,1)}, u32[]{:S(2)}) copy-start(bf16[4,512]{1,0:T(4,128)(2,1)} %wb_ref.1) | copy-start | bytes 12292
  3.2 2.3 %copy-start.10 = (bf16[4,512]{1,0:T(4,128)(2,1)S(1)}, bf16[4,512]{1,0:T(4,128)(2,1)}, u32[]{:S(2)}) copy-start(bf16[4,512]{1,0:T(4,128)(2,1)} %wc_ref.1) | copy-start | bytes 12292
  5.5 42.5 %copy-start.1 = (bf16[1024,128]{1,0:T(8,128)(2,1)}, bf16[1024,128]{1,0:T(8,128)(2,1)S(1)}, u32[]{:S(2)}) copy-start(bf16[1024,128]{1,0:T(8,128)(2,1)S(1)} %get-tuple-element.31.w_ref.refs_6_) | copy-start | bytes 786436
  5.5 6.4 %copy-start.8 = (bf16[4,4096]{1,0:T(4,128)(2,1)S(1)}, bf16[4,4096]{1,0:T(4,128)(2,1)}, u32[]{:S(2)}) copy-start(bf16[4,4096]{1,0:T(4,128)(2,1)} %refs_3_.2) | copy-start | bytes 98308
  21.9 5.6 %collective-permute-start.1 = (bf16[256,2048]{1,0:T(8,128)(2,1)S(1)}, bf16[256,2048]{1,0:T(8,128)(2,1)S(1)}, u32[]{:S(2)}, u32[]{:S(2)}) collective-permute-start(bf16[256,2048]{1,0:T(8,128)(2,1)S(1)} %get-tuple-element.26), channel_id=1, source_target_pairs={{0,4},{8,12},{1,5},{9,13},{2,6},{10,14},{3,7},{11,15},{16,20},{24,... | collective-permute-start | bytes 3145736 | tf_op jit(solution)/shard_map/ppermute | solution.py:505
  27.5 20.6 %slice-start = ((s8[8388608]{0:T(1024)(128)(4,1)}), s8[4194304]{0:T(1024)(128)(4,1)S(1)}, s32[]{:S(2)}) async-start(s8[8388608]{0:T(1024)(128)(4,1)} %bitcast.7), calls=%async_computation | async-start | bytes 8388608
  27.9 20.2 %slice-start.1 = ((s8[8388608]{0:T(1024)(128)(4,1)}), s8[4194304]{0:T(1024)(128)(4,1)S(1)}, s32[]{:S(2)}) async-start(s8[8388608]{0:T(1024)(128)(4,1)} %bitcast.7), calls=%async_computation.1 | async-start | bytes 8388608
  27.9 12.8 %collective-permute-start.4 = (bf16[256,2048]{1,0:T(8,128)(2,1)S(1)}, bf16[256,2048]{1,0:T(8,128)(2,1)S(1)}, u32[]{:S(2)}, u32[]{:S(2)}) collective-permute-start(bf16[256,2048]{1,0:T(8,128)(2,1)S(1)} %add_convert_fusion.1.refs_8_), channel_id=1, source_target_pairs={{4,8},{5,9},{6,10},{7,11},{20,24},{21,25},{22,26},{23,27}} | collective-permute-start | bytes 3145736 | tf_op jit(solution)/shard_map/ppermute | solution.py:456
  39.4 5.0 %copy-start.3 = (bf16[256,2048]{1,0:T(8,128)(2,1)}, bf16[256,2048]{1,0:T(8,128)(2,1)S(1)}, u32[]{:S(2)}) copy-start(bf16[256,2048]{1,0:T(8,128)(2,1)S(1)} %get-tuple-element.32.refs_8_) | copy-start | bytes 3145732
  39.4 4.6 %collective-permute-start.2 = (bf16[256,2048]{1,0:T(8,128)(2,1)S(1)}, bf16[256,2048]{1,0:T(8,128)(2,1)S(1)}, u32[]{:S(2)}, u32[]{:S(2)}) collective-permute-start(bf16[256,2048]{1,0:T(8,128)(2,1)S(1)} %get-tuple-element.33), channel_id=1, source_target_pairs={{0,4},{8,12},{1,5},{9,13},{2,6},{10,14},{3,7},{11,15},{16,20},{24,... | collective-permute-start | bytes 3145736 | tf_op jit(solution)/shard_map/ppermute | solution.py:505
  40.9 7.2 %copy-start.5 = (f32[4096]{0:T(1024)S(1)}, f32[4096]{0:T(1024)}, u32[]{:S(2)}) copy-start(f32[4096]{0:T(1024)} %param.24) | copy-start | bytes 49156
  40.9 7.2 %collective-permute-start.5 = (bf16[256,2048]{1,0:T(8,128)(2,1)S(1)}, bf16[256,2048]{1,0:T(8,128)(2,1)S(1)}, u32[]{:S(2)}, u32[]{:S(2)}) collective-permute-start(bf16[256,2048]{1,0:T(8,128)(2,1)S(1)} %scale.2), channel_id=1, source_target_pairs={{0,4},{8,12},{1,5},{9,13},{2,6},{10,14},{3,7},{11,15},{16,20},{24,... | collective-permute-start | bytes 3145736 | tf_op jit(solution)/shard_map/ppermute | solution.py:457
  44.4 14.1 %collective-permute-start.3 = (bf16[256,2048]{1,0:T(8,128)(2,1)S(1)}, bf16[256,2048]{1,0:T(8,128)(2,1)S(1)}, u32[]{:S(2)}, u32[]{:S(2)}) collective-permute-start(bf16[256,2048]{1,0:T(8,128)(2,1)S(1)} %add_convert_fusion), channel_id=1, source_target_pairs={{4,8},{5,9},{6,10},{7,11},{20,24},{21,25},{22,26},{23,27}} | collective-permute-start | bytes 3145736 | tf_op jit(solution)/shard_map/ppermute | solution.py:456
  58.5 3.4 %copy-start = (bf16[1024,4096]{1,0:T(8,128)(2,1)S(1)}, bf16[1024,4096]{1,0:T(8,128)(2,1)}, u32[]{:S(2)}) copy-start(bf16[1024,4096]{1,0:T(8,128)(2,1)} %final.2.refs_0_.refs_13_) | copy-start | bytes 25165828
  61.9 7.8 %copy-start.2 = (bf16[1024,128]{1,0:T(8,128)(2,1)S(1)}, bf16[1024,128]{1,0:T(8,128)(2,1)}, u32[]{:S(2)}) copy-start(bf16[1024,128]{1,0:T(8,128)(2,1)} %copy-done.1) | copy-start | bytes 786436
  61.9 7.8 %copy-start.4 = (bf16[256,2048]{1,0:T(8,128)(2,1)S(1)}, bf16[256,2048]{1,0:T(8,128)(2,1)}, u32[]{:S(2)}) copy-start(bf16[256,2048]{1,0:T(8,128)(2,1)} %copy-done.3) | copy-start | bytes 3145732
  62.1 7.6 %collective-permute-start.6 = (bf16[256,2048]{1,0:T(8,128)(2,1)S(1)}, bf16[256,2048]{1,0:T(8,128)(2,1)S(1)}, u32[]{:S(2)}, u32[]{:S(2)}) collective-permute-start(bf16[256,2048]{1,0:T(8,128)(2,1)S(1)} %scale.3), channel_id=1, source_target_pairs={{0,4},{8,12},{1,5},{9,13},{2,6},{10,14},{3,7},{11,15},{16,20},{24,... | collective-permute-start | bytes 3145736 | tf_op jit(solution)/shard_map/ppermute | solution.py:457

commit v2 on v1

--- a/solution.py
+++ b/solution.py
@@ -84,22 +84,44 @@
     em_ref[0] = split_high_low(jnp.broadcast_to(jnp.exp(middle), (16, LANES)), heads)
 
 
-def score_kernel(
-    seg_s, b_ref, c_ref, halo_ref, ids_ref, wb_ref, wc_ref, seg_ref,
-    m_ref, bt_ref, code_ref, info_ref,
-    bc_buf, seg_buf, held, *, parts
+def fill_conv(buf, held, source, halo_ref, weights_ref, codes, span):
+    pieces = source.shape[1] // LANES
+
+    @pl.when(span == 0)
+    def _():
+        for piece in range(pieces):
+            buf[piece, 8 - REACH : 8, :] = halo_ref[:, piece * LANES : (piece + 1) * LANES].astype(F32)
+
+    @pl.when(span > 0)
+    def _():
+        for piece in range(pieces):
+            buf[piece, 0:8, :] = buf[piece, SPAN : SPAN + 8, :]
+
+    weights = 0.5 * weights_ref[...].astype(F32)
+    for piece in range(pieces):
+        lanes = slice(piece * LANES, (piece + 1) * LANES)
+        buf[piece, 8 : 8 + SPAN, :] = source[:, lanes].astype(F32)
+        for row in range(0, SPAN, TILE):
+            acc = conv_tile(buf, piece, weights[:, lanes], row, TILE, codes[row : row + TILE, :])
+            held[row : row + TILE, lanes] = silu_of_half(acc)
+
+
+def entering_id(ids, k):
+    return (jnp.max(ids[k : k + 1]) - 1.0).astype(jnp.int32)
+
+
+def b_kernel(
+    seg_s, b_ref, halo_ref, ids_ref, wb_ref, seg_ref,
+    bs_ref, bt_ref, code_ref, info_ref,
+    buf, seg_buf, held, *, parts
 ):
     span = pl.program_id(0)
-    width = parts * N
-    pieces = width // LANES
     ids = ids_ref[...].astype(F32)
     start = span * SPAN
     first = seg_s[start]
     last = seg_s[start + SPAN - 1]
-    oldest_device = (jnp.max(ids[0:1]) - 1.0).astype(jnp.int32)
-    before_device = (jnp.max(ids[REACH - 1 : REACH]) - 1.0).astype(jnp.int32)
-    before = jnp.where(span == 0, before_device, seg_s[jnp.maximum(start - 1, 0)])
-    oldest = jnp.where(span == 0, oldest_device, seg_s[jnp.maximum(start - REACH, 0)])
+    before = jnp.where(span == 0, entering_id(ids, REACH - 1), seg_s[jnp.maximum(start - 1, 0)])
+    oldest = jnp.where(span == 0, entering_id(ids, 0), seg_s[jnp.maximum(start - REACH, 0)])
     cut = (first != last) | ((oldest != first) & (oldest >= 0))
     info_ref[2 * span] = cut.astype(jnp.int32)
     info_ref[2 * span + 1] = (before == last).astype(jnp.int32)
@@ -107,67 +129,56 @@
     @pl.when(span == 0)
     def _():
         seg_buf[8 - REACH : 8, :] = ids - 1.0
-        for piece in range(2 * pieces):
-            bc_buf[piece, 8 - REACH : 8, :] = halo_ref[:, piece * LANES : (piece + 1) * LANES].astype(F32)
 
     @pl.when(span > 0)
     def _():
         seg_buf[0:8, :] = seg_buf[SPAN : SPAN + 8, :]
-        for piece in range(2 * pieces):
-            bc_buf[piece, 0:8, :] = bc_buf[piece, SPAN : SPAN + 8, :]
-
-    seg_rows, seg_cols = [], []
-    for half in range(2):
-        seg_row = seg_ref[:, half * L : (half + 1) * L].astype(F32)
-        seg_col = jnp.transpose(jnp.broadcast_to(seg_row, (L, L)))
-        seg_rows.append(seg_row)
-        seg_cols.append(seg_col)
-        seg_buf[8 + half * L : 8 + (half + 1) * L, :] = seg_col[:, :LANES]
-    for half in range(2):
-        code = jnp.zeros((L, LANES), F32)
-        for step in range(1, KCONV):
-            same = seg_buf[pl.ds(8 - step + half * L, L), :] == seg_cols[half][:, :LANES]
-            code = code + jnp.where(same, 1.0, 0.0)
-        code_ref[half * L : (half + 1) * L, :] = code
-
-    weights_b = 0.5 * wb_ref[...].astype(F32)
-    weights_c = 0.5 * wc_ref[...].astype(F32)
-    for piece in range(pieces):
-        lanes = slice(piece * LANES, (piece + 1) * LANES)
-        bc_buf[piece, 8 : 8 + SPAN, :] = b_ref[:, lanes].astype(F32)
-        bc_buf[pieces + piece, 8 : 8 + SPAN, :] = c_ref[:, lanes].astype(F32)
-        for index, weights in ((piece, weights_b), (pieces + piece, weights_c)):
-            for row in range(0, SPAN, TILE):
-                acc = conv_tile(bc_buf, index, weights[:, lanes], row, TILE, code_ref[row : row + TILE, :])
-                held[index, row : row + TILE, :] = silu_of_half(acc)
-
+
+    seg_row = seg_ref[...].astype(F32)
+    seg_buf[8 : 8 + SPAN, :] = jnp.transpose(jnp.broadcast_to(seg_row, (LANES, SPAN)))
+    own = seg_buf[8 : 8 + SPAN, :]
+    code = jnp.zeros((SPAN, LANES), F32)
+    for step in range(1, KCONV):
+        code = code + jnp.where(seg_buf[8 - step : 8 - step + SPAN, :] == own, 1.0, 0.0)
+    code_ref[...] = code
+    fill_conv(buf, held, b_ref, halo_ref, wb_ref, code_ref, span)
+    bs_ref[...] = held[...].astype(BF16)
+    latest = seg_row == last.astype(F32)
+    for g in range(parts):
+        bt_ref[g] = jnp.where(latest, jnp.transpose(held[:, g * N : (g + 1) * N]), 0.0).astype(BF16)
+
+
+def score_kernel(
+    seg_s, c_ref, halo_ref, ids_ref, wc_ref, seg_ref, bs_ref, code_ref, token_ref,
+    m_ref,
+    buf, held, *, parts
+):
+    del token_ref
+    span = pl.program_id(0)
+    ids = ids_ref[...].astype(F32)
+    start = span * SPAN
+    before = jnp.where(span == 0, entering_id(ids, REACH - 1), seg_s[jnp.maximum(start - 1, 0)])
+    fill_conv(buf, held, c_ref, halo_ref, wc_ref, code_ref, span)
+    halves = [slice(half * L, (half + 1) * L) for half in range(2)]
+    seg_rows = [seg_ref[:, half].astype(F32) for half in halves]
+    seg_cols = [jnp.transpose(jnp.broadcast_to(seg_row, (L, L))) for seg_row in seg_rows]
     rows = lax.broadcasted_iota(jnp.int32, (L, L), 0)
     cols = lax.broadcasted_iota(jnp.int32, (L, L), 1)
     causal = rows >= cols
     across = (((1,), (1,)), ((), ()))
     for g in range(parts):
-        per = N // LANES
-
-        def take(first_piece, half):
-            parts_ = [held[first_piece + k, half * L : (half + 1) * L, :] for k in range(per)]
-            return jnp.concatenate(parts_, axis=1)
-
-        bs = [take(g * per, half) for half in range(2)]
-        cs = [take(pieces + g * per, half) for half in range(2)]
-        bs16 = [value.astype(BF16) for value in bs]
-        cs16 = [value.astype(BF16) for value in cs]
+        lanes = slice(g * N, (g + 1) * N)
+        cs = held[:, lanes].astype(BF16)
+        early = lax.dot_general(cs, bs_ref[halves[0], lanes], across, preferred_element_type=F32)
+        late = lax.dot_general(cs[L:], bs_ref[halves[1], lanes], across, preferred_element_type=F32)
+        allowed = [causal & (seg_cols[half] == seg_rows[half]) for half in range(2)]
+        m_ref[g, 0:L, 0:L] = jnp.where(allowed[0], early[:L], 0.0).astype(BF16)
+        m_ref[g, L:SPAN, 0:L] = jnp.where(seg_cols[1] == seg_rows[0], early[L:], 0.0).astype(BF16)
+        m_ref[g, 0:L, L + N :] = jnp.zeros((L, L), BF16)
+        m_ref[g, L:SPAN, L + N :] = jnp.where(allowed[1], late, 0.0).astype(BF16)
         for half in range(2):
-            own = slice(half * L, (half + 1) * L)
-            scores = lax.dot_general(cs16[half], bs16[half], across, preferred_element_type=F32)
-            allowed = causal & (seg_cols[half] == seg_rows[half])
-            m_ref[g, own, 0:L] = jnp.where(allowed, scores, 0.0).astype(BF16)
             enters = seg_cols[half] == before.astype(F32)
-            m_ref[g, own, L : L + N] = jnp.where(enters, cs[half], 0.0).astype(BF16)
-            latest = seg_cols[half] == last.astype(F32)
-            bt_ref[g, :, own] = jnp.transpose(jnp.where(latest, bs[half], 0.0)).astype(BF16)
-        scores = lax.dot_general(cs16[1], bs16[0], across, preferred_element_type=F32)
-        m_ref[g, L:SPAN, L + N :] = jnp.where(seg_cols[1] == seg_rows[0], scores, 0.0).astype(BF16)
-        m_ref[g, 0:L, L + N :] = jnp.zeros((L, L), BF16)
+            m_ref[g, halves[half], L : L + N] = jnp.where(enters, held[halves[half], lanes], 0.0).astype(BF16)
 
 
 def state_kernel(
@@ -229,56 +240,55 @@
 
 
 def final_kernel(
-    info_ref, u_ref, u_first_ref, gate_ref, m_ref, e_ref, w_ref, em_ref, first_ref, t0_ref, t1_ref, t2_ref, gain_ref,
-    out_ref,
+    info_ref, u_ref, gate_ref, m_ref, e_ref, w_ref, em_ref, first_ref, t0_ref, t1_ref, t2_ref, gain_ref,
+    out_ref, done_ref,
     enter, spread, held, *, first_head, heads
 ):
-    block = pl.program_id(0)
+    span = pl.program_id(0)
     width = u_ref.shape[1]
     chunks = width // CHUNK
-    spans = [slice(chunk * CHUNK, (chunk + 1) * CHUNK) for chunk in range(chunks)]
-
-    @pl.when(block == 0)
-    def _():
+    strips = [slice(chunk * CHUNK, (chunk + 1) * CHUNK) for chunk in range(chunks)]
+
+    @pl.when(span == 0)
+    def _():
+        done_ref[...] = jnp.zeros_like(done_ref)
         spread_matrix(spread, first_head, heads)
         passes = info_ref[1].astype(F32)
-        for cols in spans:
+        for cols in strips:
             early, late = (dot(em_ref[k], spread[:, cols])[0:1] for k in range(2))
             came = t0_ref[:, cols].astype(F32) + t1_ref[:, cols].astype(F32) + t2_ref[:, cols].astype(F32)
             enter[0, :, cols] = (early * came).astype(BF16)
             grown = first_ref[:, cols].astype(F32) + (passes * early * early) * came
             enter[1, :, cols] = (late * grown).astype(BF16)
 
-    def rows(odd):
-        squares = jnp.zeros((L, LANES), F32)
-        for cols in spans:
-            part = spread[:, cols]
-            u = u_ref[:, cols]
-            total = dot(m_ref[0, :, 0:L], u) + dot(m_ref[0, :, L : L + N], enter[block // 2, :, cols])
-            if odd:
-                total = total + dot(m_ref[0, :, L + N :], u_first_ref[:, cols])
-            y = dot(e_ref[...], part) * (total + dot(w_ref[...], part) * u.astype(F32))
-            v = y * silu_of_half(0.5 * gate_ref[:, cols].astype(F32))
-            held[:, cols] = v
+    squares = [jnp.zeros((L, LANES), F32) for _ in range(2)]
+    for cols in strips:
+        part = spread[:, cols]
+        sources = jnp.concatenate([u_ref[0:L, cols], enter[span, :, cols]], axis=0)
+        total = dot(m_ref[0, :, 0 : L + N], sources)
+        last = dot(m_ref[0, L:SPAN, L + N :], u_ref[L:SPAN, cols])
+        outer = dot(e_ref[...], part)
+        direct = dot(w_ref[...], part)
+        for half in range(2):
+            own = slice(half * L, (half + 1) * L)
+            sums = total[own] + direct[own] * u_ref[own, cols].astype(F32)
+            if half == 1:
+                sums = sums + last
+            v = (outer[own] * sums) * silu_of_half(0.5 * gate_ref[own, cols].astype(F32))
+            held[own, cols] = v
             v2 = v * v
             for piece in range(CHUNK // LANES):
-                squares = squares + v2[:, piece * LANES : (piece + 1) * LANES]
-        mean = jnp.sum(squares, axis=1, keepdims=True) * (1.0 / width)
+                squares[half] = squares[half] + v2[:, piece * LANES : (piece + 1) * LANES]
+    for half in range(2):
+        own = slice(half * L, (half + 1) * L)
+        mean = jnp.sum(squares[half], axis=1, keepdims=True) * (1.0 / width)
         scale = lax.rsqrt(mean + 1e-05)
-        for cols in spans:
-            out_ref[:, cols] = (held[:, cols] * scale * gain_ref[:, cols]).astype(BF16)
-
-    @pl.when(block % 2 == 0)
-    def _():
-        rows(False)
-
-    @pl.when(block % 2 == 1)
-    def _():
-        rows(True)
+        for cols in strips:
+            out_ref[own, cols] = (held[own, cols] * scale * gain_ref[:, cols]).astype(BF16)
 
 
 def state_after_kernel(*refs, first_head, heads):
-    state_kernel(*refs[:8], *refs[9:], first_head=first_head, heads=heads)
+    state_kernel(*refs[:8], *refs[10:], first_head=first_head, heads=heads)
 
 
 def scale_kernel(value_ref, factor_ref, *refs):
@@ -289,7 +299,7 @@
 
 
 def final_into_kernel(*refs, first_head, heads):
-    final_kernel(*refs[:13], *refs[14:], first_head=first_head, heads=heads)
+    final_kernel(*refs[:12], *refs[13:], first_head=first_head, heads=heads)
 
 
 def per_device(
@@ -354,50 +364,53 @@
         name="decays",
     )(dt_raw, row(dt_bias), row(a_log), row(skip))
 
-    m, bt, code, info = pl.pallas_call(
-        functools.partial(score_kernel, parts=parts),
+    halo_bc = lambda which: pl.BlockSpec((REACH, width_bc), lambda *_: (0, channels // width_bc + which))
+    ids_spec = pl.BlockSpec((REACH, LANES), lambda *_: (0, tail_width // LANES - 1))
+    seg_spec = pl.BlockSpec((1, SPAN), lambda k: (0, k))
+    wide_bc = pl.BlockSpec((SPAN, width_bc), at_row)
+    conv_scratch = [pltpu.VMEM((width_bc // LANES, SPAN + 8, LANES), F32)]
+    bs, bt, code, info = pl.pallas_call(
+        functools.partial(b_kernel, parts=parts),
         grid=(spans,),
-        in_specs=[
-            smem,
-            pl.BlockSpec((SPAN, width_bc), at_row),
-            pl.BlockSpec((SPAN, width_bc), at_row),
-            pl.BlockSpec((REACH, 2 * width_bc), lambda *_: (0, channels // (2 * width_bc))),
-            pl.BlockSpec((REACH, LANES), lambda *_: (0, tail_width // LANES - 1)),
-            pl.BlockSpec((KCONV, width_bc), whole),
-            pl.BlockSpec((KCONV, width_bc), whole),
-            pl.BlockSpec((1, SPAN), lambda k: (0, k)),
-        ],
-        out_specs=[
-            pl.BlockSpec((parts, SPAN, N + SPAN), lambda k: (0, k, 0)),
-            pl.BlockSpec((parts, N, SPAN), lambda k: (0, 0, k)),
-            narrow,
-            smem,
-        ],
+        in_specs=[smem, wide_bc, halo_bc(0), ids_spec, pl.BlockSpec((KCONV, width_bc), whole), seg_spec],
+        out_specs=[wide_bc, pl.BlockSpec((parts, N, SPAN), lambda k: (0, 0, k)), narrow, smem],
         out_shape=[
-            shape((parts, rows, N + SPAN), BF16),
+            shape((rows, width_bc), BF16),
             shape((parts, N, rows), BF16),
             shape((rows, LANES), F32),
             shape((2 * spans,), jnp.int32),
         ],
-        scratch_shapes=[
-            pltpu.VMEM((2 * width_bc // LANES, SPAN + 8, LANES), F32),
-            pltpu.VMEM((SPAN + 8, LANES), F32),
-            pltpu.VMEM((2 * width_bc // LANES, SPAN, LANES), F32),
-        ],
+        scratch_shapes=conv_scratch + [pltpu.VMEM((SPAN + 8, LANES), F32), pltpu.VMEM((SPAN, width_bc), F32)],
         compiler_params=params(1),
-        cost_estimate=cost(2 * 10**9, 6),
-        name="scores",
-    )(segment, b_in, c_in, halo, halo, conv_b, conv_c, row(segment))
+        cost_estimate=cost(10**9, 3),
+        name="b_rows",
+    )(segment, b_in, halo, halo, conv_b, row(segment))
+
+    def score(token):
+        return pl.pallas_call(
+            functools.partial(score_kernel, parts=parts),
+            grid=(spans,),
+            in_specs=[
+                smem, wide_bc, halo_bc(1), ids_spec, pl.BlockSpec((KCONV, width_bc), whole), seg_spec, wide_bc, narrow,
+                pl.BlockSpec(memory_space=pl.ANY),
+            ],
+            out_specs=pl.BlockSpec((parts, SPAN, N + SPAN), lambda k: (0, k, 0)),
+            out_shape=shape((parts, rows, N + SPAN), BF16),
+            scratch_shapes=conv_scratch + [pltpu.VMEM((SPAN, width_bc), F32)],
+            compiler_params=params(1),
+            cost_estimate=cost(3 * 10**9, 4),
+            name="scores",
+        )(segment, c_in, halo, halo, conv_c, row(segment), bs, code, token)
 
     em_spec = lambda: pl.BlockSpec((spans, 16, LANES), lambda *_: (0, 0, 0))
 
     anywhere = pl.BlockSpec(memory_space=pl.ANY)
 
-    def local(g, token):
+    def local(g, tokens):
         steps = width // step_width
         at_cols = lambda j, k: (0, g * steps + j)
         return pl.pallas_call(
-            functools.partial(state_kernel if token is None else state_after_kernel, first_head=g * heads, heads=all_heads),
+            functools.partial(state_after_kernel if tokens else state_kernel, first_head=g * heads, heads=all_heads),
             grid=(steps, spans),
             in_specs=[
                 smem,
@@ -409,7 +422,7 @@
                 em_spec(),
                 pl.BlockSpec((SPAN, LANES), lambda j, k: (k, 0)),
             ]
-            + ([] if token is None else [anywhere]),
+            + [anywhere] * len(tokens),
             out_specs=[
                 pl.BlockSpec((SPAN, step_width), lambda j, k: (k, j)),
                 pl.BlockSpec((N, step_width), lambda j, k: (0, j)),
@@ -430,7 +443,7 @@
             compiler_params=params(2),
             cost_estimate=cost(6 * 10**9, 10),
             name="state",
-        )(info, x_in, halo, conv_x, bt, a_hl, em, code, *([] if token is None else [token]))
+        )(info, x_in, halo, conv_x, bt, a_hl, em, code, *tokens)
 
     def scaled(value, factor, token):
         tokens = [] if token is None else [token]
@@ -459,18 +472,17 @@
                 leaving = leave(state, first.astype(F32) + passed.astype(F32), factor)
         return first, entering, passed
 
-    def final(g, u, first, carries, out):
+    def final(g, u, m, first, carries, out):
         at_group = lambda *_: (0, g)
-        own = pl.BlockSpec((L, width), lambda k: (k, g))
+        own = pl.BlockSpec((SPAN, width), lambda k: (k, g))
         square = pl.BlockSpec((N, width), whole)
         in_specs = [
             smem,
-            pl.BlockSpec((L, width), at_row),
-            pl.BlockSpec((L, width), lambda k: (k // 2 * 2, 0)),
+            pl.BlockSpec((SPAN, width), at_row),
             own,
-            pl.BlockSpec((1, L, N + SPAN), lambda k: (g, k, 0)),
-            pl.BlockSpec((L, LANES), at_row),
-            pl.BlockSpec((L, LANES), at_row),
+            pl.BlockSpec((1, SPAN, N + SPAN), lambda k: (g, k, 0)),
+            narrow,
+            narrow,
             em_spec(),
             square,
             square,
@@ -478,37 +490,39 @@
             square,
             pl.BlockSpec((1, width), at_group),
         ]
-        operands = [info, u, u, gate_in, m, e_hl, w_hl, em, first, *carries, row(norm_gain)]
+        operands = [info, u, gate_in, m, e_hl, w_hl, em, first, *carries, row(norm_gain)]
         if out is not None:
-            in_specs.append(pl.BlockSpec(memory_space=pl.ANY))
+            in_specs.append(anywhere)
             operands.append(out)
         return pl.pallas_call(
             functools.partial(final_kernel if out is None else final_into_kernel, first_head=g * heads, heads=all_heads),
-            grid=(blocks,),
+            grid=(spans,),
             in_specs=in_specs,
-            out_specs=own,
-            out_shape=shape((rows, channels), BF16),
+            out_specs=[own, pl.BlockSpec((8, LANES), whole)],
+            out_shape=[shape((rows, channels), BF16), shape((8, LANES), F32)],
             scratch_shapes=[
                 pltpu.VMEM((spans, N, width), BF16),
                 pltpu.VMEM((LANES, width), BF16),
-                pltpu.VMEM((L, width), F32),
+                pltpu.VMEM((SPAN, width), F32),
             ],
-            input_output_aliases={} if out is None else {13: 0},
+            input_output_aliases={} if out is None else {12: 0},
             compiler_params=params(1),
             cost_estimate=cost(6 * 10**9, 16),
             name="final",
         )(*operands)
 
-    leaving, locals_ = None, []
+    leaving, locals_, m = None, [], None
     for g in range(parts):
-        u, state, inner, factor = local(g, leaving)
+        u, state, inner, factor = local(g, [leaving, m] if g else [])
         first = lax.ppermute(state, "req", inside)
+        if m is None:
+            m = score(factor)
         leaving = leave(state, first, factor)
         locals_.append((u, inner, state, first, leaving, factor))
-    out = None
+    out = done = None
     for g in range(parts):
         u, inner, *sent = locals_[g]
-        out = final(g, u, inner, travel(*sent, out), out)
+        out, done = final(g, u, m, inner, travel(*sent, done), out)
     return out
 
 

time: 81.4 us -> 76.4 us (0.939)
  local copies, waits for them, and re-layouts: 4.31 us -> 0.93 us
  Pallas kernels: 51.6 us -> 50.1 us
    unnamed x35 -> x29, local copies, waits for them, and re-layouts: 4.31 us -> 0.93 us
    ppermute x2, waiting for transfers between devices: 6.02 us -> 4.52 us  [per_device(): first = lax.ppermute(state, 'req', inside)]
    ppermute x2, waiting for transfers between devices: 8.85 us -> 10.2 us  [travel(): passed = lax.ppermute(scaled(entering, factor, token), 'req', inside)]
    pallas_call x2, Pallas kernels: 21.1 us -> 19.9 us  [final(): pl.pallas_call(functools.partial(final_kernel if out is None else final_i...]
    pallas_call x3 -> x4, Pallas kernels: 26.9 us -> 26.7 us  [the longest x2 19 us: local(): pl.pallas_call(functools.partial(state_after_kernel if tokens else state_...]
  transfers between devices with their start and end apart: 7 -> 7, of which waited for: 4 -> 4; matrix products, arithmetic and copies ran while one was open for 1% -> 1% of each run, Pallas kernels for 29% -> 34%
where the time goes in v2:
time: 76.4 us; the launch traced here: 75.4 us
  Pallas kernels  50.1 us (66%)
  waiting for transfers between devices  14.7 us (19%)
  starting transfers between devices  8.49 us (11%)
  local copies, waits for them, and re-layouts  0.93 us (1%)
  other arithmetic  0.8 us (1%)
    pallas_call x2, Pallas kernels, final(): pl.pallas_call(functools.partial(final_kernel if out is None else final_i...  19.9 us
    pallas_call x2, Pallas kernels, local(): pl.pallas_call(functools.partial(state_after_kernel if tokens else state_...  19 us
    ppermute x2, waiting for transfers between devices, travel(): passed = lax.ppermute(scaled(entering, factor, token), 'req', inside)  10.2 us
    ppermute x2, waiting for transfers between devices, per_device(): first = lax.ppermute(state, 'req', inside)  4.52 us
    pallas_call x1, Pallas kernels, per_device(): pl.pallas_call(functools.partial(b_kernel, parts=parts), grid=(spans,), i...  4.1 us
    pallas_call x1, Pallas kernels, score(): pl.pallas_call(functools.partial(score_kernel, parts=parts), grid=(spans,...  3.61 us
    ppermute x2, starting transfers between devices, travel(): passed = lax.ppermute(scaled(entering, factor, token), 'req', inside)  2.85 us
    ppermute x2, starting transfers between devices, per_device(): first = lax.ppermute(state, 'req', inside)  2.58 us
  transfers between devices with their start and end apart: 7, of which 4 were waited for; matrix products, arithmetic and copies ran while one was open for 1% of the time, Pallas kernels for 34%

profile of v2, /device:TPU:11, one launch (start us, length us, event | category | flops | bytes accessed | tf_op | source)
XLA Modules:
  0.0 75.4 jit_solution(7308278516562197001)
XLA Ops:
  0.0 0.0 copy-start.1
  0.0 0.7 copy-done.1
  0.7 0.0 copy-start.11
  0.7 0.0 copy-start.6
  0.7 0.0 copy-start.7
  0.7 0.0 copy-start.8
  0.7 1.0 %tails.1 = bf16[3,5248]{1,0:T(4,128)(2,1)S(1)} custom-call(s32[1024]{0:T(1024)S(1)} %copy-done.1, bf16[1024,4096]{1,0:T(8,128)(2,1)} %refs_1_.1, bf16[1024,512]{1,0:T(8,128)(2,1)} %b_ref.3, bf16[1024,512]{1,0:T(8,128)(2,1)} %c_ref.3), custom_call_target="tpu_custom_call" | custom-call | flops 1000 | tf_op jit(solution)/shard_map/tails/pallas_call | solution.py:337
  1.7 1.3 %collective-permute-start = (bf16[3,5248]{1,0:T(4,128)(2,1)S(1)}, bf16[3,5248]{1,0:T(4,128)(2,1)S(1)}, u32[]{:S(2)}, u32[]{:S(2)}) collective-permute-start(bf16[3,5248]{1,0:T(4,128)(2,1)S(1)} %tails.1), channel_id=1, source_target_pairs={{0,4},{4,8},{8,12},{1,5},{5,9},{9,13},{2,6},{6,10},{10,14},{3,7},{... | collective-permute-start | bytes 94472 | tf_op jit(solution)/shard_map/ppermute | solution.py:352
  3.0 0.0 copy-done.11
  3.0 0.2 copy.15.dt_ref
  3.2 0.0 copy-done.6
  3.2 0.0 copy-done.7
  3.2 0.0 copy-done.8
  3.2 0.0 copy-start.2
  3.2 0.0 copy-start.4
  3.2 2.2 %decays.1 = (bf16[1024,128]{1,0:T(8,128)(2,1)S(1)}, bf16[1024,128]{1,0:T(8,128)(2,1)S(1)}, bf16[1024,128]{1,0:T(8,128)(2,1)S(1)}, bf16[2,16,128]{2,1,0:T(8,128)(2,1)S(1)}) custom-call(bf16[1024,64]{1,0:T(8,128)(2,1)S(1)} %copy.15.dt_ref, f32[1,64]{1,0:T(1,128)S(1)} %bitcast.15, f32[1,64]{1,0:T(1,128)S(1)} %bitcast.16, f32[1,64]{1,0:T(1,128)S(1)} %bitcast.17), custom_call_target="tpu_custom_call" | custom-call | flops 3000000000 | bytes 1048576 | tf_op jit(solution)/shard_map/decays/pallas_call | solution.py:356
  5.5 0.0 copy-start.3
  5.5 0.0 collective-permute-done.halo_ref.ids_ref.refs_2_
  5.5 0.0 copy-done.2
  5.5 0.0 copy-done.4
  5.5 4.1 %b_rows.1 = (bf16[1024,512]{1,0:T(8,128)(2,1)S(1)}, bf16[2,256,1024]{2,1,0:T(8,128)(2,1)S(1)}, f32[1024,128]{1,0:T(8,128)S(1)}, s32[4]{0:T(128)S(1)}) custom-call(s32[1024]{0:T(1024)S(1)} %copy-done.2, bf16[1024,512]{1,0:T(8,128)(2,1)} %b_ref.3, bf16[3,5248]{1,0:T(4,128)(2,1)S(1)} %collective-permute-done.halo_ref.ids_ref.refs_2_, ...), custom_call_target="tpu_custom_call" | custom-call | flops 1000000000 | bytes 3145728 | tf_op jit(solution)/shard_map/b_rows/pallas_call | solution.py:372
  9.6 0.0 copy-done.3
  9.6 0.0 copy-start.5
  9.6 9.2 %state.2 = (bf16[1024,2048]{1,0:T(8,128)(2,1)S(1)}, bf16[256,2048]{1,0:T(8,128)(2,1)S(1)}, bf16[256,2048]{1,0:T(8,128)(2,1)S(1)}, f32[1,2048]{1,0:T(1,128)S(1)}) custom-call(s32[4]{0:T(128)S(1)} %get-tuple-element.24.info_ref.refs_0_, bf16[1024,4096]{1,0:T(8,128)(2,1)} %refs_1_.1, bf16[3,5248]{1,0:T(4,128)(2,1)S(1)} %collective-permute-done.halo_ref.ids_ref.refs_2_, ...), custom_call_target="tpu_custom_call" | custom-call | flops 6000000000 | bytes 10485760 | tf_op jit(solution)/shard_map/state/pallas_call | solution.py:412
  18.8 0.0 copy-start.9
  18.8 1.3 %collective-permute-start.1 = (bf16[256,2048]{1,0:T(8,128)(2,1)S(1)}, bf16[256,2048]{1,0:T(8,128)(2,1)S(1)}, u32[]{:S(2)}, u32[]{:S(2)}) collective-permute-start(bf16[256,2048]{1,0:T(8,128)(2,1)S(1)} %get-tuple-element.29), channel_id=1, source_target_pairs={{0,4},{8,12},{1,5},{9,13},{2,6},{10,14},{3,7},{11,15},{16,20},{24,... | collective-permute-start | bytes 3145736 | tf_op jit(solution)/shard_map/ppermute | solution.py:517
  20.1 0.0 copy-done.5
  20.1 3.6 %scores.1.refs_9_.m_ref.refs_3_ = bf16[2,1024,768]{2,1,0:T(8,128)(2,1)S(1)} custom-call(s32[1024]{0:T(1024)S(1)} %copy-done.2, bf16[1024,512]{1,0:T(8,128)(2,1)} %c_ref.3, bf16[3,5248]{1,0:T(4,128)(2,1)S(1)} %collective-permute-done.halo_ref.ids_ref.refs_2_, bf16[3,5248]{1,0:T(4,128)(2,1)S(1)} %collective-permute-done.halo_ref.ids_ref.refs_2_, ...), custom_call_target="tpu_custom_call" | custom-call | flops 3000000000 | bytes 4194304 | tf_op jit(solution)/shard_map/scores/pallas_call | solution.py:390
  23.7 0.0 copy-done.9
  23.8 1.4 %collective-permute-done.1.t0_ref = bf16[256,2048]{1,0:T(8,128)(2,1)S(1)} collective-permute-done((bf16[256,2048]{1,0:T(8,128)(2,1)S(1)}, bf16[256,2048]{1,0:T(8,128)(2,1)S(1)}, u32[]{:S(2)}, u32[]{:S(2)}) %collective-permute-start.1) | collective-permute-done | bytes 1048608 | tf_op jit(solution)/shard_map/ppermute | solution.py:517
  25.2 0.0 slice-start
  25.2 0.4 add_convert_fusion.1.refs_8_
  25.6 0.0 slice-start.1
  25.6 0.9 %collective-permute-start.4 = (bf16[256,2048]{1,0:T(8,128)(2,1)S(1)}, bf16[256,2048]{1,0:T(8,128)(2,1)S(1)}, u32[]{:S(2)}, u32[]{:S(2)}) collective-permute-start(bf16[256,2048]{1,0:T(8,128)(2,1)S(1)} %add_convert_fusion.1.refs_8_), channel_id=1, source_target_pairs={{4,8},{5,9},{6,10},{7,11},{20,24},{21,25},{22,26},{23,27}} | collective-permute-start | bytes 3145736 | tf_op jit(solution)/shard_map/ppermute | solution.py:469
  26.4 9.8 %state.3 = (bf16[1024,2048]{1,0:T(8,128)(2,1)S(1)}, bf16[256,2048]{1,0:T(8,128)(2,1)S(1)}, bf16[256,2048]{1,0:T(8,128)(2,1)S(1)}, f32[1,2048]{1,0:T(1,128)S(1)}) custom-call(s32[4]{0:T(128)S(1)} %get-tuple-element.24.info_ref.refs_0_, bf16[1024,4096]{1,0:T(8,128)(2,1)} %refs_1_.1, bf16[3,5248]{1,0:T(4,128)(2,1)S(1)} %collective-permute-done.halo_ref.ids_ref.refs_2_, ...), custom_call_target="tpu_custom_call" | custom-call | flops 6000000000 | bytes 10485760 | tf_op jit(solution)/shard_map/state/pallas_call | solution.py:412
  36.3 1.3 %collective-permute-start.2 = (bf16[256,2048]{1,0:T(8,128)(2,1)S(1)}, bf16[256,2048]{1,0:T(8,128)(2,1)S(1)}, u32[]{:S(2)}, u32[]{:S(2)}) collective-permute-start(bf16[256,2048]{1,0:T(8,128)(2,1)S(1)} %get-tuple-element.36), channel_id=1, source_target_pairs={{0,4},{8,12},{1,5},{9,13},{2,6},{10,14},{3,7},{11,15},{16,20},{24,... | collective-permute-start | bytes 3145736 | tf_op jit(solution)/shard_map/ppermute | solution.py:517
  37.6 0.0 collective-permute-done.4.value_ref.t1_ref
  37.6 0.0 copy-start.10
  37.6 0.2 scale.2
  37.8 0.0 copy-start
  37.8 1.6 %collective-permute-start.5 = (bf16[256,2048]{1,0:T(8,128)(2,1)S(1)}, bf16[256,2048]{1,0:T(8,128)(2,1)S(1)}, u32[]{:S(2)}, u32[]{:S(2)}) collective-permute-start(bf16[256,2048]{1,0:T(8,128)(2,1)S(1)} %scale.2), channel_id=1, source_target_pairs={{0,4},{8,12},{1,5},{9,13},{2,6},{10,14},{3,7},{11,15},{16,20},{24,... | collective-permute-start | bytes 3145736 | tf_op jit(solution)/shard_map/ppermute | solution.py:470
  39.4 3.1 %collective-permute-done.2.refs_8_ = bf16[256,2048]{1,0:T(8,128)(2,1)S(1)} collective-permute-done((bf16[256,2048]{1,0:T(8,128)(2,1)S(1)}, bf16[256,2048]{1,0:T(8,128)(2,1)S(1)}, u32[]{:S(2)}, u32[]{:S(2)}) %collective-permute-start.2) | collective-permute-done | bytes 1048608 | tf_op jit(solution)/shard_map/ppermute | solution.py:517
  42.5 0.4 add_convert_fusion
  42.9 0.9 %collective-permute-start.3 = (bf16[256,2048]{1,0:T(8,128)(2,1)S(1)}, bf16[256,2048]{1,0:T(8,128)(2,1)S(1)}, u32[]{:S(2)}, u32[]{:S(2)}) collective-permute-start(bf16[256,2048]{1,0:T(8,128)(2,1)S(1)} %add_convert_fusion), channel_id=1, source_target_pairs={{4,8},{5,9},{6,10},{7,11},{20,24},{21,25},{22,26},{23,27}} | collective-permute-start | bytes 3145736 | tf_op jit(solution)/shard_map/ppermute | solution.py:469
  43.8 3.6 %collective-permute-done.5.t2_ref = bf16[256,2048]{1,0:T(8,128)(2,1)S(1)} collective-permute-done((bf16[256,2048]{1,0:T(8,128)(2,1)S(1)}, bf16[256,2048]{1,0:T(8,128)(2,1)S(1)}, u32[]{:S(2)}, u32[]{:S(2)}) %collective-permute-start.5) | collective-permute-done | bytes 1048608 | tf_op jit(solution)/shard_map/ppermute | solution.py:470
  47.4 0.0 slice-done
  47.4 0.0 slice-done.1
  47.4 0.0 copy-done.10
  47.4 0.0 copy-done
  47.4 10.0 %final.2 = (bf16[1024,4096]{1,0:T(8,128)(2,1)}, f32[8,128]{1,0:T(8,128)S(1)}) custom-call(s32[4]{0:T(128)S(1)} %get-tuple-element.24.info_ref.refs_0_, bf16[1024,2048]{1,0:T(8,128)(2,1)S(1)} %copy-done.10, bf16[1024,4096]{1,0:T(8,128)(2,1)S(1)} %bitcast.8, bf16[2,1024,768]{2,1,0:T(8,128)(2,1)S(1)} %scores.1.refs_9_.m_ref.refs_3_, ...), custom_call_target="tpu_custom_call" | custom-call | flops 6000000000 | bytes 16777216 | tf_op jit(solution)/shard_map/final/pallas_call | solution.py:497
  57.4 0.0 collective-permute-done.3.value_ref.refs_9_
  57.4 0.2 scale.3
  57.6 1.3 %collective-permute-start.6 = (bf16[256,2048]{1,0:T(8,128)(2,1)S(1)}, bf16[256,2048]{1,0:T(8,128)(2,1)S(1)}, u32[]{:S(2)}, u32[]{:S(2)}) collective-permute-start(bf16[256,2048]{1,0:T(8,128)(2,1)S(1)} %scale.3), channel_id=1, source_target_pairs={{0,4},{8,12},{1,5},{9,13},{2,6},{10,14},{3,7},{11,15},{16,20},{24,... | collective-permute-start | bytes 3145736 | tf_op jit(solution)/shard_map/ppermute | solution.py:470
  58.9 6.6 %collective-permute-done.6.refs_10_ = bf16[256,2048]{1,0:T(8,128)(2,1)S(1)} collective-permute-done((bf16[256,2048]{1,0:T(8,128)(2,1)S(1)}, bf16[256,2048]{1,0:T(8,128)(2,1)S(1)}, u32[]{:S(2)}, u32[]{:S(2)}) %collective-permute-start.6) | collective-permute-done | bytes 1048608 | tf_op jit(solution)/shard_map/ppermute | solution.py:470
  65.5 9.9 %final.3 = (bf16[1024,4096]{1,0:T(8,128)(2,1)}, f32[8,128]{1,0:T(8,128)}) custom-call(s32[4]{0:T(128)S(1)} %get-tuple-element.24.info_ref.refs_0_, bf16[1024,2048]{1,0:T(8,128)(2,1)S(1)} %get-tuple-element.32.refs_1_, bf16[1024,4096]{1,0:T(8,128)(2,1)S(1)} %bitcast.8, ...), custom_call_target="tpu_custom_call", output_to_operand_aliasing={{0}: (12, {})} | custom-call | flops 6000000000 | bytes 16777216 | tf_op jit(solution)/shard_map/final/pallas_call | solution.py:497
  (1 shorter events, 0.0 us)
Async XLA Ops:
  0.0 0.7 copy-start.1
  0.7 2.3 %copy-start.11 = (bf16[1024,64]{0,1:T(8,128)(2,1)S(1)}, bf16[1024,64]{0,1:T(8,128)(2,1)}, u32[]{:S(2)}) copy-start(bf16[1024,64]{0,1:T(8,128)(2,1)} %param.17) | copy-start | bytes 393220
  0.7 2.5 %copy-start.6 = (f32[64]{0:T(128)S(1)}, f32[64]{0:T(128)}, u32[]{:S(2)}) copy-start(f32[64]{0:T(128)} %param.21) | copy-start | bytes 772
  0.7 2.5 %copy-start.7 = (f32[64]{0:T(128)S(1)}, f32[64]{0:T(128)}, u32[]{:S(2)}) copy-start(f32[64]{0:T(128)} %param.22) | copy-start | bytes 772
  0.7 2.5 %copy-start.8 = (f32[64]{0:T(128)S(1)}, f32[64]{0:T(128)}, u32[]{:S(2)}) copy-start(f32[64]{0:T(128)} %param.23) | copy-start | bytes 772
  1.7 3.8 %collective-permute-start = (bf16[3,5248]{1,0:T(4,128)(2,1)S(1)}, bf16[3,5248]{1,0:T(4,128)(2,1)S(1)}, u32[]{:S(2)}, u32[]{:S(2)}) collective-permute-start(bf16[3,5248]{1,0:T(4,128)(2,1)S(1)} %tails.1), channel_id=1, source_target_pairs={{0,4},{4,8},{8,12},{1,5},{5,9},{9,13},{2,6},{6,10},{10,14},{3,7},{... | collective-permute-start | bytes 94472 | tf_op jit(solution)/shard_map/ppermute | solution.py:352
  3.2 2.3 %copy-start.2 = (s32[1024]{0:T(1024)S(1)}, s32[1024]{0:T(1024)}, u32[]{:S(2)}) copy-start(s32[1024]{0:T(1024)} %seg_s.5) | copy-start | bytes 12292
  3.2 2.3 %copy-start.4 = (bf16[4,512]{1,0:T(4,128)(2,1)S(1)}, bf16[4,512]{1,0:T(4,128)(2,1)}, u32[]{:S(2)}) copy-start(bf16[4,512]{1,0:T(4,128)(2,1)} %wb_ref.1) | copy-start | bytes 12292
  5.5 4.1 %copy-start.3 = (bf16[4,4096]{1,0:T(4,128)(2,1)S(1)}, bf16[4,4096]{1,0:T(4,128)(2,1)}, u32[]{:S(2)}) copy-start(bf16[4,4096]{1,0:T(4,128)(2,1)} %refs_3_.1) | copy-start | bytes 98308
  9.6 10.5 %copy-start.5 = (bf16[4,512]{1,0:T(4,128)(2,1)S(1)}, bf16[4,512]{1,0:T(4,128)(2,1)}, u32[]{:S(2)}) copy-start(bf16[4,512]{1,0:T(4,128)(2,1)} %wc_ref.1) | copy-start | bytes 12292
  18.8 4.9 %copy-start.9 = (bf16[1024,2048]{1,0:T(8,128)(2,1)}, bf16[1024,2048]{1,0:T(8,128)(2,1)S(1)}, u32[]{:S(2)}) copy-start(bf16[1024,2048]{1,0:T(8,128)(2,1)S(1)} %get-tuple-element.38.u_ref) | copy-start | bytes 12582916
  18.8 6.3 %collective-permute-start.1 = (bf16[256,2048]{1,0:T(8,128)(2,1)S(1)}, bf16[256,2048]{1,0:T(8,128)(2,1)S(1)}, u32[]{:S(2)}, u32[]{:S(2)}) collective-permute-start(bf16[256,2048]{1,0:T(8,128)(2,1)S(1)} %get-tuple-element.29), channel_id=1, source_target_pairs={{0,4},{8,12},{1,5},{9,13},{2,6},{10,14},{3,7},{11,15},{16,20},{24,... | collective-permute-start | bytes 3145736 | tf_op jit(solution)/shard_map/ppermute | solution.py:517
  25.2 22.2 %slice-start = ((s8[8388608]{0:T(1024)(128)(4,1)}), s8[4194304]{0:T(1024)(128)(4,1)S(1)}, s32[]{:S(2)}) async-start(s8[8388608]{0:T(1024)(128)(4,1)} %bitcast.7), calls=%async_computation | async-start | bytes 8388608
  25.6 21.8 %slice-start.1 = ((s8[8388608]{0:T(1024)(128)(4,1)}), s8[4194304]{0:T(1024)(128)(4,1)S(1)}, s32[]{:S(2)}) async-start(s8[8388608]{0:T(1024)(128)(4,1)} %bitcast.7), calls=%async_computation.1 | async-start | bytes 8388608
  25.6 12.0 %collective-permute-start.4 = (bf16[256,2048]{1,0:T(8,128)(2,1)S(1)}, bf16[256,2048]{1,0:T(8,128)(2,1)S(1)}, u32[]{:S(2)}, u32[]{:S(2)}) collective-permute-start(bf16[256,2048]{1,0:T(8,128)(2,1)S(1)} %add_convert_fusion.1.refs_8_), channel_id=1, source_target_pairs={{4,8},{5,9},{6,10},{7,11},{20,24},{21,25},{22,26},{23,27}} | collective-permute-start | bytes 3145736 | tf_op jit(solution)/shard_map/ppermute | solution.py:469
  36.3 6.2 %collective-permute-start.2 = (bf16[256,2048]{1,0:T(8,128)(2,1)S(1)}, bf16[256,2048]{1,0:T(8,128)(2,1)S(1)}, u32[]{:S(2)}, u32[]{:S(2)}) collective-permute-start(bf16[256,2048]{1,0:T(8,128)(2,1)S(1)} %get-tuple-element.36), channel_id=1, source_target_pairs={{0,4},{8,12},{1,5},{9,13},{2,6},{10,14},{3,7},{11,15},{16,20},{24,... | collective-permute-start | bytes 3145736 | tf_op jit(solution)/shard_map/ppermute | solution.py:517
  37.6 9.8 %copy-start.10 = (bf16[1024,2048]{1,0:T(8,128)(2,1)S(1)}, bf16[1024,2048]{1,0:T(8,128)(2,1)}, u32[]{:S(2)}) copy-start(bf16[1024,2048]{1,0:T(8,128)(2,1)} %copy-done.9) | copy-start | bytes 12582916
  37.8 9.6 %copy-start = (f32[4096]{0:T(1024)S(1)}, f32[4096]{0:T(1024)}, u32[]{:S(2)}) copy-start(f32[4096]{0:T(1024)} %param.24) | copy-start | bytes 49156
  37.8 9.6 %collective-permute-start.5 = (bf16[256,2048]{1,0:T(8,128)(2,1)S(1)}, bf16[256,2048]{1,0:T(8,128)(2,1)S(1)}, u32[]{:S(2)}, u32[]{:S(2)}) collective-permute-start(bf16[256,2048]{1,0:T(8,128)(2,1)S(1)} %scale.2), channel_id=1, source_target_pairs={{0,4},{8,12},{1,5},{9,13},{2,6},{10,14},{3,7},{11,15},{16,20},{24,... | collective-permute-start | bytes 3145736 | tf_op jit(solution)/shard_map/ppermute | solution.py:470
  42.9 14.5 %collective-permute-start.3 = (bf16[256,2048]{1,0:T(8,128)(2,1)S(1)}, bf16[256,2048]{1,0:T(8,128)(2,1)S(1)}, u32[]{:S(2)}, u32[]{:S(2)}) collective-permute-start(bf16[256,2048]{1,0:T(8,128)(2,1)S(1)} %add_convert_fusion), channel_id=1, source_target_pairs={{4,8},{5,9},{6,10},{7,11},{20,24},{21,25},{22,26},{23,27}} | collective-permute-start | bytes 3145736 | tf_op jit(solution)/shard_map/ppermute | solution.py:469
  57.6 7.9 %collective-permute-start.6 = (bf16[256,2048]{1,0:T(8,128)(2,1)S(1)}, bf16[256,2048]{1,0:T(8,128)(2,1)S(1)}, u32[]{:S(2)}, u32[]{:S(2)}) collective-permute-start(bf16[256,2048]{1,0:T(8,128)(2,1)S(1)} %scale.3), channel_id=1, source_target_pairs={{0,4},{8,12},{1,5},{9,13},{2,6},{10,14},{3,7},{11,15},{16,20},{24,... | collective-permute-start | bytes 3145736 | tf_op jit(solution)/shard_map/ppermute | solution.py:470

commit v3 on v2

--- a/solution.py
+++ b/solution.py
@@ -315,7 +315,7 @@
     spans = rows // SPAN
     assert spans == 2
     devices = lax.axis_size("req")
-    step_width = width // 2
+    step_width = width
     shape = jax.ShapeDtypeStruct
     smem = pl.BlockSpec(memory_space=pltpu.SMEM)
     whole = lambda *_: (0, 0)

time: 76.4 us -> 75.2 us (0.984)
  Pallas kernels: 50.1 us -> 48.6 us
    pallas_call x2, Pallas kernels: 19 us -> 17.4 us  [local(): pl.pallas_call(functools.partial(state_after_kernel if tokens else state_...]
where the time goes in v3:
time: 75.2 us; the launch traced here: 74.6 us
  Pallas kernels  48.6 us (65%)
  waiting for transfers between devices  15.3 us (20%)
  starting transfers between devices  8.71 us (12%)
  local copies, waits for them, and re-layouts  0.93 us (1%)
  other arithmetic  0.8 us (1%)
    pallas_call x2, Pallas kernels, final(): pl.pallas_call(functools.partial(final_kernel if out is None else final_i...  19.9 us
    pallas_call x2, Pallas kernels, local(): pl.pallas_call(functools.partial(state_after_kernel if tokens else state_...  17.4 us
    ppermute x2, waiting for transfers between devices, travel(): passed = lax.ppermute(scaled(entering, factor, token), 'req', inside)  10.9 us
    ppermute x2, waiting for transfers between devices, per_device(): first = lax.ppermute(state, 'req', inside)  4.31 us
    pallas_call x1, Pallas kernels, per_device(): pl.pallas_call(functools.partial(b_kernel, parts=parts), grid=(spans,), i...  4.1 us
    pallas_call x1, Pallas kernels, score(): pl.pallas_call(functools.partial(score_kernel, parts=parts), grid=(spans,...  3.61 us
    ppermute x2, starting transfers between devices, travel(): passed = lax.ppermute(scaled(entering, factor, token), 'req', inside)  2.85 us
    ppermute x2, starting transfers between devices, per_device(): first = lax.ppermute(state, 'req', inside)  2.58 us
  transfers between devices with their start and end apart: 7, of which 4 were waited for; matrix products, arithmetic and copies ran while one was open for 1% of the time, Pallas kernels for 34%

profile of v3, /device:TPU:11, one launch (start us, length us, event | category | flops | bytes accessed | tf_op | source)
XLA Modules:
  0.0 74.6 jit_solution(9140373731272362591)
XLA Ops:
  0.0 0.0 copy-start.1
  0.0 0.7 copy-done.1
  0.7 0.0 copy-start.11
  0.7 0.0 copy-start.6
  0.7 0.0 copy-start.7
  0.7 0.0 copy-start.8
  0.7 1.0 %tails.1 = bf16[3,5248]{1,0:T(4,128)(2,1)S(1)} custom-call(s32[1024]{0:T(1024)S(1)} %copy-done.1, bf16[1024,4096]{1,0:T(8,128)(2,1)} %refs_1_.1, bf16[1024,512]{1,0:T(8,128)(2,1)} %b_ref.3, bf16[1024,512]{1,0:T(8,128)(2,1)} %c_ref.3), custom_call_target="tpu_custom_call" | custom-call | flops 1000 | tf_op jit(solution)/shard_map/tails/pallas_call | solution.py:337
  1.7 1.3 %collective-permute-start = (bf16[3,5248]{1,0:T(4,128)(2,1)S(1)}, bf16[3,5248]{1,0:T(4,128)(2,1)S(1)}, u32[]{:S(2)}, u32[]{:S(2)}) collective-permute-start(bf16[3,5248]{1,0:T(4,128)(2,1)S(1)} %tails.1), channel_id=1, source_target_pairs={{0,4},{4,8},{8,12},{1,5},{5,9},{9,13},{2,6},{6,10},{10,14},{3,7},{... | collective-permute-start | bytes 94472 | tf_op jit(solution)/shard_map/ppermute | solution.py:352
  3.0 0.0 copy-done.11
  3.0 0.2 copy.15.dt_ref
  3.2 0.0 copy-done.6
  3.2 0.0 copy-done.7
  3.2 0.0 copy-done.8
  3.2 0.0 copy-start.2
  3.2 0.0 copy-start.4
  3.2 2.2 %decays.1 = (bf16[1024,128]{1,0:T(8,128)(2,1)S(1)}, bf16[1024,128]{1,0:T(8,128)(2,1)S(1)}, bf16[1024,128]{1,0:T(8,128)(2,1)S(1)}, bf16[2,16,128]{2,1,0:T(8,128)(2,1)S(1)}) custom-call(bf16[1024,64]{1,0:T(8,128)(2,1)S(1)} %copy.15.dt_ref, f32[1,64]{1,0:T(1,128)S(1)} %bitcast.15, f32[1,64]{1,0:T(1,128)S(1)} %bitcast.16, f32[1,64]{1,0:T(1,128)S(1)} %bitcast.17), custom_call_target="tpu_custom_call" | custom-call | flops 3000000000 | bytes 1048576 | tf_op jit(solution)/shard_map/decays/pallas_call | solution.py:356
  5.5 0.0 copy-start.3
  5.5 0.0 collective-permute-done.halo_ref.ids_ref.refs_2_
  5.5 0.0 copy-done.2
  5.5 0.0 copy-done.4
  5.5 4.1 %b_rows.1 = (bf16[1024,512]{1,0:T(8,128)(2,1)S(1)}, bf16[2,256,1024]{2,1,0:T(8,128)(2,1)S(1)}, f32[1024,128]{1,0:T(8,128)S(1)}, s32[4]{0:T(128)S(1)}) custom-call(s32[1024]{0:T(1024)S(1)} %copy-done.2, bf16[1024,512]{1,0:T(8,128)(2,1)} %b_ref.3, bf16[3,5248]{1,0:T(4,128)(2,1)S(1)} %collective-permute-done.halo_ref.ids_ref.refs_2_, ...), custom_call_target="tpu_custom_call" | custom-call | flops 1000000000 | bytes 3145728 | tf_op jit(solution)/shard_map/b_rows/pallas_call | solution.py:372
  9.6 0.0 copy-done.3
  9.6 0.0 copy-start.5
  9.6 8.4 %state.2 = (bf16[1024,2048]{1,0:T(8,128)(2,1)S(1)}, bf16[256,2048]{1,0:T(8,128)(2,1)S(1)}, bf16[256,2048]{1,0:T(8,128)(2,1)S(1)}, f32[1,2048]{1,0:T(1,128)S(1)}) custom-call(s32[4]{0:T(128)S(1)} %get-tuple-element.24.info_ref.refs_0_, bf16[1024,4096]{1,0:T(8,128)(2,1)} %refs_1_.1, bf16[3,5248]{1,0:T(4,128)(2,1)S(1)} %collective-permute-done.halo_ref.ids_ref.refs_2_, ...), custom_call_target="tpu_custom_call" | custom-call | flops 6000000000 | bytes 10485760 | tf_op jit(solution)/shard_map/state/pallas_call | solution.py:412
  18.0 0.0 copy-start.9
  18.0 1.3 %collective-permute-start.1 = (bf16[256,2048]{1,0:T(8,128)(2,1)S(1)}, bf16[256,2048]{1,0:T(8,128)(2,1)S(1)}, u32[]{:S(2)}, u32[]{:S(2)}) collective-permute-start(bf16[256,2048]{1,0:T(8,128)(2,1)S(1)} %get-tuple-element.29), channel_id=1, source_target_pairs={{0,4},{8,12},{1,5},{9,13},{2,6},{10,14},{3,7},{11,15},{16,20},{24,... | collective-permute-start | bytes 3145736 | tf_op jit(solution)/shard_map/ppermute | solution.py:517
  19.3 0.0 copy-done.5
  19.3 3.6 %scores.1.refs_9_.m_ref.refs_3_ = bf16[2,1024,768]{2,1,0:T(8,128)(2,1)S(1)} custom-call(s32[1024]{0:T(1024)S(1)} %copy-done.2, bf16[1024,512]{1,0:T(8,128)(2,1)} %c_ref.3, bf16[3,5248]{1,0:T(4,128)(2,1)S(1)} %collective-permute-done.halo_ref.ids_ref.refs_2_, bf16[3,5248]{1,0:T(4,128)(2,1)S(1)} %collective-permute-done.halo_ref.ids_ref.refs_2_, ...), custom_call_target="tpu_custom_call" | custom-call | flops 3000000000 | bytes 4194304 | tf_op jit(solution)/shard_map/scores/pallas_call | solution.py:390
  23.0 0.0 copy-done.9
  23.0 1.4 %collective-permute-done.1.t0_ref = bf16[256,2048]{1,0:T(8,128)(2,1)S(1)} collective-permute-done((bf16[256,2048]{1,0:T(8,128)(2,1)S(1)}, bf16[256,2048]{1,0:T(8,128)(2,1)S(1)}, u32[]{:S(2)}, u32[]{:S(2)}) %collective-permute-start.1) | collective-permute-done | bytes 1048608 | tf_op jit(solution)/shard_map/ppermute | solution.py:517
  24.4 0.0 slice-start
  24.4 0.4 add_convert_fusion.1.refs_8_
  24.8 0.0 slice-start.1
  24.8 1.0 %collective-permute-start.4 = (bf16[256,2048]{1,0:T(8,128)(2,1)S(1)}, bf16[256,2048]{1,0:T(8,128)(2,1)S(1)}, u32[]{:S(2)}, u32[]{:S(2)}) collective-permute-start(bf16[256,2048]{1,0:T(8,128)(2,1)S(1)} %add_convert_fusion.1.refs_8_), channel_id=1, source_target_pairs={{4,8},{5,9},{6,10},{7,11},{20,24},{21,25},{22,26},{23,27}} | collective-permute-start | bytes 3145736 | tf_op jit(solution)/shard_map/ppermute | solution.py:469
  25.8 9.0 %state.3 = (bf16[1024,2048]{1,0:T(8,128)(2,1)S(1)}, bf16[256,2048]{1,0:T(8,128)(2,1)S(1)}, bf16[256,2048]{1,0:T(8,128)(2,1)S(1)}, f32[1,2048]{1,0:T(1,128)S(1)}) custom-call(s32[4]{0:T(128)S(1)} %get-tuple-element.24.info_ref.refs_0_, bf16[1024,4096]{1,0:T(8,128)(2,1)} %refs_1_.1, bf16[3,5248]{1,0:T(4,128)(2,1)S(1)} %collective-permute-done.halo_ref.ids_ref.refs_2_, ...), custom_call_target="tpu_custom_call" | custom-call | flops 6000000000 | bytes 10485760 | tf_op jit(solution)/shard_map/state/pallas_call | solution.py:412
  34.9 1.3 %collective-permute-start.2 = (bf16[256,2048]{1,0:T(8,128)(2,1)S(1)}, bf16[256,2048]{1,0:T(8,128)(2,1)S(1)}, u32[]{:S(2)}, u32[]{:S(2)}) collective-permute-start(bf16[256,2048]{1,0:T(8,128)(2,1)S(1)} %get-tuple-element.36), channel_id=1, source_target_pairs={{0,4},{8,12},{1,5},{9,13},{2,6},{10,14},{3,7},{11,15},{16,20},{24,... | collective-permute-start | bytes 3145736 | tf_op jit(solution)/shard_map/ppermute | solution.py:517
  36.2 0.0 collective-permute-done.4.value_ref.t1_ref
  36.2 0.0 copy-start.10
  36.2 0.2 scale.2
  36.4 0.0 copy-start
  36.4 1.6 %collective-permute-start.5 = (bf16[256,2048]{1,0:T(8,128)(2,1)S(1)}, bf16[256,2048]{1,0:T(8,128)(2,1)S(1)}, u32[]{:S(2)}, u32[]{:S(2)}) collective-permute-start(bf16[256,2048]{1,0:T(8,128)(2,1)S(1)} %scale.2), channel_id=1, source_target_pairs={{0,4},{8,12},{1,5},{9,13},{2,6},{10,14},{3,7},{11,15},{16,20},{24,... | collective-permute-start | bytes 3145736 | tf_op jit(solution)/shard_map/ppermute | solution.py:470
  38.0 2.9 %collective-permute-done.2.refs_8_ = bf16[256,2048]{1,0:T(8,128)(2,1)S(1)} collective-permute-done((bf16[256,2048]{1,0:T(8,128)(2,1)S(1)}, bf16[256,2048]{1,0:T(8,128)(2,1)S(1)}, u32[]{:S(2)}, u32[]{:S(2)}) %collective-permute-start.2) | collective-permute-done | bytes 1048608 | tf_op jit(solution)/shard_map/ppermute | solution.py:517
  40.9 0.4 add_convert_fusion
  41.3 0.9 %collective-permute-start.3 = (bf16[256,2048]{1,0:T(8,128)(2,1)S(1)}, bf16[256,2048]{1,0:T(8,128)(2,1)S(1)}, u32[]{:S(2)}, u32[]{:S(2)}) collective-permute-start(bf16[256,2048]{1,0:T(8,128)(2,1)S(1)} %add_convert_fusion), channel_id=1, source_target_pairs={{4,8},{5,9},{6,10},{7,11},{20,24},{21,25},{22,26},{23,27}} | collective-permute-start | bytes 3145736 | tf_op jit(solution)/shard_map/ppermute | solution.py:469
  42.3 4.3 %collective-permute-done.5.t2_ref = bf16[256,2048]{1,0:T(8,128)(2,1)S(1)} collective-permute-done((bf16[256,2048]{1,0:T(8,128)(2,1)S(1)}, bf16[256,2048]{1,0:T(8,128)(2,1)S(1)}, u32[]{:S(2)}, u32[]{:S(2)}) %collective-permute-start.5) | collective-permute-done | bytes 1048608 | tf_op jit(solution)/shard_map/ppermute | solution.py:470
  46.6 0.0 slice-done
  46.6 0.0 slice-done.1
  46.6 0.0 copy-done.10
  46.6 0.0 copy-done
  46.6 10.0 %final.2 = (bf16[1024,4096]{1,0:T(8,128)(2,1)}, f32[8,128]{1,0:T(8,128)S(1)}) custom-call(s32[4]{0:T(128)S(1)} %get-tuple-element.24.info_ref.refs_0_, bf16[1024,2048]{1,0:T(8,128)(2,1)S(1)} %copy-done.10, bf16[1024,4096]{1,0:T(8,128)(2,1)S(1)} %bitcast.8, bf16[2,1024,768]{2,1,0:T(8,128)(2,1)S(1)} %scores.1.refs_9_.m_ref.refs_3_, ...), custom_call_target="tpu_custom_call" | custom-call | flops 6000000000 | bytes 16777216 | tf_op jit(solution)/shard_map/final/pallas_call | solution.py:497
  56.6 0.0 collective-permute-done.3.value_ref.refs_9_
  56.6 0.2 scale.3
  56.8 1.3 %collective-permute-start.6 = (bf16[256,2048]{1,0:T(8,128)(2,1)S(1)}, bf16[256,2048]{1,0:T(8,128)(2,1)S(1)}, u32[]{:S(2)}, u32[]{:S(2)}) collective-permute-start(bf16[256,2048]{1,0:T(8,128)(2,1)S(1)} %scale.3), channel_id=1, source_target_pairs={{0,4},{8,12},{1,5},{9,13},{2,6},{10,14},{3,7},{11,15},{16,20},{24,... | collective-permute-start | bytes 3145736 | tf_op jit(solution)/shard_map/ppermute | solution.py:470
  58.1 6.6 %collective-permute-done.6.refs_10_ = bf16[256,2048]{1,0:T(8,128)(2,1)S(1)} collective-permute-done((bf16[256,2048]{1,0:T(8,128)(2,1)S(1)}, bf16[256,2048]{1,0:T(8,128)(2,1)S(1)}, u32[]{:S(2)}, u32[]{:S(2)}) %collective-permute-start.6) | collective-permute-done | bytes 1048608 | tf_op jit(solution)/shard_map/ppermute | solution.py:470
  64.7 9.9 %final.3 = (bf16[1024,4096]{1,0:T(8,128)(2,1)}, f32[8,128]{1,0:T(8,128)}) custom-call(s32[4]{0:T(128)S(1)} %get-tuple-element.24.info_ref.refs_0_, bf16[1024,2048]{1,0:T(8,128)(2,1)S(1)} %get-tuple-element.32.refs_1_, bf16[1024,4096]{1,0:T(8,128)(2,1)S(1)} %bitcast.8, ...), custom_call_target="tpu_custom_call", output_to_operand_aliasing={{0}: (12, {})} | custom-call | flops 6000000000 | bytes 16777216 | tf_op jit(solution)/shard_map/final/pallas_call | solution.py:497
  (1 shorter events, 0.0 us)
Async XLA Ops:
  0.0 0.7 copy-start.1
  0.7 2.3 %copy-start.11 = (bf16[1024,64]{0,1:T(8,128)(2,1)S(1)}, bf16[1024,64]{0,1:T(8,128)(2,1)}, u32[]{:S(2)}) copy-start(bf16[1024,64]{0,1:T(8,128)(2,1)} %param.17) | copy-start | bytes 393220
  0.7 2.5 %copy-start.6 = (f32[64]{0:T(128)S(1)}, f32[64]{0:T(128)}, u32[]{:S(2)}) copy-start(f32[64]{0:T(128)} %param.21) | copy-start | bytes 772
  0.7 2.5 %copy-start.7 = (f32[64]{0:T(128)S(1)}, f32[64]{0:T(128)}, u32[]{:S(2)}) copy-start(f32[64]{0:T(128)} %param.22) | copy-start | bytes 772
  0.7 2.5 %copy-start.8 = (f32[64]{0:T(128)S(1)}, f32[64]{0:T(128)}, u32[]{:S(2)}) copy-start(f32[64]{0:T(128)} %param.23) | copy-start | bytes 772
  1.7 3.8 %collective-permute-start = (bf16[3,5248]{1,0:T(4,128)(2,1)S(1)}, bf16[3,5248]{1,0:T(4,128)(2,1)S(1)}, u32[]{:S(2)}, u32[]{:S(2)}) collective-permute-start(bf16[3,5248]{1,0:T(4,128)(2,1)S(1)} %tails.1), channel_id=1, source_target_pairs={{0,4},{4,8},{8,12},{1,5},{5,9},{9,13},{2,6},{6,10},{10,14},{3,7},{... | collective-permute-start | bytes 94472 | tf_op jit(solution)/shard_map/ppermute | solution.py:352
  3.2 2.3 %copy-start.2 = (s32[1024]{0:T(1024)S(1)}, s32[1024]{0:T(1024)}, u32[]{:S(2)}) copy-start(s32[1024]{0:T(1024)} %seg_s.5) | copy-start | bytes 12292
  3.2 2.3 %copy-start.4 = (bf16[4,512]{1,0:T(4,128)(2,1)S(1)}, bf16[4,512]{1,0:T(4,128)(2,1)}, u32[]{:S(2)}) copy-start(bf16[4,512]{1,0:T(4,128)(2,1)} %wb_ref.1) | copy-start | bytes 12292
  5.5 4.1 %copy-start.3 = (bf16[4,4096]{1,0:T(4,128)(2,1)S(1)}, bf16[4,4096]{1,0:T(4,128)(2,1)}, u32[]{:S(2)}) copy-start(bf16[4,4096]{1,0:T(4,128)(2,1)} %refs_3_.1) | copy-start | bytes 98308
  9.6 9.7 %copy-start.5 = (bf16[4,512]{1,0:T(4,128)(2,1)S(1)}, bf16[4,512]{1,0:T(4,128)(2,1)}, u32[]{:S(2)}) copy-start(bf16[4,512]{1,0:T(4,128)(2,1)} %wc_ref.1) | copy-start | bytes 12292
  18.0 4.9 %copy-start.9 = (bf16[1024,2048]{1,0:T(8,128)(2,1)}, bf16[1024,2048]{1,0:T(8,128)(2,1)S(1)}, u32[]{:S(2)}) copy-start(bf16[1024,2048]{1,0:T(8,128)(2,1)S(1)} %get-tuple-element.38.u_ref) | copy-start | bytes 12582916
  18.0 6.3 %collective-permute-start.1 = (bf16[256,2048]{1,0:T(8,128)(2,1)S(1)}, bf16[256,2048]{1,0:T(8,128)(2,1)S(1)}, u32[]{:S(2)}, u32[]{:S(2)}) collective-permute-start(bf16[256,2048]{1,0:T(8,128)(2,1)S(1)} %get-tuple-element.29), channel_id=1, source_target_pairs={{0,4},{8,12},{1,5},{9,13},{2,6},{10,14},{3,7},{11,15},{16,20},{24,... | collective-permute-start | bytes 3145736 | tf_op jit(solution)/shard_map/ppermute | solution.py:517
  24.4 22.2 %slice-start = ((s8[8388608]{0:T(1024)(128)(4,1)}), s8[4194304]{0:T(1024)(128)(4,1)S(1)}, s32[]{:S(2)}) async-start(s8[8388608]{0:T(1024)(128)(4,1)} %bitcast.7), calls=%async_computation | async-start | bytes 8388608
  24.8 21.8 %slice-start.1 = ((s8[8388608]{0:T(1024)(128)(4,1)}), s8[4194304]{0:T(1024)(128)(4,1)S(1)}, s32[]{:S(2)}) async-start(s8[8388608]{0:T(1024)(128)(4,1)} %bitcast.7), calls=%async_computation.1 | async-start | bytes 8388608
  24.8 11.4 %collective-permute-start.4 = (bf16[256,2048]{1,0:T(8,128)(2,1)S(1)}, bf16[256,2048]{1,0:T(8,128)(2,1)S(1)}, u32[]{:S(2)}, u32[]{:S(2)}) collective-permute-start(bf16[256,2048]{1,0:T(8,128)(2,1)S(1)} %add_convert_fusion.1.refs_8_), channel_id=1, source_target_pairs={{4,8},{5,9},{6,10},{7,11},{20,24},{21,25},{22,26},{23,27}} | collective-permute-start | bytes 3145736 | tf_op jit(solution)/shard_map/ppermute | solution.py:469
  34.9 6.0 %collective-permute-start.2 = (bf16[256,2048]{1,0:T(8,128)(2,1)S(1)}, bf16[256,2048]{1,0:T(8,128)(2,1)S(1)}, u32[]{:S(2)}, u32[]{:S(2)}) collective-permute-start(bf16[256,2048]{1,0:T(8,128)(2,1)S(1)} %get-tuple-element.36), channel_id=1, source_target_pairs={{0,4},{8,12},{1,5},{9,13},{2,6},{10,14},{3,7},{11,15},{16,20},{24,... | collective-permute-start | bytes 3145736 | tf_op jit(solution)/shard_map/ppermute | solution.py:517
  36.2 10.4 %copy-start.10 = (bf16[1024,2048]{1,0:T(8,128)(2,1)S(1)}, bf16[1024,2048]{1,0:T(8,128)(2,1)}, u32[]{:S(2)}) copy-start(bf16[1024,2048]{1,0:T(8,128)(2,1)} %copy-done.9) | copy-start | bytes 12582916
  36.4 10.2 %copy-start = (f32[4096]{0:T(1024)S(1)}, f32[4096]{0:T(1024)}, u32[]{:S(2)}) copy-start(f32[4096]{0:T(1024)} %param.24) | copy-start | bytes 49156
  36.4 10.2 %collective-permute-start.5 = (bf16[256,2048]{1,0:T(8,128)(2,1)S(1)}, bf16[256,2048]{1,0:T(8,128)(2,1)S(1)}, u32[]{:S(2)}, u32[]{:S(2)}) collective-permute-start(bf16[256,2048]{1,0:T(8,128)(2,1)S(1)} %scale.2), channel_id=1, source_target_pairs={{0,4},{8,12},{1,5},{9,13},{2,6},{10,14},{3,7},{11,15},{16,20},{24,... | collective-permute-start | bytes 3145736 | tf_op jit(solution)/shard_map/ppermute | solution.py:470
  41.3 15.3 %collective-permute-start.3 = (bf16[256,2048]{1,0:T(8,128)(2,1)S(1)}, bf16[256,2048]{1,0:T(8,128)(2,1)S(1)}, u32[]{:S(2)}, u32[]{:S(2)}) collective-permute-start(bf16[256,2048]{1,0:T(8,128)(2,1)S(1)} %add_convert_fusion), channel_id=1, source_target_pairs={{4,8},{5,9},{6,10},{7,11},{20,24},{21,25},{22,26},{23,27}} | collective-permute-start | bytes 3145736 | tf_op jit(solution)/shard_map/ppermute | solution.py:469
  56.8 7.9 %collective-permute-start.6 = (bf16[256,2048]{1,0:T(8,128)(2,1)S(1)}, bf16[256,2048]{1,0:T(8,128)(2,1)S(1)}, u32[]{:S(2)}, u32[]{:S(2)}) collective-permute-start(bf16[256,2048]{1,0:T(8,128)(2,1)S(1)} %scale.3), channel_id=1, source_target_pairs={{0,4},{8,12},{1,5},{9,13},{2,6},{10,14},{3,7},{11,15},{16,20},{24,... | collective-permute-start | bytes 3145736 | tf_op jit(solution)/shard_map/ppermute | solution.py:470

commit v4 on v3

--- a/solution.py
+++ b/solution.py
@@ -143,9 +143,9 @@
     code_ref[...] = code
     fill_conv(buf, held, b_ref, halo_ref, wb_ref, code_ref, span)
     bs_ref[...] = held[...].astype(BF16)
-    latest = seg_row == last.astype(F32)
+    latest = jnp.where(seg_row == last.astype(F32), 1.0, 0.0).astype(BF16)
     for g in range(parts):
-        bt_ref[g] = jnp.where(latest, jnp.transpose(held[:, g * N : (g + 1) * N]), 0.0).astype(BF16)
+        bt_ref[g] = jnp.transpose(bs_ref[:, g * N : (g + 1) * N]) * latest
 
 
 def score_kernel(
@@ -288,7 +288,7 @@
 
 
 def state_after_kernel(*refs, first_head, heads):
-    state_kernel(*refs[:8], *refs[10:], first_head=first_head, heads=heads)
+    state_kernel(*refs[:8], *refs[9:], first_head=first_head, heads=heads)
 
 
 def scale_kernel(value_ref, factor_ref, *refs):
@@ -321,8 +321,8 @@
     whole = lambda *_: (0, 0)
     at_row = lambda k, *_: (k, 0)
 
-    def params(axes):
-        return pltpu.CompilerParams(dimension_semantics=("arbitrary",) * axes, vmem_limit_bytes=30 << 20)
+    def params(axes, mib=16):
+        return pltpu.CompilerParams(dimension_semantics=("arbitrary",) * axes, vmem_limit_bytes=mib << 20)
 
     def cost(flops, mib):
         return pl.CostEstimate(flops=flops, bytes_accessed=mib << 20, transcendentals=0)
@@ -440,7 +440,7 @@
                 pltpu.VMEM((spans, N, step_width), F32),
                 pltpu.VMEM((LANES, step_width), BF16),
             ],
-            compiler_params=params(2),
+            compiler_params=params(2, 24),
             cost_estimate=cost(6 * 10**9, 10),
             name="state",
         )(info, x_in, halo, conv_x, bt, a_hl, em, code, *tokens)
@@ -467,7 +467,7 @@
         rounds = devices // 2 - 1
         for turn in range(rounds):
             entering = lax.ppermute(leaving, "req", across)
-            passed = lax.ppermute(scaled(entering, factor, token), "req", inside)
+            passed = lax.ppermute(scaled(entering, factor, token), "req", inside[1:])
             if turn < rounds - 1:
                 leaving = leave(state, first.astype(F32) + passed.astype(F32), factor)
         return first, entering, passed
@@ -475,7 +475,7 @@
     def final(g, u, m, first, carries, out):
         at_group = lambda *_: (0, g)
         own = pl.BlockSpec((SPAN, width), lambda k: (k, g))
-        square = pl.BlockSpec((N, width), whole)
+        square = pl.BlockSpec((N, width), whole, pipeline_mode=pl.Buffered(1))
         in_specs = [
             smem,
             pl.BlockSpec((SPAN, width), at_row),
@@ -506,19 +506,18 @@
                 pltpu.VMEM((SPAN, width), F32),
             ],
             input_output_aliases={} if out is None else {12: 0},
-            compiler_params=params(1),
+            compiler_params=params(1, 26),
             cost_estimate=cost(6 * 10**9, 16),
             name="final",
         )(*operands)
 
     leaving, locals_, m = None, [], None
     for g in range(parts):
-        u, state, inner, factor = local(g, [leaving, m] if g else [])
+        u, state, inner, factor = local(g, [leaving] if g else [])
         first = lax.ppermute(state, "req", inside)
-        if m is None:
-            m = score(factor)
         leaving = leave(state, first, factor)
         locals_.append((u, inner, state, first, leaving, factor))
+    m = score(factor)
     out = done = None
     for g in range(parts):
         u, inner, *sent = locals_[g]

time: 75.2 us -> 73.4 us (0.976)
  waiting for transfers between devices: 15.3 us -> 13 us
  Pallas kernels: 48.6 us -> 49.7 us
    ppermute x2, waiting for transfers between devices: 10.9 us -> 8.03 us  [travel(): passed = lax.ppermute(scaled(entering, factor, token), 'req', inside[1:])]
    pallas_call x2, Pallas kernels: 17.4 us -> 18.4 us  [local(): pl.pallas_call(functools.partial(state_after_kernel if tokens else state_...]
where the time goes in v4:
time: 73.4 us; the launch traced here: 73.3 us
  Pallas kernels  49.7 us (68%)
  waiting for transfers between devices  13 us (18%)
  starting transfers between devices  8.58 us (12%)
  local copies, waits for them, and re-layouts  0.92 us (1%)
  other arithmetic  0.8 us (1%)
    pallas_call x2, Pallas kernels, final(): pl.pallas_call(functools.partial(final_kernel if out is None else final_i...  20 us
    pallas_call x2, Pallas kernels, local(): pl.pallas_call(functools.partial(state_after_kernel if tokens else state_...  18.4 us
    ppermute x2, waiting for transfers between devices, travel(): passed = lax.ppermute(scaled(entering, factor, token), 'req', inside[1:])  8.03 us
    ppermute x2, waiting for transfers between devices, per_device(): first = lax.ppermute(state, 'req', inside)  5 us
    pallas_call x1, Pallas kernels, per_device(): pl.pallas_call(functools.partial(b_kernel, parts=parts), grid=(spans,), i...  3.96 us
    pallas_call x1, Pallas kernels, score(): pl.pallas_call(functools.partial(score_kernel, parts=parts), grid=(spans,...  3.72 us
    ppermute x2, starting transfers between devices, travel(): passed = lax.ppermute(scaled(entering, factor, token), 'req', inside[1:])  2.85 us
    ppermute x2, starting transfers between devices, per_device(): first = lax.ppermute(state, 'req', inside)  2.58 us
  transfers between devices with their start and end apart: 7, of which 4 were waited for; matrix products, arithmetic and copies ran while one was open for 1% of the time, Pallas kernels for 34%

profile of v4, /device:TPU:11, one launch (start us, length us, event | category | flops | bytes accessed | tf_op | source)
XLA Modules:
  0.0 73.3 jit_solution(8526069566540344740)
XLA Ops:
  0.0 0.0 copy-start.1
  0.0 0.7 copy-done.1
  0.7 0.0 copy-start.9
  0.7 0.0 copy-start.6
  0.7 0.0 copy-start.7
  0.7 0.0 copy-start.8
  0.7 1.0 %tails.1 = bf16[3,5248]{1,0:T(4,128)(2,1)S(1)} custom-call(s32[1024]{0:T(1024)S(1)} %copy-done.1, bf16[1024,4096]{1,0:T(8,128)(2,1)} %refs_1_.1, bf16[1024,512]{1,0:T(8,128)(2,1)} %b_ref.3, bf16[1024,512]{1,0:T(8,128)(2,1)} %c_ref.3), custom_call_target="tpu_custom_call" | custom-call | flops 1000 | tf_op jit(solution)/shard_map/tails/pallas_call | solution.py:337
  1.7 1.3 %collective-permute-start = (bf16[3,5248]{1,0:T(4,128)(2,1)S(1)}, bf16[3,5248]{1,0:T(4,128)(2,1)S(1)}, u32[]{:S(2)}, u32[]{:S(2)}) collective-permute-start(bf16[3,5248]{1,0:T(4,128)(2,1)S(1)} %tails.1), channel_id=1, source_target_pairs={{0,4},{4,8},{8,12},{1,5},{5,9},{9,13},{2,6},{6,10},{10,14},{3,7},{... | collective-permute-start | bytes 94472 | tf_op jit(solution)/shard_map/ppermute | solution.py:352
  3.0 0.0 copy-done.9
  3.0 0.2 copy.15.dt_ref
  3.2 0.0 copy-done.6
  3.2 0.0 copy-done.7
  3.2 0.0 copy-done.8
  3.2 0.0 copy-start.2
  3.2 0.0 copy-start.4
  3.2 2.2 %decays.1 = (bf16[1024,128]{1,0:T(8,128)(2,1)S(1)}, bf16[1024,128]{1,0:T(8,128)(2,1)S(1)}, bf16[1024,128]{1,0:T(8,128)(2,1)S(1)}, bf16[2,16,128]{2,1,0:T(8,128)(2,1)S(1)}) custom-call(bf16[1024,64]{1,0:T(8,128)(2,1)S(1)} %copy.15.dt_ref, f32[1,64]{1,0:T(1,128)S(1)} %bitcast.15, f32[1,64]{1,0:T(1,128)S(1)} %bitcast.16, f32[1,64]{1,0:T(1,128)S(1)} %bitcast.17), custom_call_target="tpu_custom_call" | custom-call | flops 3000000000 | bytes 1048576 | tf_op jit(solution)/shard_map/decays/pallas_call | solution.py:356
  5.5 0.0 copy-start.3
  5.5 0.0 collective-permute-done.halo_ref.ids_ref.refs_2_
  5.5 0.0 copy-done.2
  5.5 0.0 copy-done.4
  5.5 4.0 %b_rows.1 = (bf16[1024,512]{1,0:T(8,128)(2,1)S(1)}, bf16[2,256,1024]{2,1,0:T(8,128)(2,1)S(1)}, f32[1024,128]{1,0:T(8,128)S(1)}, s32[4]{0:T(128)S(1)}) custom-call(s32[1024]{0:T(1024)S(1)} %copy-done.2, bf16[1024,512]{1,0:T(8,128)(2,1)} %b_ref.3, bf16[3,5248]{1,0:T(4,128)(2,1)S(1)} %collective-permute-done.halo_ref.ids_ref.refs_2_, ...), custom_call_target="tpu_custom_call" | custom-call | flops 1000000000 | bytes 3145728 | tf_op jit(solution)/shard_map/b_rows/pallas_call | solution.py:372
  9.5 0.0 copy-done.3
  9.5 9.2 %state.2 = (bf16[1024,2048]{1,0:T(8,128)(2,1)S(1)}, bf16[256,2048]{1,0:T(8,128)(2,1)S(1)}, bf16[256,2048]{1,0:T(8,128)(2,1)S(1)}, f32[1,2048]{1,0:T(1,128)S(1)}) custom-call(s32[4]{0:T(128)S(1)} %get-tuple-element.24.info_ref.refs_0_, bf16[1024,4096]{1,0:T(8,128)(2,1)} %refs_1_.1, bf16[3,5248]{1,0:T(4,128)(2,1)S(1)} %collective-permute-done.halo_ref.ids_ref.refs_2_, ...), custom_call_target="tpu_custom_call" | custom-call | flops 6000000000 | bytes 10485760 | tf_op jit(solution)/shard_map/state/pallas_call | solution.py:412
  18.7 1.3 %collective-permute-start.1 = (bf16[256,2048]{1,0:T(8,128)(2,1)S(1)}, bf16[256,2048]{1,0:T(8,128)(2,1)S(1)}, u32[]{:S(2)}, u32[]{:S(2)}) collective-permute-start(bf16[256,2048]{1,0:T(8,128)(2,1)S(1)} %get-tuple-element.29), channel_id=1, source_target_pairs={{0,4},{8,12},{1,5},{9,13},{2,6},{10,14},{3,7},{11,15},{16,20},{24,... | collective-permute-start | bytes 3145736 | tf_op jit(solution)/shard_map/ppermute | solution.py:517
  20.0 3.5 %collective-permute-done.1.t0_ref = bf16[256,2048]{1,0:T(8,128)(2,1)S(1)} collective-permute-done((bf16[256,2048]{1,0:T(8,128)(2,1)S(1)}, bf16[256,2048]{1,0:T(8,128)(2,1)S(1)}, u32[]{:S(2)}, u32[]{:S(2)}) %collective-permute-start.1) | collective-permute-done | bytes 1048608 | tf_op jit(solution)/shard_map/ppermute | solution.py:517
  23.5 0.4 add_convert_fusion.1.refs_8_
  23.9 0.9 %collective-permute-start.4 = (bf16[256,2048]{1,0:T(8,128)(2,1)S(1)}, bf16[256,2048]{1,0:T(8,128)(2,1)S(1)}, u32[]{:S(2)}, u32[]{:S(2)}) collective-permute-start(bf16[256,2048]{1,0:T(8,128)(2,1)S(1)} %add_convert_fusion.1.refs_8_), channel_id=1, source_target_pairs={{4,8},{5,9},{6,10},{7,11},{20,24},{21,25},{22,26},{23,27}} | collective-permute-start | bytes 3145736 | tf_op jit(solution)/shard_map/ppermute | solution.py:469
  24.8 9.3 %state.3 = (bf16[1024,2048]{1,0:T(8,128)(2,1)S(1)}, bf16[256,2048]{1,0:T(8,128)(2,1)S(1)}, bf16[256,2048]{1,0:T(8,128)(2,1)S(1)}, f32[1,2048]{1,0:T(1,128)S(1)}) custom-call(s32[4]{0:T(128)S(1)} %get-tuple-element.24.info_ref.refs_0_, bf16[1024,4096]{1,0:T(8,128)(2,1)} %refs_1_.1, bf16[3,5248]{1,0:T(4,128)(2,1)S(1)} %collective-permute-done.halo_ref.ids_ref.refs_2_, ...), custom_call_target="tpu_custom_call" | custom-call | flops 6000000000 | bytes 10485760 | tf_op jit(solution)/shard_map/state/pallas_call | solution.py:412
  34.1 1.3 %collective-permute-start.2 = (bf16[256,2048]{1,0:T(8,128)(2,1)S(1)}, bf16[256,2048]{1,0:T(8,128)(2,1)S(1)}, u32[]{:S(2)}, u32[]{:S(2)}) collective-permute-start(bf16[256,2048]{1,0:T(8,128)(2,1)S(1)} %get-tuple-element.37), channel_id=1, source_target_pairs={{0,4},{8,12},{1,5},{9,13},{2,6},{10,14},{3,7},{11,15},{16,20},{24,... | collective-permute-start | bytes 3145736 | tf_op jit(solution)/shard_map/ppermute | solution.py:517
  35.4 0.0 collective-permute-done.4.value_ref.t1_ref
  35.4 0.0 slice-start
  35.4 0.2 scale.2
  35.6 0.0 copy-start.5
  35.6 1.6 %collective-permute-start.5 = (bf16[256,2048]{1,0:T(8,128)(2,1)S(1)}, bf16[256,2048]{1,0:T(8,128)(2,1)S(1)}, u32[]{:S(2)}, u32[]{:S(2)}) collective-permute-start(bf16[256,2048]{1,0:T(8,128)(2,1)S(1)} %scale.2), channel_id=1, source_target_pairs={{8,12},{9,13},{10,14},{11,15},{24,28},{25,29},{26,30},{27,31}} | collective-permute-start | bytes 3145736 | tf_op jit(solution)/shard_map/ppermute | solution.py:470
  37.2 1.5 %collective-permute-done.2.refs_8_ = bf16[256,2048]{1,0:T(8,128)(2,1)S(1)} collective-permute-done((bf16[256,2048]{1,0:T(8,128)(2,1)S(1)}, bf16[256,2048]{1,0:T(8,128)(2,1)S(1)}, u32[]{:S(2)}, u32[]{:S(2)}) %collective-permute-start.2) | collective-permute-done | bytes 1048608 | tf_op jit(solution)/shard_map/ppermute | solution.py:517
  38.7 0.4 add_convert_fusion
  39.1 0.9 %collective-permute-start.3 = (bf16[256,2048]{1,0:T(8,128)(2,1)S(1)}, bf16[256,2048]{1,0:T(8,128)(2,1)S(1)}, u32[]{:S(2)}, u32[]{:S(2)}) collective-permute-start(bf16[256,2048]{1,0:T(8,128)(2,1)S(1)} %add_convert_fusion), channel_id=1, source_target_pairs={{4,8},{5,9},{6,10},{7,11},{20,24},{21,25},{22,26},{23,27}} | collective-permute-start | bytes 3145736 | tf_op jit(solution)/shard_map/ppermute | solution.py:469
  40.0 0.0 copy-done.5
  40.0 0.0 slice-start.1
  40.0 0.0 copy-start
  40.1 3.7 %scores.1.m_ref.refs_3_ = bf16[2,1024,768]{2,1,0:T(8,128)(2,1)S(1)} custom-call(s32[1024]{0:T(1024)S(1)} %copy-done.2, bf16[1024,512]{1,0:T(8,128)(2,1)} %c_ref.3, bf16[3,5248]{1,0:T(4,128)(2,1)S(1)} %collective-permute-done.halo_ref.ids_ref.refs_2_, bf16[3,5248]{1,0:T(4,128)(2,1)S(1)} %collective-permute-done.halo_ref.ids_ref.refs_2_, ...), custom_call_target="tpu_custom_call" | custom-call | flops 3000000000 | bytes 4194304 | tf_op jit(solution)/shard_map/scores/pallas_call | solution.py:390
  43.8 1.3 %collective-permute-done.5.t2_ref = bf16[256,2048]{1,0:T(8,128)(2,1)S(1)} collective-permute-done((bf16[256,2048]{1,0:T(8,128)(2,1)S(1)}, bf16[256,2048]{1,0:T(8,128)(2,1)S(1)}, u32[]{:S(2)}, u32[]{:S(2)}) %collective-permute-start.5) | collective-permute-done | bytes 1048608 | tf_op jit(solution)/shard_map/ppermute | solution.py:470
  45.1 0.0 slice-done
  45.1 0.0 slice-done.1
  45.1 0.0 copy-done
  45.1 9.9 %final.2 = (bf16[1024,4096]{1,0:T(8,128)(2,1)}, f32[8,128]{1,0:T(8,128)S(1)}) custom-call(s32[4]{0:T(128)S(1)} %get-tuple-element.24.info_ref.refs_0_, bf16[1024,2048]{1,0:T(8,128)(2,1)S(1)} %get-tuple-element.38.u_ref, bf16[1024,4096]{1,0:T(8,128)(2,1)S(1)} %bitcast.8, bf16[2,1024,768]{2,1,0:T(8,128)(2,1)S(1)} %scores.1.m_ref.refs_3_, ...), custom_call_target="tpu_custom_call" | custom-call | flops 6000000000 | bytes 16777216 | tf_op jit(solution)/shard_map/final/pallas_call | solution.py:497
  55.0 0.0 collective-permute-done.3.value_ref.refs_9_
  55.0 0.2 scale.3
  55.2 1.3 %collective-permute-start.6 = (bf16[256,2048]{1,0:T(8,128)(2,1)S(1)}, bf16[256,2048]{1,0:T(8,128)(2,1)S(1)}, u32[]{:S(2)}, u32[]{:S(2)}) collective-permute-start(bf16[256,2048]{1,0:T(8,128)(2,1)S(1)} %scale.3), channel_id=1, source_target_pairs={{8,12},{9,13},{10,14},{11,15},{24,28},{25,29},{26,30},{27,31}} | collective-permute-start | bytes 3145736 | tf_op jit(solution)/shard_map/ppermute | solution.py:470
  56.5 6.7 %collective-permute-done.6.refs_10_ = bf16[256,2048]{1,0:T(8,128)(2,1)S(1)} collective-permute-done((bf16[256,2048]{1,0:T(8,128)(2,1)S(1)}, bf16[256,2048]{1,0:T(8,128)(2,1)S(1)}, u32[]{:S(2)}, u32[]{:S(2)}) %collective-permute-start.6) | collective-permute-done | bytes 1048608 | tf_op jit(solution)/shard_map/ppermute | solution.py:470
  63.2 10.1 %final.3 = (bf16[1024,4096]{1,0:T(8,128)(2,1)}, f32[8,128]{1,0:T(8,128)}) custom-call(s32[4]{0:T(128)S(1)} %get-tuple-element.24.info_ref.refs_0_, bf16[1024,2048]{1,0:T(8,128)(2,1)S(1)} %get-tuple-element.31.refs_1_, bf16[1024,4096]{1,0:T(8,128)(2,1)S(1)} %bitcast.8, ...), custom_call_target="tpu_custom_call", output_to_operand_aliasing={{0}: (12, {})} | custom-call | flops 6000000000 | bytes 16777216 | tf_op jit(solution)/shard_map/final/pallas_call | solution.py:497
  (1 shorter events, 0.0 us)
Async XLA Ops:
  0.0 0.7 copy-start.1
  0.7 2.3 %copy-start.9 = (bf16[1024,64]{0,1:T(8,128)(2,1)S(1)}, bf16[1024,64]{0,1:T(8,128)(2,1)}, u32[]{:S(2)}) copy-start(bf16[1024,64]{0,1:T(8,128)(2,1)} %param.17) | copy-start | bytes 393220
  0.7 2.5 %copy-start.6 = (f32[64]{0:T(128)S(1)}, f32[64]{0:T(128)}, u32[]{:S(2)}) copy-start(f32[64]{0:T(128)} %param.21) | copy-start | bytes 772
  0.7 2.5 %copy-start.7 = (f32[64]{0:T(128)S(1)}, f32[64]{0:T(128)}, u32[]{:S(2)}) copy-start(f32[64]{0:T(128)} %param.22) | copy-start | bytes 772
  0.7 2.5 %copy-start.8 = (f32[64]{0:T(128)S(1)}, f32[64]{0:T(128)}, u32[]{:S(2)}) copy-start(f32[64]{0:T(128)} %param.23) | copy-start | bytes 772
  1.7 3.8 %collective-permute-start = (bf16[3,5248]{1,0:T(4,128)(2,1)S(1)}, bf16[3,5248]{1,0:T(4,128)(2,1)S(1)}, u32[]{:S(2)}, u32[]{:S(2)}) collective-permute-start(bf16[3,5248]{1,0:T(4,128)(2,1)S(1)} %tails.1), channel_id=1, source_target_pairs={{0,4},{4,8},{8,12},{1,5},{5,9},{9,13},{2,6},{6,10},{10,14},{3,7},{... | collective-permute-start | bytes 94472 | tf_op jit(solution)/shard_map/ppermute | solution.py:352
  3.2 2.3 %copy-start.2 = (s32[1024]{0:T(1024)S(1)}, s32[1024]{0:T(1024)}, u32[]{:S(2)}) copy-start(s32[1024]{0:T(1024)} %seg_s.5) | copy-start | bytes 12292
  3.2 2.3 %copy-start.4 = (bf16[4,512]{1,0:T(4,128)(2,1)S(1)}, bf16[4,512]{1,0:T(4,128)(2,1)}, u32[]{:S(2)}) copy-start(bf16[4,512]{1,0:T(4,128)(2,1)} %wb_ref.1) | copy-start | bytes 12292
  5.5 4.0 %copy-start.3 = (bf16[4,4096]{1,0:T(4,128)(2,1)S(1)}, bf16[4,4096]{1,0:T(4,128)(2,1)}, u32[]{:S(2)}) copy-start(bf16[4,4096]{1,0:T(4,128)(2,1)} %refs_3_.1) | copy-start | bytes 98308
  18.7 4.8 %collective-permute-start.1 = (bf16[256,2048]{1,0:T(8,128)(2,1)S(1)}, bf16[256,2048]{1,0:T(8,128)(2,1)S(1)}, u32[]{:S(2)}, u32[]{:S(2)}) collective-permute-start(bf16[256,2048]{1,0:T(8,128)(2,1)S(1)} %get-tuple-element.29), channel_id=1, source_target_pairs={{0,4},{8,12},{1,5},{9,13},{2,6},{10,14},{3,7},{11,15},{16,20},{24,... | collective-permute-start | bytes 3145736 | tf_op jit(solution)/shard_map/ppermute | solution.py:517
  23.9 11.5 %collective-permute-start.4 = (bf16[256,2048]{1,0:T(8,128)(2,1)S(1)}, bf16[256,2048]{1,0:T(8,128)(2,1)S(1)}, u32[]{:S(2)}, u32[]{:S(2)}) collective-permute-start(bf16[256,2048]{1,0:T(8,128)(2,1)S(1)} %add_convert_fusion.1.refs_8_), channel_id=1, source_target_pairs={{4,8},{5,9},{6,10},{7,11},{20,24},{21,25},{22,26},{23,27}} | collective-permute-start | bytes 3145736 | tf_op jit(solution)/shard_map/ppermute | solution.py:469
  34.1 4.6 %collective-permute-start.2 = (bf16[256,2048]{1,0:T(8,128)(2,1)S(1)}, bf16[256,2048]{1,0:T(8,128)(2,1)S(1)}, u32[]{:S(2)}, u32[]{:S(2)}) collective-permute-start(bf16[256,2048]{1,0:T(8,128)(2,1)S(1)} %get-tuple-element.37), channel_id=1, source_target_pairs={{0,4},{8,12},{1,5},{9,13},{2,6},{10,14},{3,7},{11,15},{16,20},{24,... | collective-permute-start | bytes 3145736 | tf_op jit(solution)/shard_map/ppermute | solution.py:517
  35.4 9.7 %slice-start = ((s8[8388608]{0:T(1024)(128)(4,1)}), s8[4194304]{0:T(1024)(128)(4,1)S(1)}, s32[]{:S(2)}) async-start(s8[8388608]{0:T(1024)(128)(4,1)} %bitcast.7), calls=%async_computation | async-start | bytes 8388608
  35.6 4.4 %copy-start.5 = (bf16[4,512]{1,0:T(4,128)(2,1)S(1)}, bf16[4,512]{1,0:T(4,128)(2,1)}, u32[]{:S(2)}) copy-start(bf16[4,512]{1,0:T(4,128)(2,1)} %wc_ref.1) | copy-start | bytes 12292
  35.6 9.5 %collective-permute-start.5 = (bf16[256,2048]{1,0:T(8,128)(2,1)S(1)}, bf16[256,2048]{1,0:T(8,128)(2,1)S(1)}, u32[]{:S(2)}, u32[]{:S(2)}) collective-permute-start(bf16[256,2048]{1,0:T(8,128)(2,1)S(1)} %scale.2), channel_id=1, source_target_pairs={{8,12},{9,13},{10,14},{11,15},{24,28},{25,29},{26,30},{27,31}} | collective-permute-start | bytes 3145736 | tf_op jit(solution)/shard_map/ppermute | solution.py:470
  39.1 16.0 %collective-permute-start.3 = (bf16[256,2048]{1,0:T(8,128)(2,1)S(1)}, bf16[256,2048]{1,0:T(8,128)(2,1)S(1)}, u32[]{:S(2)}, u32[]{:S(2)}) collective-permute-start(bf16[256,2048]{1,0:T(8,128)(2,1)S(1)} %add_convert_fusion), channel_id=1, source_target_pairs={{4,8},{5,9},{6,10},{7,11},{20,24},{21,25},{22,26},{23,27}} | collective-permute-start | bytes 3145736 | tf_op jit(solution)/shard_map/ppermute | solution.py:469
  40.0 5.1 %slice-start.1 = ((s8[8388608]{0:T(1024)(128)(4,1)}), s8[4194304]{0:T(1024)(128)(4,1)S(1)}, s32[]{:S(2)}) async-start(s8[8388608]{0:T(1024)(128)(4,1)} %bitcast.7), calls=%async_computation.1 | async-start | bytes 8388608
  40.0 5.1 %copy-start = (f32[4096]{0:T(1024)S(1)}, f32[4096]{0:T(1024)}, u32[]{:S(2)}) copy-start(f32[4096]{0:T(1024)} %param.24) | copy-start | bytes 49156
  55.2 8.0 %collective-permute-start.6 = (bf16[256,2048]{1,0:T(8,128)(2,1)S(1)}, bf16[256,2048]{1,0:T(8,128)(2,1)S(1)}, u32[]{:S(2)}, u32[]{:S(2)}) collective-permute-start(bf16[256,2048]{1,0:T(8,128)(2,1)S(1)} %scale.3), channel_id=1, source_target_pairs={{8,12},{9,13},{10,14},{11,15},{24,28},{25,29},{26,30},{27,31}} | collective-permute-start | bytes 3145736 | tf_op jit(solution)/shard_map/ppermute | solution.py:470

commit v5 on v4

--- a/solution.py
+++ b/solution.py
@@ -240,7 +240,7 @@
 
 
 def final_kernel(
-    info_ref, u_ref, gate_ref, m_ref, e_ref, w_ref, em_ref, first_ref, t0_ref, t1_ref, t2_ref, gain_ref,
+    info_ref, u_ref, gate_ref, m_ref, e_ref, w_ref, em_ref, first_ref, t0_ref, t1_ref, gain_ref,
     out_ref, done_ref,
     enter, spread, held, *, first_head, heads
 ):
@@ -256,7 +256,7 @@
         passes = info_ref[1].astype(F32)
         for cols in strips:
             early, late = (dot(em_ref[k], spread[:, cols])[0:1] for k in range(2))
-            came = t0_ref[:, cols].astype(F32) + t1_ref[:, cols].astype(F32) + t2_ref[:, cols].astype(F32)
+            came = t0_ref[:, cols].astype(F32) + t1_ref[:, cols].astype(F32)
             enter[0, :, cols] = (early * came).astype(BF16)
             grown = first_ref[:, cols].astype(F32) + (passes * early * early) * came
             enter[1, :, cols] = (late * grown).astype(BF16)
@@ -299,7 +299,7 @@
 
 
 def final_into_kernel(*refs, first_head, heads):
-    final_kernel(*refs[:12], *refs[13:], first_head=first_head, heads=heads)
+    final_kernel(*refs[:11], *refs[12:], first_head=first_head, heads=heads)
 
 
 def per_device(
@@ -470,7 +470,7 @@
             passed = lax.ppermute(scaled(entering, factor, token), "req", inside[1:])
             if turn < rounds - 1:
                 leaving = leave(state, first.astype(F32) + passed.astype(F32), factor)
-        return first, entering, passed
+        return first + entering, passed
 
     def final(g, u, m, first, carries, out):
         at_group = lambda *_: (0, g)
@@ -484,7 +484,6 @@
             narrow,
             narrow,
             em_spec(),
-            square,
             square,
             square,
             square,
@@ -505,7 +504,7 @@
                 pltpu.VMEM((LANES, width), BF16),
                 pltpu.VMEM((SPAN, width), F32),
             ],
-            input_output_aliases={} if out is None else {12: 0},
+            input_output_aliases={} if out is None else {11: 0},
             compiler_params=params(1, 26),
             cost_estimate=cost(6 * 10**9, 16),
             name="final",
@@ -521,7 +520,7 @@
     out = done = None
     for g in range(parts):
         u, inner, *sent = locals_[g]
-        out, done = final(g, u, m, inner, travel(*sent, done), out)
+        out, done = final(g, u, m, inner, travel(*sent, m if done is None else done), out)
     return out
 
 

time: 73.4 us -> 73.7 us (level); the launches traced: 73.3 us -> 72.7 us
  Pallas kernels: 49.7 us -> 48.9 us
  other arithmetic: 0.8 us -> 1.6 us
    add x0 -> x2, other arithmetic: none -> 0.79 us  [travel(): return (first + entering, passed)]
  transfers between devices with their start and end apart: 7 -> 7, of which waited for: 4 -> 3; matrix products, arithmetic and copies ran while one was open for 1% -> 2% of each run, Pallas kernels for 34% -> 34%
where the time goes in v5:
time: 73.7 us; the launch traced here: 72.7 us
  Pallas kernels  48.9 us (66%)
  waiting for transfers between devices  12.4 us (17%)
  starting transfers between devices  8.58 us (12%)
  other arithmetic  1.6 us (2%)
  local copies, waits for them, and re-layouts  0.92 us (1%)
    pallas_call x2, Pallas kernels, final(): pl.pallas_call(functools.partial(final_kernel if out is None else final_i...  19.5 us
    pallas_call x2, Pallas kernels, local(): pl.pallas_call(functools.partial(state_after_kernel if tokens else state_...  18.2 us
    ppermute x2, waiting for transfers between devices, travel(): passed = lax.ppermute(scaled(entering, factor, token), 'req', inside[1:])  8.04 us
    ppermute x2, waiting for transfers between devices, per_device(): first = lax.ppermute(state, 'req', inside)  4.32 us
    pallas_call x1, Pallas kernels, per_device(): pl.pallas_call(functools.partial(b_kernel, parts=parts), grid=(spans,), i...  3.94 us
    pallas_call x1, Pallas kernels, score(): pl.pallas_call(functools.partial(score_kernel, parts=parts), grid=(spans,...  3.69 us
    ppermute x2, starting transfers between devices, travel(): passed = lax.ppermute(scaled(entering, factor, token), 'req', inside[1:])  2.85 us
    ppermute x2, starting transfers between devices, per_device(): first = lax.ppermute(state, 'req', inside)  2.58 us
  transfers between devices with their start and end apart: 7, of which 3 were waited for; matrix products, arithmetic and copies ran while one was open for 2% of the time, Pallas kernels for 34%

profile of v5, /device:TPU:11, one launch (start us, length us, event | category | flops | bytes accessed | tf_op | source)
XLA Modules:
  0.0 72.7 jit_solution(7883021965797970900)
XLA Ops:
  0.0 0.0 copy-start.1
  0.0 0.7 copy-done.1
  0.7 0.0 copy-start.9
  0.7 0.0 copy-start.6
  0.7 0.0 copy-start.7
  0.7 0.0 copy-start.8
  0.7 1.0 %tails.1 = bf16[3,5248]{1,0:T(4,128)(2,1)S(1)} custom-call(s32[1024]{0:T(1024)S(1)} %copy-done.1, bf16[1024,4096]{1,0:T(8,128)(2,1)} %refs_1_.1, bf16[1024,512]{1,0:T(8,128)(2,1)} %b_ref.3, bf16[1024,512]{1,0:T(8,128)(2,1)} %c_ref.3), custom_call_target="tpu_custom_call" | custom-call | flops 1000 | tf_op jit(solution)/shard_map/tails/pallas_call | solution.py:337
  1.7 1.3 %collective-permute-start = (bf16[3,5248]{1,0:T(4,128)(2,1)S(1)}, bf16[3,5248]{1,0:T(4,128)(2,1)S(1)}, u32[]{:S(2)}, u32[]{:S(2)}) collective-permute-start(bf16[3,5248]{1,0:T(4,128)(2,1)S(1)} %tails.1), channel_id=1, source_target_pairs={{0,4},{4,8},{8,12},{1,5},{5,9},{9,13},{2,6},{6,10},{10,14},{3,7},{... | collective-permute-start | bytes 94472 | tf_op jit(solution)/shard_map/ppermute | solution.py:352
  3.0 0.0 copy-done.9
  3.0 0.2 copy.15.dt_ref
  3.2 0.0 copy-done.6
  3.2 0.0 copy-done.7
  3.2 0.0 copy-done.8
  3.2 0.0 copy-start.2
  3.2 0.0 copy-start.4
  3.2 2.2 %decays.1 = (bf16[1024,128]{1,0:T(8,128)(2,1)S(1)}, bf16[1024,128]{1,0:T(8,128)(2,1)S(1)}, bf16[1024,128]{1,0:T(8,128)(2,1)S(1)}, bf16[2,16,128]{2,1,0:T(8,128)(2,1)S(1)}) custom-call(bf16[1024,64]{1,0:T(8,128)(2,1)S(1)} %copy.15.dt_ref, f32[1,64]{1,0:T(1,128)S(1)} %bitcast.15, f32[1,64]{1,0:T(1,128)S(1)} %bitcast.16, f32[1,64]{1,0:T(1,128)S(1)} %bitcast.17), custom_call_target="tpu_custom_call" | custom-call | flops 3000000000 | bytes 1048576 | tf_op jit(solution)/shard_map/decays/pallas_call | solution.py:356
  5.5 0.0 copy-start.3
  5.5 0.0 collective-permute-done.halo_ref.ids_ref.refs_2_
  5.5 0.0 copy-done.2
  5.5 0.0 copy-done.4
  5.5 3.9 %b_rows.1 = (bf16[1024,512]{1,0:T(8,128)(2,1)S(1)}, bf16[2,256,1024]{2,1,0:T(8,128)(2,1)S(1)}, f32[1024,128]{1,0:T(8,128)S(1)}, s32[4]{0:T(128)S(1)}) custom-call(s32[1024]{0:T(1024)S(1)} %copy-done.2, bf16[1024,512]{1,0:T(8,128)(2,1)} %b_ref.3, bf16[3,5248]{1,0:T(4,128)(2,1)S(1)} %collective-permute-done.halo_ref.ids_ref.refs_2_, ...), custom_call_target="tpu_custom_call" | custom-call | flops 1000000000 | bytes 3145728 | tf_op jit(solution)/shard_map/b_rows/pallas_call | solution.py:372
  9.5 0.0 copy-done.3
  9.5 9.1 %state.2 = (bf16[1024,2048]{1,0:T(8,128)(2,1)S(1)}, bf16[256,2048]{1,0:T(8,128)(2,1)S(1)}, bf16[256,2048]{1,0:T(8,128)(2,1)S(1)}, f32[1,2048]{1,0:T(1,128)S(1)}) custom-call(s32[4]{0:T(128)S(1)} %get-tuple-element.24.info_ref.refs_0_, bf16[1024,4096]{1,0:T(8,128)(2,1)} %refs_1_.1, bf16[3,5248]{1,0:T(4,128)(2,1)S(1)} %collective-permute-done.halo_ref.ids_ref.refs_2_, ...), custom_call_target="tpu_custom_call" | custom-call | flops 6000000000 | bytes 10485760 | tf_op jit(solution)/shard_map/state/pallas_call | solution.py:412
  18.6 1.3 %collective-permute-start.1 = (bf16[256,2048]{1,0:T(8,128)(2,1)S(1)}, bf16[256,2048]{1,0:T(8,128)(2,1)S(1)}, u32[]{:S(2)}, u32[]{:S(2)}) collective-permute-start(bf16[256,2048]{1,0:T(8,128)(2,1)S(1)} %get-tuple-element.29), channel_id=1, source_target_pairs={{0,4},{8,12},{1,5},{9,13},{2,6},{10,14},{3,7},{11,15},{16,20},{24,... | collective-permute-start | bytes 3145736 | tf_op jit(solution)/shard_map/ppermute | solution.py:516
  19.9 4.3 %collective-permute-done.1 = bf16[256,2048]{1,0:T(8,128)(2,1)S(1)} collective-permute-done((bf16[256,2048]{1,0:T(8,128)(2,1)S(1)}, bf16[256,2048]{1,0:T(8,128)(2,1)S(1)}, u32[]{:S(2)}, u32[]{:S(2)}) %collective-permute-start.1) | collective-permute-done | bytes 1048608 | tf_op jit(solution)/shard_map/ppermute | solution.py:516
  24.2 0.4 add_convert_fusion.1.refs_8_
  24.6 0.0 copy-start.5
  24.6 0.9 %collective-permute-start.4 = (bf16[256,2048]{1,0:T(8,128)(2,1)S(1)}, bf16[256,2048]{1,0:T(8,128)(2,1)S(1)}, u32[]{:S(2)}, u32[]{:S(2)}) collective-permute-start(bf16[256,2048]{1,0:T(8,128)(2,1)S(1)} %add_convert_fusion.1.refs_8_), channel_id=1, source_target_pairs={{4,8},{5,9},{6,10},{7,11},{20,24},{21,25},{22,26},{23,27}} | collective-permute-start | bytes 3145736 | tf_op jit(solution)/shard_map/ppermute | solution.py:469
  25.6 9.1 %state.3 = (bf16[1024,2048]{1,0:T(8,128)(2,1)S(1)}, bf16[256,2048]{1,0:T(8,128)(2,1)S(1)}, bf16[256,2048]{1,0:T(8,128)(2,1)S(1)}, f32[1,2048]{1,0:T(1,128)S(1)}) custom-call(s32[4]{0:T(128)S(1)} %get-tuple-element.24.info_ref.refs_0_, bf16[1024,4096]{1,0:T(8,128)(2,1)} %refs_1_.1, bf16[3,5248]{1,0:T(4,128)(2,1)S(1)} %collective-permute-done.halo_ref.ids_ref.refs_2_, ...), custom_call_target="tpu_custom_call" | custom-call | flops 6000000000 | bytes 10485760 | tf_op jit(solution)/shard_map/state/pallas_call | solution.py:412
  34.7 1.3 %collective-permute-start.2 = (bf16[256,2048]{1,0:T(8,128)(2,1)S(1)}, bf16[256,2048]{1,0:T(8,128)(2,1)S(1)}, u32[]{:S(2)}, u32[]{:S(2)}) collective-permute-start(bf16[256,2048]{1,0:T(8,128)(2,1)S(1)} %get-tuple-element.37), channel_id=1, source_target_pairs={{0,4},{8,12},{1,5},{9,13},{2,6},{10,14},{3,7},{11,15},{16,20},{24,... | collective-permute-start | bytes 3145736 | tf_op jit(solution)/shard_map/ppermute | solution.py:516
  36.0 0.0 copy-done.5
  36.0 0.0 slice-start
  36.0 3.7 %scores.1.refs_0_.m_ref.refs_3_ = bf16[2,1024,768]{2,1,0:T(8,128)(2,1)S(1)} custom-call(s32[1024]{0:T(1024)S(1)} %copy-done.2, bf16[1024,512]{1,0:T(8,128)(2,1)} %c_ref.3, bf16[3,5248]{1,0:T(4,128)(2,1)S(1)} %collective-permute-done.halo_ref.ids_ref.refs_2_, bf16[3,5248]{1,0:T(4,128)(2,1)S(1)} %collective-permute-done.halo_ref.ids_ref.refs_2_, ...), custom_call_target="tpu_custom_call" | custom-call | flops 3000000000 | bytes 4194304 | tf_op jit(solution)/shard_map/scores/pallas_call | solution.py:390
  39.7 0.0 slice-start.1
  39.7 0.0 collective-permute-done.4.value_ref
  39.7 0.2 scale.2
  39.9 1.6 %collective-permute-start.5 = (bf16[256,2048]{1,0:T(8,128)(2,1)S(1)}, bf16[256,2048]{1,0:T(8,128)(2,1)S(1)}, u32[]{:S(2)}, u32[]{:S(2)}) collective-permute-start(bf16[256,2048]{1,0:T(8,128)(2,1)S(1)} %scale.2), channel_id=1, source_target_pairs={{8,12},{9,13},{10,14},{11,15},{24,28},{25,29},{26,30},{27,31}} | collective-permute-start | bytes 3145736 | tf_op jit(solution)/shard_map/ppermute | solution.py:470
  41.5 0.0 collective-permute-done.2
  41.5 0.4 add_convert_fusion
  41.9 0.0 copy-start
  41.9 0.9 %collective-permute-start.3 = (bf16[256,2048]{1,0:T(8,128)(2,1)S(1)}, bf16[256,2048]{1,0:T(8,128)(2,1)S(1)}, u32[]{:S(2)}, u32[]{:S(2)}) collective-permute-start(bf16[256,2048]{1,0:T(8,128)(2,1)S(1)} %add_convert_fusion), channel_id=1, source_target_pairs={{4,8},{5,9},{6,10},{7,11},{20,24},{21,25},{22,26},{23,27}} | collective-permute-start | bytes 3145736 | tf_op jit(solution)/shard_map/ppermute | solution.py:469
  42.9 0.4 add.15.t0_ref
  43.3 1.6 %collective-permute-done.5.t1_ref = bf16[256,2048]{1,0:T(8,128)(2,1)S(1)} collective-permute-done((bf16[256,2048]{1,0:T(8,128)(2,1)S(1)}, bf16[256,2048]{1,0:T(8,128)(2,1)S(1)}, u32[]{:S(2)}, u32[]{:S(2)}) %collective-permute-start.5) | collective-permute-done | bytes 1048608 | tf_op jit(solution)/shard_map/ppermute | solution.py:470
  44.9 0.0 slice-done
  44.9 0.0 slice-done.1
  44.9 0.0 copy-done
  44.9 9.7 %final.2 = (bf16[1024,4096]{1,0:T(8,128)(2,1)}, f32[8,128]{1,0:T(8,128)S(1)}) custom-call(s32[4]{0:T(128)S(1)} %get-tuple-element.24.info_ref.refs_0_, bf16[1024,2048]{1,0:T(8,128)(2,1)S(1)} %get-tuple-element.38.u_ref, bf16[1024,4096]{1,0:T(8,128)(2,1)S(1)} %bitcast.8, bf16[2,1024,768]{2,1,0:T(8,128)(2,1)S(1)} %scores.1.refs_0_.m_ref.refs_3_, ...), custom_call_target="tpu_custom_call" | custom-call | flops 6000000000 | bytes 16777216 | tf_op jit(solution)/shard_map/final/pallas_call | solution.py:496
  54.6 0.0 collective-permute-done.3.value_ref
  54.6 0.2 scale.3
  54.8 1.3 %collective-permute-start.6 = (bf16[256,2048]{1,0:T(8,128)(2,1)S(1)}, bf16[256,2048]{1,0:T(8,128)(2,1)S(1)}, u32[]{:S(2)}, u32[]{:S(2)}) collective-permute-start(bf16[256,2048]{1,0:T(8,128)(2,1)S(1)} %scale.3), channel_id=1, source_target_pairs={{8,12},{9,13},{10,14},{11,15},{24,28},{25,29},{26,30},{27,31}} | collective-permute-start | bytes 3145736 | tf_op jit(solution)/shard_map/ppermute | solution.py:470
  56.1 0.4 add.14.refs_8_
  56.5 6.4 %collective-permute-done.6.refs_9_ = bf16[256,2048]{1,0:T(8,128)(2,1)S(1)} collective-permute-done((bf16[256,2048]{1,0:T(8,128)(2,1)S(1)}, bf16[256,2048]{1,0:T(8,128)(2,1)S(1)}, u32[]{:S(2)}, u32[]{:S(2)}) %collective-permute-start.6) | collective-permute-done | bytes 1048608 | tf_op jit(solution)/shard_map/ppermute | solution.py:470
  62.9 9.8 %final.3 = (bf16[1024,4096]{1,0:T(8,128)(2,1)}, f32[8,128]{1,0:T(8,128)}) custom-call(s32[4]{0:T(128)S(1)} %get-tuple-element.24.info_ref.refs_0_, bf16[1024,2048]{1,0:T(8,128)(2,1)S(1)} %get-tuple-element.31.refs_1_, bf16[1024,4096]{1,0:T(8,128)(2,1)S(1)} %bitcast.8, ...), custom_call_target="tpu_custom_call", output_to_operand_aliasing={{0}: (11, {})} | custom-call | flops 6000000000 | bytes 16777216 | tf_op jit(solution)/shard_map/final/pallas_call | solution.py:496
  (1 shorter events, 0.0 us)
Async XLA Ops:
  0.0 0.7 copy-start.1
  0.7 2.3 %copy-start.9 = (bf16[1024,64]{0,1:T(8,128)(2,1)S(1)}, bf16[1024,64]{0,1:T(8,128)(2,1)}, u32[]{:S(2)}) copy-start(bf16[1024,64]{0,1:T(8,128)(2,1)} %param.17) | copy-start | bytes 393220
  0.7 2.5 %copy-start.6 = (f32[64]{0:T(128)S(1)}, f32[64]{0:T(128)}, u32[]{:S(2)}) copy-start(f32[64]{0:T(128)} %param.21) | copy-start | bytes 772
  0.7 2.5 %copy-start.7 = (f32[64]{0:T(128)S(1)}, f32[64]{0:T(128)}, u32[]{:S(2)}) copy-start(f32[64]{0:T(128)} %param.22) | copy-start | bytes 772
  0.7 2.5 %copy-start.8 = (f32[64]{0:T(128)S(1)}, f32[64]{0:T(128)}, u32[]{:S(2)}) copy-start(f32[64]{0:T(128)} %param.23) | copy-start | bytes 772
  1.7 3.8 %collective-permute-start = (bf16[3,5248]{1,0:T(4,128)(2,1)S(1)}, bf16[3,5248]{1,0:T(4,128)(2,1)S(1)}, u32[]{:S(2)}, u32[]{:S(2)}) collective-permute-start(bf16[3,5248]{1,0:T(4,128)(2,1)S(1)} %tails.1), channel_id=1, source_target_pairs={{0,4},{4,8},{8,12},{1,5},{5,9},{9,13},{2,6},{6,10},{10,14},{3,7},{... | collective-permute-start | bytes 94472 | tf_op jit(solution)/shard_map/ppermute | solution.py:352
  3.2 2.3 %copy-start.2 = (s32[1024]{0:T(1024)S(1)}, s32[1024]{0:T(1024)}, u32[]{:S(2)}) copy-start(s32[1024]{0:T(1024)} %seg_s.5) | copy-start | bytes 12292
  3.2 2.3 %copy-start.4 = (bf16[4,512]{1,0:T(4,128)(2,1)S(1)}, bf16[4,512]{1,0:T(4,128)(2,1)}, u32[]{:S(2)}) copy-start(bf16[4,512]{1,0:T(4,128)(2,1)} %wb_ref.1) | copy-start | bytes 12292
  5.5 4.0 %copy-start.3 = (bf16[4,4096]{1,0:T(4,128)(2,1)S(1)}, bf16[4,4096]{1,0:T(4,128)(2,1)}, u32[]{:S(2)}) copy-start(bf16[4,4096]{1,0:T(4,128)(2,1)} %refs_3_.1) | copy-start | bytes 98308
  18.6 5.6 %collective-permute-start.1 = (bf16[256,2048]{1,0:T(8,128)(2,1)S(1)}, bf16[256,2048]{1,0:T(8,128)(2,1)S(1)}, u32[]{:S(2)}, u32[]{:S(2)}) collective-permute-start(bf16[256,2048]{1,0:T(8,128)(2,1)S(1)} %get-tuple-element.29), channel_id=1, source_target_pairs={{0,4},{8,12},{1,5},{9,13},{2,6},{10,14},{3,7},{11,15},{16,20},{24,... | collective-permute-start | bytes 3145736 | tf_op jit(solution)/shard_map/ppermute | solution.py:516
  24.6 11.4 %copy-start.5 = (bf16[4,512]{1,0:T(4,128)(2,1)S(1)}, bf16[4,512]{1,0:T(4,128)(2,1)}, u32[]{:S(2)}) copy-start(bf16[4,512]{1,0:T(4,128)(2,1)} %wc_ref.1) | copy-start | bytes 12292
  24.6 15.1 %collective-permute-start.4 = (bf16[256,2048]{1,0:T(8,128)(2,1)S(1)}, bf16[256,2048]{1,0:T(8,128)(2,1)S(1)}, u32[]{:S(2)}, u32[]{:S(2)}) collective-permute-start(bf16[256,2048]{1,0:T(8,128)(2,1)S(1)} %add_convert_fusion.1.refs_8_), channel_id=1, source_target_pairs={{4,8},{5,9},{6,10},{7,11},{20,24},{21,25},{22,26},{23,27}} | collective-permute-start | bytes 3145736 | tf_op jit(solution)/shard_map/ppermute | solution.py:469
  34.7 6.8 %collective-permute-start.2 = (bf16[256,2048]{1,0:T(8,128)(2,1)S(1)}, bf16[256,2048]{1,0:T(8,128)(2,1)S(1)}, u32[]{:S(2)}, u32[]{:S(2)}) collective-permute-start(bf16[256,2048]{1,0:T(8,128)(2,1)S(1)} %get-tuple-element.37), channel_id=1, source_target_pairs={{0,4},{8,12},{1,5},{9,13},{2,6},{10,14},{3,7},{11,15},{16,20},{24,... | collective-permute-start | bytes 3145736 | tf_op jit(solution)/shard_map/ppermute | solution.py:516
  36.0 8.9 %slice-start = ((s8[8388608]{0:T(1024)(128)(4,1)}), s8[4194304]{0:T(1024)(128)(4,1)S(1)}, s32[]{:S(2)}) async-start(s8[8388608]{0:T(1024)(128)(4,1)} %bitcast.7), calls=%async_computation | async-start | bytes 8388608
  39.7 5.2 %slice-start.1 = ((s8[8388608]{0:T(1024)(128)(4,1)}), s8[4194304]{0:T(1024)(128)(4,1)S(1)}, s32[]{:S(2)}) async-start(s8[8388608]{0:T(1024)(128)(4,1)} %bitcast.7), calls=%async_computation.1 | async-start | bytes 8388608
  39.9 4.9 %collective-permute-start.5 = (bf16[256,2048]{1,0:T(8,128)(2,1)S(1)}, bf16[256,2048]{1,0:T(8,128)(2,1)S(1)}, u32[]{:S(2)}, u32[]{:S(2)}) collective-permute-start(bf16[256,2048]{1,0:T(8,128)(2,1)S(1)} %scale.2), channel_id=1, source_target_pairs={{8,12},{9,13},{10,14},{11,15},{24,28},{25,29},{26,30},{27,31}} | collective-permute-start | bytes 3145736 | tf_op jit(solution)/shard_map/ppermute | solution.py:470
  41.9 3.0 %copy-start = (f32[4096]{0:T(1024)S(1)}, f32[4096]{0:T(1024)}, u32[]{:S(2)}) copy-start(f32[4096]{0:T(1024)} %param.24) | copy-start | bytes 49156
  41.9 12.7 %collective-permute-start.3 = (bf16[256,2048]{1,0:T(8,128)(2,1)S(1)}, bf16[256,2048]{1,0:T(8,128)(2,1)S(1)}, u32[]{:S(2)}, u32[]{:S(2)}) collective-permute-start(bf16[256,2048]{1,0:T(8,128)(2,1)S(1)} %add_convert_fusion), channel_id=1, source_target_pairs={{4,8},{5,9},{6,10},{7,11},{20,24},{21,25},{22,26},{23,27}} | collective-permute-start | bytes 3145736 | tf_op jit(solution)/shard_map/ppermute | solution.py:469
  54.8 8.1 %collective-permute-start.6 = (bf16[256,2048]{1,0:T(8,128)(2,1)S(1)}, bf16[256,2048]{1,0:T(8,128)(2,1)S(1)}, u32[]{:S(2)}, u32[]{:S(2)}) collective-permute-start(bf16[256,2048]{1,0:T(8,128)(2,1)S(1)} %scale.3), channel_id=1, source_target_pairs={{8,12},{9,13},{10,14},{11,15},{24,28},{25,29},{26,30},{27,31}} | collective-permute-start | bytes 3145736 | tf_op jit(solution)/shard_map/ppermute | solution.py:470

commit v6 on v5

--- a/solution.py
+++ b/solution.py
@@ -348,7 +348,7 @@
         compiler_params=params(1),
         cost_estimate=cost(1000, 0),
         name="tails",
-    )(segment, x_in, b_in, c_in)
+    )(pltpu.with_memory_space_constraint(segment, pltpu.HBM), x_in, b_in, c_in)
     halo = lax.ppermute(tail, "req", shift)
 
     row = lambda value: value.reshape(1, -1)

time: 73.7 us -> 72.3 us (0.981)
  Pallas kernels: 48.9 us -> 47.5 us
  waiting for transfers between devices: 12.4 us -> 13.6 us
    pallas_call x2, Pallas kernels: 18.2 us -> 16.8 us  [local(): pl.pallas_call(functools.partial(state_after_kernel if tokens else state_...]
    ppermute x2, waiting for transfers between devices: 4.32 us -> 5.06 us  [per_device(): first = lax.ppermute(state, 'req', inside)]
where the time goes in v6:
time: 72.3 us; the launch traced here: 71.8 us
  Pallas kernels  47.5 us (66%)
  waiting for transfers between devices  13.6 us (19%)
  starting transfers between devices  8.58 us (12%)
  other arithmetic  1.6 us (2%)
    pallas_call x2, Pallas kernels, final(): pl.pallas_call(functools.partial(final_kernel if out is None else final_i...  19.5 us
    pallas_call x2, Pallas kernels, local(): pl.pallas_call(functools.partial(state_after_kernel if tokens else state_...  16.8 us
    ppermute x2, waiting for transfers between devices, travel(): passed = lax.ppermute(scaled(entering, factor, token), 'req', inside[1:])  8.55 us
    ppermute x2, waiting for transfers between devices, per_device(): first = lax.ppermute(state, 'req', inside)  5.06 us
    pallas_call x1, Pallas kernels, per_device(): pl.pallas_call(functools.partial(b_kernel, parts=parts), grid=(spans,), i...  3.94 us
    pallas_call x1, Pallas kernels, score(): pl.pallas_call(functools.partial(score_kernel, parts=parts), grid=(spans,...  3.69 us
    ppermute x2, starting transfers between devices, travel(): passed = lax.ppermute(scaled(entering, factor, token), 'req', inside[1:])  2.85 us
    ppermute x2, starting transfers between devices, per_device(): first = lax.ppermute(state, 'req', inside)  2.58 us
  transfers between devices with their start and end apart: 7, of which 3 were waited for; matrix products, arithmetic and copies ran while one was open for 2% of the time, Pallas kernels for 34%

profile of v6, /device:TPU:11, one launch (start us, length us, event | category | flops | bytes accessed | tf_op | source)
XLA Modules:
  0.0 71.8 jit_solution(9869935983718900436)
XLA Ops:
  0.0 0.0 copy-start.8
  0.0 0.0 copy-start.7
  0.0 0.0 copy-start.6
  0.0 0.0 copy-start.5
  0.0 1.0 %tails.1 = bf16[3,5248]{1,0:T(4,128)(2,1)S(1)} custom-call(s32[1024]{0:T(1024)} %seg_s.5, bf16[1024,4096]{1,0:T(8,128)(2,1)} %refs_1_.1, bf16[1024,512]{1,0:T(8,128)(2,1)} %b_ref.3, bf16[1024,512]{1,0:T(8,128)(2,1)} %c_ref.3), custom_call_target="tpu_custom_call" | custom-call | flops 1000 | tf_op jit(solution)/shard_map/tails/pallas_call | solution.py:337
  1.0 1.3 %collective-permute-start = (bf16[3,5248]{1,0:T(4,128)(2,1)S(1)}, bf16[3,5248]{1,0:T(4,128)(2,1)S(1)}, u32[]{:S(2)}, u32[]{:S(2)}) collective-permute-start(bf16[3,5248]{1,0:T(4,128)(2,1)S(1)} %tails.1), channel_id=1, source_target_pairs={{0,4},{4,8},{8,12},{1,5},{5,9},{9,13},{2,6},{6,10},{10,14},{3,7},{... | collective-permute-start | bytes 94472 | tf_op jit(solution)/shard_map/ppermute | solution.py:352
  2.3 0.0 copy-done.8
  2.3 0.2 copy.15.dt_ref
  2.5 0.0 copy-done.7
  2.5 0.0 copy-done.6
  2.5 0.0 copy-done.5
  2.5 0.0 copy-start.1
  2.5 0.0 copy-start.3
  2.6 2.2 %decays.1 = (bf16[1024,128]{1,0:T(8,128)(2,1)S(1)}, bf16[1024,128]{1,0:T(8,128)(2,1)S(1)}, bf16[1024,128]{1,0:T(8,128)(2,1)S(1)}, bf16[2,16,128]{2,1,0:T(8,128)(2,1)S(1)}) custom-call(bf16[1024,64]{1,0:T(8,128)(2,1)S(1)} %copy.15.dt_ref, f32[1,64]{1,0:T(1,128)S(1)} %bitcast.15, f32[1,64]{1,0:T(1,128)S(1)} %bitcast.16, f32[1,64]{1,0:T(1,128)S(1)} %bitcast.17), custom_call_target="tpu_custom_call" | custom-call | flops 3000000000 | bytes 1048576 | tf_op jit(solution)/shard_map/decays/pallas_call | solution.py:356
  4.8 0.0 copy-start.2
  4.8 0.0 collective-permute-done.halo_ref.ids_ref.refs_2_
  4.8 0.0 copy-done.1
  4.8 0.0 copy-done.3
  4.8 3.9 %b_rows.1 = (bf16[1024,512]{1,0:T(8,128)(2,1)S(1)}, bf16[2,256,1024]{2,1,0:T(8,128)(2,1)S(1)}, f32[1024,128]{1,0:T(8,128)S(1)}, s32[4]{0:T(128)S(1)}) custom-call(s32[1024]{0:T(1024)S(1)} %copy-done.1, bf16[1024,512]{1,0:T(8,128)(2,1)} %b_ref.3, bf16[3,5248]{1,0:T(4,128)(2,1)S(1)} %collective-permute-done.halo_ref.ids_ref.refs_2_, ...), custom_call_target="tpu_custom_call" | custom-call | flops 1000000000 | bytes 3145728 | tf_op jit(solution)/shard_map/b_rows/pallas_call | solution.py:372
  8.8 0.0 copy-done.2
  8.8 8.4 %state.2 = (bf16[1024,2048]{1,0:T(8,128)(2,1)S(1)}, bf16[256,2048]{1,0:T(8,128)(2,1)S(1)}, bf16[256,2048]{1,0:T(8,128)(2,1)S(1)}, f32[1,2048]{1,0:T(1,128)S(1)}) custom-call(s32[4]{0:T(128)S(1)} %get-tuple-element.24.info_ref.refs_0_, bf16[1024,4096]{1,0:T(8,128)(2,1)} %refs_1_.1, bf16[3,5248]{1,0:T(4,128)(2,1)S(1)} %collective-permute-done.halo_ref.ids_ref.refs_2_, ...), custom_call_target="tpu_custom_call" | custom-call | flops 6000000000 | bytes 10485760 | tf_op jit(solution)/shard_map/state/pallas_call | solution.py:412
  17.2 1.3 %collective-permute-start.1 = (bf16[256,2048]{1,0:T(8,128)(2,1)S(1)}, bf16[256,2048]{1,0:T(8,128)(2,1)S(1)}, u32[]{:S(2)}, u32[]{:S(2)}) collective-permute-start(bf16[256,2048]{1,0:T(8,128)(2,1)S(1)} %get-tuple-element.29), channel_id=1, source_target_pairs={{0,4},{8,12},{1,5},{9,13},{2,6},{10,14},{3,7},{11,15},{16,20},{24,... | collective-permute-start | bytes 3145736 | tf_op jit(solution)/shard_map/ppermute | solution.py:516
  18.5 5.1 %collective-permute-done.1 = bf16[256,2048]{1,0:T(8,128)(2,1)S(1)} collective-permute-done((bf16[256,2048]{1,0:T(8,128)(2,1)S(1)}, bf16[256,2048]{1,0:T(8,128)(2,1)S(1)}, u32[]{:S(2)}, u32[]{:S(2)}) %collective-permute-start.1) | collective-permute-done | bytes 1048608 | tf_op jit(solution)/shard_map/ppermute | solution.py:516
  23.5 0.4 add_convert_fusion.1.refs_8_
  23.9 0.0 copy-start.4
  24.0 0.9 %collective-permute-start.4 = (bf16[256,2048]{1,0:T(8,128)(2,1)S(1)}, bf16[256,2048]{1,0:T(8,128)(2,1)S(1)}, u32[]{:S(2)}, u32[]{:S(2)}) collective-permute-start(bf16[256,2048]{1,0:T(8,128)(2,1)S(1)} %add_convert_fusion.1.refs_8_), channel_id=1, source_target_pairs={{4,8},{5,9},{6,10},{7,11},{20,24},{21,25},{22,26},{23,27}} | collective-permute-start | bytes 3145736 | tf_op jit(solution)/shard_map/ppermute | solution.py:469
  24.9 8.4 %state.3 = (bf16[1024,2048]{1,0:T(8,128)(2,1)S(1)}, bf16[256,2048]{1,0:T(8,128)(2,1)S(1)}, bf16[256,2048]{1,0:T(8,128)(2,1)S(1)}, f32[1,2048]{1,0:T(1,128)S(1)}) custom-call(s32[4]{0:T(128)S(1)} %get-tuple-element.24.info_ref.refs_0_, bf16[1024,4096]{1,0:T(8,128)(2,1)} %refs_1_.1, bf16[3,5248]{1,0:T(4,128)(2,1)S(1)} %collective-permute-done.halo_ref.ids_ref.refs_2_, ...), custom_call_target="tpu_custom_call" | custom-call | flops 6000000000 | bytes 10485760 | tf_op jit(solution)/shard_map/state/pallas_call | solution.py:412
  33.3 1.3 %collective-permute-start.2 = (bf16[256,2048]{1,0:T(8,128)(2,1)S(1)}, bf16[256,2048]{1,0:T(8,128)(2,1)S(1)}, u32[]{:S(2)}, u32[]{:S(2)}) collective-permute-start(bf16[256,2048]{1,0:T(8,128)(2,1)S(1)} %get-tuple-element.37), channel_id=1, source_target_pairs={{0,4},{8,12},{1,5},{9,13},{2,6},{10,14},{3,7},{11,15},{16,20},{24,... | collective-permute-start | bytes 3145736 | tf_op jit(solution)/shard_map/ppermute | solution.py:516
  34.6 0.0 copy-done.4
  34.6 0.0 slice-start
  34.6 3.7 %scores.1.refs_0_.m_ref.refs_3_ = bf16[2,1024,768]{2,1,0:T(8,128)(2,1)S(1)} custom-call(s32[1024]{0:T(1024)S(1)} %copy-done.1, bf16[1024,512]{1,0:T(8,128)(2,1)} %c_ref.3, bf16[3,5248]{1,0:T(4,128)(2,1)S(1)} %collective-permute-done.halo_ref.ids_ref.refs_2_, bf16[3,5248]{1,0:T(4,128)(2,1)S(1)} %collective-permute-done.halo_ref.ids_ref.refs_2_, ...), custom_call_target="tpu_custom_call" | custom-call | flops 3000000000 | bytes 4194304 | tf_op jit(solution)/shard_map/scores/pallas_call | solution.py:390
  38.3 0.0 slice-start.1
  38.3 0.0 collective-permute-done.4.value_ref
  38.3 0.2 scale.2
  38.5 1.6 %collective-permute-start.5 = (bf16[256,2048]{1,0:T(8,128)(2,1)S(1)}, bf16[256,2048]{1,0:T(8,128)(2,1)S(1)}, u32[]{:S(2)}, u32[]{:S(2)}) collective-permute-start(bf16[256,2048]{1,0:T(8,128)(2,1)S(1)} %scale.2), channel_id=1, source_target_pairs={{8,12},{9,13},{10,14},{11,15},{24,28},{25,29},{26,30},{27,31}} | collective-permute-start | bytes 3145736 | tf_op jit(solution)/shard_map/ppermute | solution.py:470
  40.0 0.0 collective-permute-done.2
  40.1 0.4 add_convert_fusion
  40.5 0.0 copy-start
  40.5 0.9 %collective-permute-start.3 = (bf16[256,2048]{1,0:T(8,128)(2,1)S(1)}, bf16[256,2048]{1,0:T(8,128)(2,1)S(1)}, u32[]{:S(2)}, u32[]{:S(2)}) collective-permute-start(bf16[256,2048]{1,0:T(8,128)(2,1)S(1)} %add_convert_fusion), channel_id=1, source_target_pairs={{4,8},{5,9},{6,10},{7,11},{20,24},{21,25},{22,26},{23,27}} | collective-permute-start | bytes 3145736 | tf_op jit(solution)/shard_map/ppermute | solution.py:469
  41.4 0.4 add.15.t0_ref
  41.8 2.1 %collective-permute-done.5.t1_ref = bf16[256,2048]{1,0:T(8,128)(2,1)S(1)} collective-permute-done((bf16[256,2048]{1,0:T(8,128)(2,1)S(1)}, bf16[256,2048]{1,0:T(8,128)(2,1)S(1)}, u32[]{:S(2)}, u32[]{:S(2)}) %collective-permute-start.5) | collective-permute-done | bytes 1048608 | tf_op jit(solution)/shard_map/ppermute | solution.py:470
  44.0 0.0 slice-done
  44.0 0.0 slice-done.1
  44.0 0.0 copy-done
  44.0 9.7 %final.2 = (bf16[1024,4096]{1,0:T(8,128)(2,1)}, f32[8,128]{1,0:T(8,128)S(1)}) custom-call(s32[4]{0:T(128)S(1)} %get-tuple-element.24.info_ref.refs_0_, bf16[1024,2048]{1,0:T(8,128)(2,1)S(1)} %get-tuple-element.38.u_ref, bf16[1024,4096]{1,0:T(8,128)(2,1)S(1)} %bitcast.8, bf16[2,1024,768]{2,1,0:T(8,128)(2,1)S(1)} %scores.1.refs_0_.m_ref.refs_3_, ...), custom_call_target="tpu_custom_call" | custom-call | flops 6000000000 | bytes 16777216 | tf_op jit(solution)/shard_map/final/pallas_call | solution.py:496
  53.7 0.0 collective-permute-done.3.value_ref
  53.7 0.2 scale.3
  53.9 1.3 %collective-permute-start.6 = (bf16[256,2048]{1,0:T(8,128)(2,1)S(1)}, bf16[256,2048]{1,0:T(8,128)(2,1)S(1)}, u32[]{:S(2)}, u32[]{:S(2)}) collective-permute-start(bf16[256,2048]{1,0:T(8,128)(2,1)S(1)} %scale.3), channel_id=1, source_target_pairs={{8,12},{9,13},{10,14},{11,15},{24,28},{25,29},{26,30},{27,31}} | collective-permute-start | bytes 3145736 | tf_op jit(solution)/shard_map/ppermute | solution.py:470
  55.2 0.4 add.14.refs_8_
  55.6 6.4 %collective-permute-done.6.refs_9_ = bf16[256,2048]{1,0:T(8,128)(2,1)S(1)} collective-permute-done((bf16[256,2048]{1,0:T(8,128)(2,1)S(1)}, bf16[256,2048]{1,0:T(8,128)(2,1)S(1)}, u32[]{:S(2)}, u32[]{:S(2)}) %collective-permute-start.6) | collective-permute-done | bytes 1048608 | tf_op jit(solution)/shard_map/ppermute | solution.py:470
  62.0 9.8 %final.3 = (bf16[1024,4096]{1,0:T(8,128)(2,1)}, f32[8,128]{1,0:T(8,128)}) custom-call(s32[4]{0:T(128)S(1)} %get-tuple-element.24.info_ref.refs_0_, bf16[1024,2048]{1,0:T(8,128)(2,1)S(1)} %get-tuple-element.31.refs_1_, bf16[1024,4096]{1,0:T(8,128)(2,1)S(1)} %bitcast.8, ...), custom_call_target="tpu_custom_call", output_to_operand_aliasing={{0}: (11, {})} | custom-call | flops 6000000000 | bytes 16777216 | tf_op jit(solution)/shard_map/final/pallas_call | solution.py:496
  (1 shorter events, 0.0 us)
Async XLA Ops:
  0.0 2.3 %copy-start.8 = (bf16[1024,64]{0,1:T(8,128)(2,1)S(1)}, bf16[1024,64]{0,1:T(8,128)(2,1)}, u32[]{:S(2)}) copy-start(bf16[1024,64]{0,1:T(8,128)(2,1)} %param.17) | copy-start | bytes 393220
  0.0 2.5 %copy-start.7 = (f32[64]{0:T(128)S(1)}, f32[64]{0:T(128)}, u32[]{:S(2)}) copy-start(f32[64]{0:T(128)} %param.23) | copy-start | bytes 772
  0.0 2.5 %copy-start.6 = (f32[64]{0:T(128)S(1)}, f32[64]{0:T(128)}, u32[]{:S(2)}) copy-start(f32[64]{0:T(128)} %param.22) | copy-start | bytes 772
  0.0 2.5 %copy-start.5 = (f32[64]{0:T(128)S(1)}, f32[64]{0:T(128)}, u32[]{:S(2)}) copy-start(f32[64]{0:T(128)} %param.21) | copy-start | bytes 772
  1.0 3.8 %collective-permute-start = (bf16[3,5248]{1,0:T(4,128)(2,1)S(1)}, bf16[3,5248]{1,0:T(4,128)(2,1)S(1)}, u32[]{:S(2)}, u32[]{:S(2)}) collective-permute-start(bf16[3,5248]{1,0:T(4,128)(2,1)S(1)} %tails.1), channel_id=1, source_target_pairs={{0,4},{4,8},{8,12},{1,5},{5,9},{9,13},{2,6},{6,10},{10,14},{3,7},{... | collective-permute-start | bytes 94472 | tf_op jit(solution)/shard_map/ppermute | solution.py:352
  2.5 2.3 %copy-start.1 = (s32[1024]{0:T(1024)S(1)}, s32[1024]{0:T(1024)}, u32[]{:S(2)}) copy-start(s32[1024]{0:T(1024)} %seg_s.5) | copy-start | bytes 12292
  2.5 2.3 %copy-start.3 = (bf16[4,512]{1,0:T(4,128)(2,1)S(1)}, bf16[4,512]{1,0:T(4,128)(2,1)}, u32[]{:S(2)}) copy-start(bf16[4,512]{1,0:T(4,128)(2,1)} %wb_ref.1) | copy-start | bytes 12292
  4.8 4.0 %copy-start.2 = (bf16[4,4096]{1,0:T(4,128)(2,1)S(1)}, bf16[4,4096]{1,0:T(4,128)(2,1)}, u32[]{:S(2)}) copy-start(bf16[4,4096]{1,0:T(4,128)(2,1)} %refs_3_.1) | copy-start | bytes 98308
  17.2 6.4 %collective-permute-start.1 = (bf16[256,2048]{1,0:T(8,128)(2,1)S(1)}, bf16[256,2048]{1,0:T(8,128)(2,1)S(1)}, u32[]{:S(2)}, u32[]{:S(2)}) collective-permute-start(bf16[256,2048]{1,0:T(8,128)(2,1)S(1)} %get-tuple-element.29), channel_id=1, source_target_pairs={{0,4},{8,12},{1,5},{9,13},{2,6},{10,14},{3,7},{11,15},{16,20},{24,... | collective-permute-start | bytes 3145736 | tf_op jit(solution)/shard_map/ppermute | solution.py:516
  23.9 10.6 %copy-start.4 = (bf16[4,512]{1,0:T(4,128)(2,1)S(1)}, bf16[4,512]{1,0:T(4,128)(2,1)}, u32[]{:S(2)}) copy-start(bf16[4,512]{1,0:T(4,128)(2,1)} %wc_ref.1) | copy-start | bytes 12292
  24.0 14.3 %collective-permute-start.4 = (bf16[256,2048]{1,0:T(8,128)(2,1)S(1)}, bf16[256,2048]{1,0:T(8,128)(2,1)S(1)}, u32[]{:S(2)}, u32[]{:S(2)}) collective-permute-start(bf16[256,2048]{1,0:T(8,128)(2,1)S(1)} %add_convert_fusion.1.refs_8_), channel_id=1, source_target_pairs={{4,8},{5,9},{6,10},{7,11},{20,24},{21,25},{22,26},{23,27}} | collective-permute-start | bytes 3145736 | tf_op jit(solution)/shard_map/ppermute | solution.py:469
  33.3 6.8 %collective-permute-start.2 = (bf16[256,2048]{1,0:T(8,128)(2,1)S(1)}, bf16[256,2048]{1,0:T(8,128)(2,1)S(1)}, u32[]{:S(2)}, u32[]{:S(2)}) collective-permute-start(bf16[256,2048]{1,0:T(8,128)(2,1)S(1)} %get-tuple-element.37), channel_id=1, source_target_pairs={{0,4},{8,12},{1,5},{9,13},{2,6},{10,14},{3,7},{11,15},{16,20},{24,... | collective-permute-start | bytes 3145736 | tf_op jit(solution)/shard_map/ppermute | solution.py:516
  34.6 9.4 %slice-start = ((s8[8388608]{0:T(1024)(128)(4,1)}), s8[4194304]{0:T(1024)(128)(4,1)S(1)}, s32[]{:S(2)}) async-start(s8[8388608]{0:T(1024)(128)(4,1)} %bitcast.7), calls=%async_computation | async-start | bytes 8388608
  38.3 5.7 %slice-start.1 = ((s8[8388608]{0:T(1024)(128)(4,1)}), s8[4194304]{0:T(1024)(128)(4,1)S(1)}, s32[]{:S(2)}) async-start(s8[8388608]{0:T(1024)(128)(4,1)} %bitcast.7), calls=%async_computation.1 | async-start | bytes 8388608
  38.5 5.5 %collective-permute-start.5 = (bf16[256,2048]{1,0:T(8,128)(2,1)S(1)}, bf16[256,2048]{1,0:T(8,128)(2,1)S(1)}, u32[]{:S(2)}, u32[]{:S(2)}) collective-permute-start(bf16[256,2048]{1,0:T(8,128)(2,1)S(1)} %scale.2), channel_id=1, source_target_pairs={{8,12},{9,13},{10,14},{11,15},{24,28},{25,29},{26,30},{27,31}} | collective-permute-start | bytes 3145736 | tf_op jit(solution)/shard_map/ppermute | solution.py:470
  40.5 3.5 %copy-start = (f32[4096]{0:T(1024)S(1)}, f32[4096]{0:T(1024)}, u32[]{:S(2)}) copy-start(f32[4096]{0:T(1024)} %param.24) | copy-start | bytes 49156
  40.5 13.2 %collective-permute-start.3 = (bf16[256,2048]{1,0:T(8,128)(2,1)S(1)}, bf16[256,2048]{1,0:T(8,128)(2,1)S(1)}, u32[]{:S(2)}, u32[]{:S(2)}) collective-permute-start(bf16[256,2048]{1,0:T(8,128)(2,1)S(1)} %add_convert_fusion), channel_id=1, source_target_pairs={{4,8},{5,9},{6,10},{7,11},{20,24},{21,25},{22,26},{23,27}} | collective-permute-start | bytes 3145736 | tf_op jit(solution)/shard_map/ppermute | solution.py:469
  53.9 8.1 %collective-permute-start.6 = (bf16[256,2048]{1,0:T(8,128)(2,1)S(1)}, bf16[256,2048]{1,0:T(8,128)(2,1)S(1)}, u32[]{:S(2)}, u32[]{:S(2)}) collective-permute-start(bf16[256,2048]{1,0:T(8,128)(2,1)S(1)} %scale.3), channel_id=1, source_target_pairs={{8,12},{9,13},{10,14},{11,15},{24,28},{25,29},{26,30},{27,31}} | collective-permute-start | bytes 3145736 | tf_op jit(solution)/shard_map/ppermute | solution.py:470
